TPU v7x, 256 devices: a whole 4x4x8 slice. The times are simulated.
256 devices in a mesh: rows: 8 (over z_hi, core), cols: 16 (over x, y), batch: 2 (over z_lo).
Axes of the slice: x: 4, y: 4, z: 8 (z_hi: 4, z_lo: 2; z = z_hi * 2 + z_lo), core: 2. Of those that a mesh axis runs over, the one named last changes fastest.
Arguments:
- fine_input: bfloat16 [2, 256, 2048, 128], P('batch', 'rows', 'cols'), may hold values from -60 to 60
- coarse: bfloat16 [2, 64, 512, 512], P('batch', 'rows', 'cols'), may hold values from -6 to 6
- rain_bins: int32 [2, 256, 2048], P('batch', 'rows', 'cols'), may hold values from 0 to 63
- w_qkv: bfloat16 [512, 1536], replicated, may hold values from -0.25 to 0.25
- w_out: bfloat16 [512, 512], replicated, may hold values from -0.25 to 0.25
- w_up: bfloat16 [512, 128], replicated, may hold values from -0.25 to 0.25
- w_conv: bfloat16 [3, 3, 128, 128], replicated, may hold values from -0.4375 to 0.4375
- w_head: bfloat16 [128, 9], replicated, may hold values from -0.5 to 0.5
Outputs:
- quantiles: float32 [2, 9, 256, 2048], P('batch', None, 'rows', 'cols')
- loss_value: float32 [], replicated
- grad_qkv: float32 [512, 1536], replicated
- grad_out: float32 [512, 512], replicated
- grad_up: float32 [512, 128], replicated
- grad_conv: float32 [3, 3, 128, 128], replicated
- grad_head: float32 [128, 9], replicated
- grad_fine: float32 [2, 256, 2048, 128], P('batch', 'rows', 'cols')
All inputs are finite; a program needn't handle non-finite values.
Results may differ from a plain program's by a relative error of at most 0.015.
Values may be sent and summed in bfloat16 or wider, within the bound.
A program may use at most 64 MiB of HBM per device.

v0:
```python
import jax
import jax.numpy as jnp
from jax import lax
from jax.sharding import PartitionSpec as P

HEAD_DIM = 32
QUANT = 9


def with_halo(block, sides, width):
    for axis, dim in sides:
        count = lax.axis_size(axis)
        forward = [(i, i + 1) for i in range(count - 1)]
        backward = [(target, source) for source, target in forward]
        low = lax.ppermute(
            lax.slice_in_dim(block, block.shape[dim] - width, None, axis=dim), axis, forward
        )
        high = lax.ppermute(lax.slice_in_dim(block, 0, width, axis=dim), axis, backward)
        block = jnp.concatenate([low, block, high], axis=dim)
    return block


def regroup(block):
    return lax.all_to_all(block, ("rows", "cols"), split_axis=0, concat_axis=0, tiled=True)


def attend(tokens, w_qkv, w_out):
    members, groups, width = tokens.shape
    heads = width // HEAD_DIM
    projected = jnp.einsum("sgw,wk->sgk", tokens, w_qkv, preferred_element_type=jnp.float32).astype(
        jnp.bfloat16
    )
    query = projected[:, :, :width].reshape(members, groups, heads, HEAD_DIM)
    keyed = projected[:, :, width : 2 * width].reshape(members, groups, heads, HEAD_DIM)
    valued = projected[:, :, 2 * width :].reshape(members, groups, heads, HEAD_DIM)
    scores = jnp.einsum(
        "sghd,tghd->ghst", query, keyed, preferred_element_type=jnp.float32
    ) * HEAD_DIM ** (-0.5)
    peak = jnp.max(scores, axis=-1, keepdims=True)
    powers = jnp.exp(scores - peak)
    probability = powers / jnp.sum(powers, axis=-1, keepdims=True)
    prob_b = probability.astype(jnp.bfloat16)
    mixed = jnp.einsum(
        "ghst,tghd->sghd", prob_b, valued, preferred_element_type=jnp.float32
    ).astype(jnp.bfloat16)
    mixed = mixed.reshape(members, groups, width)
    result = jnp.einsum("sgw,wk->sgk", mixed, w_out, preferred_element_type=jnp.float32)
    return (result, (query, keyed, valued, probability, prob_b, mixed))


def attend_back(tokens, w_out, saved, cotangent):
    query, keyed, valued, probability, prob_b, mixed = saved
    members, groups, heads, _ = query.shape
    width = heads * HEAD_DIM
    grad_out = jnp.einsum("sgw,sgk->wk", mixed, cotangent, preferred_element_type=jnp.float32)
    mix_grad = jnp.einsum(
        "sgk,wk->sgw", cotangent, w_out, preferred_element_type=jnp.float32
    ).astype(jnp.bfloat16)
    mix_grad = mix_grad.reshape(members, groups, heads, HEAD_DIM)
    dprob = jnp.einsum("sghd,tghd->ghst", mix_grad, valued, preferred_element_type=jnp.float32)
    dvalue = jnp.einsum("ghst,sghd->tghd", prob_b, mix_grad, preferred_element_type=jnp.float32)
    inner = jnp.sum(probability * dprob, axis=-1, keepdims=True)
    dscore = (probability * (dprob - inner) * HEAD_DIM ** (-0.5)).astype(jnp.bfloat16)
    dquery = jnp.einsum("ghst,tghd->sghd", dscore, keyed, preferred_element_type=jnp.float32)
    dkey = jnp.einsum("ghst,sghd->tghd", dscore, query, preferred_element_type=jnp.float32)
    dproj = jnp.concatenate(
        [
            dquery.reshape(members, groups, width),
            dkey.reshape(members, groups, width),
            dvalue.reshape(members, groups, width),
        ],
        axis=-1,
    ).astype(jnp.bfloat16)
    grad_qkv = jnp.einsum("sgw,sgk->wk", tokens, dproj, preferred_element_type=jnp.float32)
    return (grad_qkv, grad_out)


def body(fine_input, coarse, rain_bins, w_qkv, w_out, w_up, w_conv, w_head):
    samples, coarse_rows, coarse_cols, width = coarse.shape
    fine_rows, fine_cols, channels = fine_input.shape[1:]
    peers = lax.axis_size("rows") * lax.axis_size("cols")
    groups = coarse_rows * coarse_cols // peers
    grid_tokens = regroup(coarse.reshape(peers, groups, width))
    result, saved = attend(grid_tokens, w_qkv, w_out)
    attended = regroup(result.astype(jnp.bfloat16)).reshape(coarse.shape)
    context = (coarse.astype(jnp.float32) + attended.astype(jnp.float32)).astype(jnp.bfloat16)
    lifted = jnp.einsum("bijw,wc->bijc", context, w_up, preferred_element_type=jnp.float32)
    spread = jnp.repeat(jnp.repeat(lifted, 4, axis=1), 4, axis=2)
    hidden = fine_input.astype(jnp.float32) + spread
    active = jax.nn.gelu(hidden).astype(jnp.bfloat16)
    padded = with_halo(active, (("rows", 1), ("cols", 2)), 1)
    conv_out = jnp.zeros(hidden.shape, jnp.float32)
    for row_tap in range(3):
        for col_tap in range(3):
            window = padded[:, row_tap : row_tap + fine_rows, col_tap : col_tap + fine_cols]
            conv_out = conv_out + jnp.einsum(
                "bhwc,ck->bhwk",
                window,
                w_conv[row_tap, col_tap],
                preferred_element_type=jnp.float32,
            )
    outer = (hidden + conv_out).astype(jnp.bfloat16)
    quantiles = jnp.einsum("bhwc,cq->bqhw", outer, w_head, preferred_element_type=jnp.float32)
    target = rain_bins.astype(jnp.float32)[:, None] / 16.0 - 1.0
    levels = ((jnp.arange(QUANT) + 1).astype(jnp.float32) / (QUANT + 1.0))[None, :, None, None]
    error_term = target - quantiles
    weight_term = jnp.where(error_term < 0.0, 1.0 - levels, levels)
    magnitude = jnp.abs(error_term)
    huber_term = jnp.where(magnitude <= 1.0, 0.5 * error_term * error_term, magnitude - 0.5)
    loss_part = jnp.sum(weight_term * huber_term)
    pixel_count = (
        samples
        * lax.axis_size("batch")
        * fine_rows
        * lax.axis_size("rows")
        * fine_cols
        * lax.axis_size("cols")
    )
    root_count = jnp.sqrt(jnp.asarray(pixel_count, jnp.float32))
    dpred = (-weight_term * jnp.clip(error_term, -1.0, 1.0) / root_count).astype(jnp.bfloat16)
    grad_head = jnp.einsum("bhwc,bqhw->cq", outer, dpred, preferred_element_type=jnp.float32)
    douter = jnp.einsum("bqhw,cq->bhwc", dpred, w_head, preferred_element_type=jnp.float32)
    douter_b = douter.astype(jnp.bfloat16)
    grad_pad = with_halo(douter_b, (("rows", 1), ("cols", 2)), 1)
    dactive = jnp.zeros(hidden.shape, jnp.float32)
    kernel_rows = []
    for row_tap in range(3):
        kernel_row = []
        for col_tap in range(3):
            window = padded[:, row_tap : row_tap + fine_rows, col_tap : col_tap + fine_cols]
            kernel_row.append(
                jnp.einsum("bhwc,bhwk->ck", window, douter_b, preferred_element_type=jnp.float32)
            )
            back_window = grad_pad[
                :, 2 - row_tap : 2 - row_tap + fine_rows, 2 - col_tap : 2 - col_tap + fine_cols
            ]
            dactive = dactive + jnp.einsum(
                "bhwk,ck->bhwc",
                back_window,
                w_conv[row_tap, col_tap],
                preferred_element_type=jnp.float32,
            )
        kernel_rows.append(jnp.stack(kernel_row))
    grad_conv = jnp.stack(kernel_rows)
    slope = jax.vjp(jax.nn.gelu, hidden)[1](dactive)[0]
    dhidden = douter + slope
    grad_fine = dhidden * root_count
    dlift = (
        dhidden.reshape(samples, coarse_rows, 4, coarse_cols, 4, channels)
        .sum(axis=(2, 4))
        .astype(jnp.bfloat16)
    )
    grad_up = jnp.einsum("bijw,bijc->wc", context, dlift, preferred_element_type=jnp.float32)
    dcontext = jnp.einsum("bijc,wc->bijw", dlift, w_up, preferred_element_type=jnp.float32).astype(
        jnp.bfloat16
    )
    grid_grads = regroup(dcontext.reshape(peers, groups, width))
    grad_qkv, grad_out = attend_back(grid_tokens, w_out, saved, grid_grads)
    grad_qkv, grad_out, grad_up, grad_conv, grad_head, loss_total = lax.psum(
        (grad_qkv, grad_out, grad_up, grad_conv, grad_head, loss_part), ("rows", "cols", "batch")
    )
    loss_value = loss_total / (pixel_count * QUANT)
    return (quantiles, loss_value, grad_qkv, grad_out, grad_up, grad_conv, grad_head, grad_fine)


def solution(mesh):
    placed = (
        P("batch", "rows", "cols", None),
        P("batch", "rows", "cols", None),
        P("batch", "rows", "cols"),
        P(),
        P(),
        P(),
        P(),
        P(),
    )
    return jax.shard_map(
        body,
        mesh=mesh,
        in_specs=placed,
        out_specs=(
            P("batch", None, "rows", "cols"),
            P(),
            P(),
            P(),
            P(),
            P(),
            P(),
            P("batch", "rows", "cols", None),
        ),
        check_vma=False,
    )
```

profile of v0, /device:TPU:1, one launch (start us, length us, event | category | flops | bytes accessed | tf_op | source)
XLA Modules:
  0.0 455.8 jit_solution(9587879471108387762)
XLA Ops:
  7.2 1.2 reshape.268
  8.4 32.1 %all_to_all.15 = bf16[128,2,512]{2,1,0:T(2,128)(2,1)S(1)} all-to-all(bf16[128,2,512]{2,1,0:T(2,128)(2,1)S(1)} %reshape.268), channel_id=1, replica_groups=mesh['rows'=8,'cols'=16,'batch'=2] {'rows','cols'}, dimensions={0} | all-to-all | bytes 524288 | tf_op jit(solution)/shard_map/all_to_all | solution.py:24
  42.6 1.3 copy-done.31
  46.2 6.0 %all-to-all-start.1 = ((bf16[128,2,512]{2,1,0:T(2,128)(2,1)}), bf16[128,2,512]{2,1,0:T(2,128)(2,1)S(1)}, u32[]{:S(2)}, u32[]{:S(2)}) async-start(bf16[128,2,512]{2,1,0:T(2,128)(2,1)} %copy.70), calls=%async_computation.1 | async-start | bytes 524288 | tf_op jit(solution)/shard_map/all_to_all | solution.py:24
  52.4 16.1 %all-to-all-done.1 = bf16[128,2,512]{2,1,0:T(2,128)(2,1)S(1)} async-done(((bf16[128,2,512]{2,1,0:T(2,128)(2,1)}), bf16[128,2,512]{2,1,0:T(2,128)(2,1)S(1)}, u32[]{:S(2)}, u32[]{:S(2)}) %all-to-all-start.1) | async-done | bytes 262176 | tf_op jit(solution)/shard_map/all_to_all | solution.py:24
  70.8 1.9 collective-permute-start
  72.7 2.4 collective-permute-start.1
  75.6 3.3 collective-permute-done.1
  78.9 1.3 collective-permute-start.3
  80.2 4.2 collective-permute-start.2
  88.1 1.4 fusion.12
  94.4 1.1 convolution_bitcast_fusion.6
  95.6 1.1 convolution_bitcast_fusion.9
  99.3 1.9 collective-permute-start.5
  101.2 4.5 collective-permute-start.4
  108.1 3.4 collective-permute-start.7
  111.5 1.5 collective-permute-start.6
  113.9 2.1 collective-permute-done.6
  118.9 3.5 broadcast_multiply_fusion
  122.4 1.3 reduce_sum.38
  123.7 1.1 convolution_convert_fusion.3
  125.6 18.3 %all-to-all-start.2 = ((bf16[128,2,512]{2,1,0:T(2,128)(2,1)}), bf16[128,2,512]{2,1,0:T(2,128)(2,1)S(1)}, u32[]{:S(2)}, u32[]{:S(2)}) async-start(bf16[128,2,512]{2,1,0:T(2,128)(2,1)} %reshape.293), calls=%async_computation.2 | async-start | bytes 524288 | tf_op jit(solution)/shard_map/all_to_all | solution.py:24
  147.9 12.4 %all-to-all-done.2 = bf16[128,2,512]{2,1,0:T(2,128)(2,1)S(1)} async-done(((bf16[128,2,512]{2,1,0:T(2,128)(2,1)}), bf16[128,2,512]{2,1,0:T(2,128)(2,1)S(1)}, u32[]{:S(2)}, u32[]{:S(2)}) %all-to-all-start.2) | async-done | bytes 262176 | tf_op jit(solution)/shard_map/all_to_all | solution.py:24
  160.8 2.3 convolution_convert_fusion.1
  163.1 1.9 fusion.155
  165.0 4.2 fusion.24
  169.2 4.2 fusion.27
  173.4 1.3 convolution_bitcast_fusion.1
  174.7 2.2 convolution_bitcast_fusion
  178.2 73.5 %all-reduce = (f32[]{:T(128)}, f32[128,9]{0,1:T(8,128)}) all-reduce(f32[]{:T(128)} %get-tuple-element.55, f32[128,9]{0,1:T(8,128)S(1)} %convolution_bitcast_fusion.12), channel_id=1, replica_groups=mesh['rows'=8,'cols'=16,'batch'=2] {'rows','cols','batch'}, use_global_device_ids=true, to_apply=%region_3.4 | all-reduce | flops 1153 | bytes 9224 | tf_op jit(solution)/shard_map/psum | solution.py:159
  253.1 188.4 %all-reduce.4.cloned.1.call-done = (f32[512,1536]{0,1:T(8,128)}, f32[512,512]{1,0:T(8,128)}, f32[512,128]{1,0:T(8,128)}, f32[3,3,128,128]{3,2,1,0:T(8,128)}) async-done(((f32[512,1536]{0,1:T(8,128)}, f32[512,512]{1,0:T(8,128)}, f32[512,128]{1,0:T(8,128)}, f32[3,3,128,128]{3,2,1,0:T(8,128)}), (f32[512,1536]{0,1:T(8,128)}, f32[512,512]{1,0:T(8,128)}, f32[512,128]{1,0:T(8,128)}, ...) | async-done | bytes 5046288 | tf_op jit(solution)/shard_map/psum | solution.py:159
  441.5 3.7 copy.88
  (135 shorter events, 34.1 us)
Async XLA Ops:
  7.2 33.3 %copy-start = (bf16[512,1536]{1,0:T(8,128)(2,1)S(1)}, bf16[512,1536]{1,0:T(8,128)(2,1)}, u32[]{:S(2)}) copy-start(bf16[512,1536]{1,0:T(8,128)(2,1)} %param.11) | copy-start | bytes 4718596
  41.5 2.8 copy-start.22
  41.7 2.6 copy-start.10
  44.3 8.0 %copy-start.15 = (bf16[2,16,32,128]{3,2,1,0:T(8,128)(2,1)}, bf16[2,16,32,128]{3,2,1,0:T(8,128)(2,1)S(1)}, u32[]{:S(2)}) copy-start(bf16[2,16,32,128]{3,2,1,0:T(8,128)(2,1)S(1)} %convolution_convert_fusion.5) | copy-start | bytes 786436
  44.3 8.0 %copy-start.25 = (s32[1,32,128]{2,1,0:T(8,128)S(1)}, s32[1,32,128]{2,1,0:T(8,128)}, u32[]{:S(2)}) copy-start(s32[1,32,128]{2,1,0:T(8,128)} %param.10) | copy-start | bytes 49156
  44.3 24.2 %copy-start.13 = (bf16[1,8,32,512]{3,2,1,0:T(8,128)(2,1)S(1)}, bf16[1,8,32,512]{3,2,1,0:T(8,128)(2,1)}, u32[]{:S(2)}) copy-start(bf16[1,8,32,512]{3,2,1,0:T(8,128)(2,1)} %param.9) | copy-start | bytes 786436
  44.3 24.2 %copy-start.18 = (bf16[512,128]{1,0:T(8,128)(2,1)S(1)}, bf16[512,128]{1,0:T(8,128)(2,1)}, u32[]{:S(2)}) copy-start(bf16[512,128]{1,0:T(8,128)(2,1)} %param.13) | copy-start | bytes 393220
  46.2 22.2 %all-to-all-start.1 = ((bf16[128,2,512]{2,1,0:T(2,128)(2,1)}), bf16[128,2,512]{2,1,0:T(2,128)(2,1)S(1)}, u32[]{:S(2)}, u32[]{:S(2)}) async-start(bf16[128,2,512]{2,1,0:T(2,128)(2,1)} %copy.70), calls=%async_computation.1 | async-start | bytes 524288 | tf_op jit(solution)/shard_map/all_to_all | solution.py:24
  52.3 38.3 %copy-start.27 = (f32[9]{0:T(128)}, f32[9]{0:T(128)S(1)}, u32[]{:S(2)}) copy-start(f32[9]{0:T(128)S(1)} %broadcast_subtract_fusion) | copy-start | bytes 112
  52.3 38.2 %copy-start.29 = (f32[9]{0:T(128)}, f32[9]{0:T(128)S(1)}, u32[]{:S(2)}) copy-start(f32[9]{0:T(128)S(1)} %convert_multiply_fusion) | copy-start | bytes 112
  69.9 5.2 %copy-start.9 = (bf16[3,3,128,128]{3,2,1,0:T(8,128)(2,1)S(1)}, bf16[3,3,128,128]{3,2,1,0:T(8,128)(2,1)}, u32[]{:S(2)}) copy-start(bf16[3,3,128,128]{3,2,1,0:T(8,128)(2,1)} %param.14) | copy-start | bytes 884740
  70.8 4.8 %collective-permute-start = (bf16[1,1,128,128]{3,2,1,0:T(8,128)(2,1)S(1)}, bf16[1,1,128,128]{3,2,1,0:T(8,128)(2,1)S(1)}, u32[]{:S(2)}, u32[]{:S(2)}) collective-permute-start(bf16[1,1,128,128]{3,2,1,0:T(8,128)(2,1)S(1)} %get-tuple-element.48), channel_id=1, source_target_pairs={{0,32},{32,64},{64,96},{96,128},{128,160},{160,192},{192,224},{1,3... | collective-permute-start | bytes 98312 | tf_op jit(solution)/shard_map/ppermute | solution.py:15
  72.7 6.1 %collective-permute-start.1 = (bf16[1,1,128,128]{3,2,1,0:T(8,128)(2,1)S(1)}, bf16[1,1,128,128]{3,2,1,0:T(8,128)(2,1)S(1)}, u32[]{:S(2)}, u32[]{:S(2)}) collective-permute-start(bf16[1,1,128,128]{3,2,1,0:T(8,128)(2,1)S(1)} %get-tuple-element.49), channel_id=1, source_target_pairs={{32,0},{64,32},{96,64},{128,96},{160,128},{192,160},{224,192},{33,... | collective-permute-start | bytes 98312 | tf_op jit(solution)/shard_map/ppermute | solution.py:18
  78.9 6.3 %collective-permute-start.3 = (bf16[1,34,1,128]{3,2,1,0:T(2,128)(2,1)S(1)}, bf16[1,34,1,128]{3,2,1,0:T(2,128)(2,1)S(1)}, u32[]{:S(2)}, u32[]{:S(2)}) collective-permute-start(bf16[1,34,1,128]{3,2,1,0:T(2,128)(2,1)S(1)} %get-tuple-element.44), channel_id=1, source_target_pairs={{2,0},{4,2},{6,4},{8,6},{10,8},{12,10},{14,12},{16,14},{18,16},{20... | collective-permute-start | bytes 26120 | tf_op jit(solution)/shard_map/ppermute | solution.py:18
  80.2 5.0 %collective-permute-start.2 = (bf16[1,34,1,128]{3,2,1,0:T(2,128)(2,1)S(1)}, bf16[1,34,1,128]{3,2,1,0:T(2,128)(2,1)S(1)}, u32[]{:S(2)}, u32[]{:S(2)}) collective-permute-start(bf16[1,34,1,128]{3,2,1,0:T(2,128)(2,1)S(1)} %get-tuple-element.45), channel_id=1, source_target_pairs={{0,2},{2,4},{4,6},{6,8},{8,10},{10,12},{12,14},{14,16},{16,18},{18... | collective-permute-start | bytes 26120 | tf_op jit(solution)/shard_map/ppermute | solution.py:15
  99.3 8.7 %collective-permute-start.5 = (bf16[1,1,128,128]{3,2,1,0:T(8,128)(2,1)S(1)}, bf16[1,1,128,128]{3,2,1,0:T(8,128)(2,1)S(1)}, u32[]{:S(2)}, u32[]{:S(2)}) collective-permute-start(bf16[1,1,128,128]{3,2,1,0:T(8,128)(2,1)S(1)} %get-tuple-element.46), channel_id=1, source_target_pairs={{32,0},{64,32},{96,64},{128,96},{160,128},{192,160},{224,192},{33,... | collective-permute-start | bytes 98312 | tf_op jit(solution)/shard_map/ppermute | solution.py:18
  101.2 6.8 %collective-permute-start.4 = (bf16[1,1,128,128]{3,2,1,0:T(8,128)(2,1)S(1)}, bf16[1,1,128,128]{3,2,1,0:T(8,128)(2,1)S(1)}, u32[]{:S(2)}, u32[]{:S(2)}) collective-permute-start(bf16[1,1,128,128]{3,2,1,0:T(8,128)(2,1)S(1)} %get-tuple-element.47), channel_id=1, source_target_pairs={{0,32},{32,64},{64,96},{96,128},{128,160},{160,192},{192,224},{1,3... | collective-permute-start | bytes 98312 | tf_op jit(solution)/shard_map/ppermute | solution.py:15
  108.1 5.8 %collective-permute-start.7 = (bf16[1,34,1,128]{3,2,1,0:T(2,128)(2,1)S(1)}, bf16[1,34,1,128]{3,2,1,0:T(2,128)(2,1)S(1)}, u32[]{:S(2)}, u32[]{:S(2)}) collective-permute-start(bf16[1,34,1,128]{3,2,1,0:T(2,128)(2,1)S(1)} %get-tuple-element.40), channel_id=1, source_target_pairs={{0,2},{2,4},{4,6},{6,8},{8,10},{10,12},{12,14},{14,16},{16,18},{18... | collective-permute-start | bytes 26120 | tf_op jit(solution)/shard_map/ppermute | solution.py:15
  111.5 4.5 collective-permute-start.6
  123.7 23.2 %copy-start.8 = (f32[1,8,32,512]{3,2,1,0:T(8,128)S(1)}, f32[1,8,32,512]{3,2,1,0:T(8,128)}, u32[]{:S(2)}) copy-start(f32[1,8,32,512]{3,2,1,0:T(8,128)} %copy-done.7) | copy-start | bytes 1572868
  123.7 23.2 %copy-start.14 = (bf16[1,8,32,512]{3,2,1,0:T(8,128)(2,1)S(1)}, bf16[1,8,32,512]{3,2,1,0:T(8,128)(2,1)}, u32[]{:S(2)}) copy-start(bf16[1,8,32,512]{3,2,1,0:T(8,128)(2,1)} %param.9) | copy-start | bytes 786436
  123.7 23.2 %copy-start.19 = (bf16[8,32,128]{2,1,0:T(8,128)(2,1)S(1)}, bf16[8,32,128]{2,1,0:T(8,128)(2,1)}, u32[]{:S(2)}) copy-start(bf16[8,32,128]{2,1,0:T(8,128)(2,1)} %reduce_sum.38) | copy-start | bytes 196612
  125.6 34.6 %copy-start.6 = (bf16[512,512]{1,0:T(8,128)(2,1)S(1)}, bf16[512,512]{1,0:T(8,128)(2,1)}, u32[]{:S(2)}) copy-start(bf16[512,512]{1,0:T(8,128)(2,1)} %param.12) | copy-start | bytes 1572868
  125.6 34.6 %all-to-all-start.2 = ((bf16[128,2,512]{2,1,0:T(2,128)(2,1)}), bf16[128,2,512]{2,1,0:T(2,128)(2,1)S(1)}, u32[]{:S(2)}, u32[]{:S(2)}) async-start(bf16[128,2,512]{2,1,0:T(2,128)(2,1)} %reshape.293), calls=%async_computation.2 | async-start | bytes 524288 | tf_op jit(solution)/shard_map/all_to_all | solution.py:24
  144.0 297.6 %all-reduce.4.cloned.1.call-start = ((), (), s32[]{:S(2)}) async-start(), calls=%async_computation.3 | async-start | bytes 10092544 | tf_op jit(solution)/shard_map/psum | solution.py:159
  146.0 14.8 %copy-start.33 = (f32[2,16,128]{2,1,0:T(8,128)S(1)}, f32[2,16,128]{2,1,0:T(8,128)}, u32[]{:S(2)}) copy-start(f32[2,16,128]{2,1,0:T(8,128)} %copy-done.32) | copy-start | bytes 49156
  160.8 2.3 copy-start.11
  163.1 1.9 copy-start.21
  165.0 4.2 copy-start.23
  169.2 4.3 copy-start.16
  441.5 3.7 copy-start.12
  441.5 6.3 %copy-start.1 = (bf16[512,1536]{1,0:T(8,128)(2,1)S(1)}, bf16[512,1536]{1,0:T(8,128)(2,1)}, u32[]{:S(2)}) copy-start(bf16[512,1536]{1,0:T(8,128)(2,1)} %param.11) | copy-start | bytes 4718596
  (13 other events, 16.0 us)
Sparse Core Ops, SparseCore 0:
  177.1 264.4 all-reduce.3
where the time goes:
time: 458 us; the launch traced here: 456 us
  waiting for transfers between devices  222 us (48%)
  blocking collectives  106 us (23%)
  starting transfers between devices  45.6 us (10%)
  matrix products  44.5 us (10%)
  between operations  16.4 us (4%)
  local copies, waits for them, and re-layouts  14.9 us (3%)
  other arithmetic  6.44 us (1%)
    psum x1, waiting for transfers between devices, body(): lax.psum((grad_qkv, grad_out, grad_up, grad_conv, grad_head, loss_part),...  188 us
    psum x1, blocking collectives, body(): lax.psum((grad_qkv, grad_out, grad_up, grad_conv, grad_head, loss_part),...  73.5 us
    all_to_all x1, blocking collectives, regroup(): lax.all_to_all(block, ('rows', 'cols'), split_axis=0, concat_axis=0, tile...  32.1 us
    all_to_all x2, waiting for transfers between devices, regroup(): lax.all_to_all(block, ('rows', 'cols'), split_axis=0, concat_axis=0, tile...  28.4 us
    all_to_all x2, starting transfers between devices, regroup(): lax.all_to_all(block, ('rows', 'cols'), split_axis=0, concat_axis=0, tile...  24.4 us
    ppermute x4, starting transfers between devices, with_halo(): lax.ppermute(lax.slice_in_dim(block, block.shape[dim] - width, None, axis...  14 us
    unnamed x73, local copies, waits for them, and re-layouts  10.7 us
    dot_general x9, matrix products, body(): jnp.einsum('bhwc,bhwk->ck', window, douter_b, preferred_element_type=jnp....  9.96 us
  transfers between devices with their start and end apart: 11, of which 5 were waited for; matrix products, arithmetic and copies ran while one was open for 2% of the time, Pallas kernels for 0%

commit v1 on v0

--- a/solution.py
+++ b/solution.py
@@ -1,10 +1,168 @@
 import jax
 import jax.numpy as jnp
 from jax import lax
+from jax.experimental import pallas as pl
+from jax.experimental.pallas import tpu as pltpu
 from jax.sharding import PartitionSpec as P
 
 HEAD_DIM = 32
 QUANT = 9
+UNITS = 1280
+MESH = pl.DeviceIdType.MESH
+
+
+def meet(targets):
+    barrier = pltpu.get_barrier_semaphore()
+    for target in targets:
+        pl.semaphore_signal(barrier, inc=1, device_id=target, device_id_type=MESH)
+    pl.semaphore_wait(barrier, len(targets))
+
+
+def add_blocks(dst, dst_at, terms, count, step):
+    def one(i, carry):
+        at = i * step
+        total = None
+        for ref, start in terms:
+            value = ref[pl.ds(start + at, step)].astype(jnp.float32)
+            total = value if total is None else total + value
+        dst[pl.ds(dst_at + at, step)] = total.astype(dst.dtype)
+        return carry
+
+    lax.fori_loop(0, count // step, one, 0)
+
+
+def reduce_kernel(g, out, got0, sum0, got1, sum1, got2, sum2, got3, ss0, rs0, ss1, rs1, ss2, rs2, ss3, rs3,
+                  sa3, ra3, sa2, ra2, sa1, ra1, sa0, ra0):
+    row, col, batch = lax.axis_index("rows"), lax.axis_index("cols"), lax.axis_index("batch")
+    core, deep = row % 2, (row // 2) * 2 + batch
+    x, y = col // 4, col % 4
+    first = x * (1 - core) + y * core
+    second = y * (1 - core) + x * core
+    other = {"rows": row + 1 - 2 * core}
+    u0, u1, u2, u3 = UNITS // 2, UNITS // 8, UNITS // 32, UNITS // 256
+
+    def in_first(k):
+        p = (first + k) % 4
+        return p, {"cols": (p * 4 + y) * (1 - core) + (x * 4 + p) * core}
+
+    def in_second(k):
+        p = (second + k) % 4
+        return p, {"cols": (x * 4 + p) * (1 - core) + (p * 4 + y) * core}
+
+    def in_deep(k):
+        p = (deep + k) % 8
+        return p, {"rows": (p // 2) * 2 + core, "batch": p % 2}
+
+    def copy(src, dst, send, recv, to):
+        return pltpu.make_async_remote_copy(src_ref=src, dst_ref=dst, send_sem=send, recv_sem=recv,
+                                            device_id=to, device_id_type=MESH)
+
+    meet([other] + [in_first(k)[1] for k in (1, 2, 3)] + [in_second(k)[1] for k in (1, 2, 3)]
+         + [in_deep(k)[1] for k in range(1, 8)])
+
+    near = []
+    for q in range(4):
+        c = copy(g.at[pl.ds((1 - core) * u0 + q * u1, u1)], got0.at[pl.ds(q * u1, u1)], ss0.at[q], rs0.at[q], other)
+        c.start()
+        near.append(c)
+    for c in near:
+        c.wait()
+    add_blocks(sum0, 0, [(g, core * u0), (got0, 0)], u0, 8)
+
+    def scatter(src, size, got, total, send, recv, where, mine, n, step):
+        copies = []
+        for k in range(1, n):
+            p, to = where(k)
+            c = copy(src.at[pl.ds(p * size, size)], got.at[k - 1], send.at[k - 1], recv.at[k - 1], to)
+            c.start()
+            copies.append(c)
+        for c in copies:
+            c.wait()
+        def one(i, carry):
+            at = i * step
+            value = src[pl.ds(mine * size + at, step)].astype(jnp.float32)
+            for k in range(n - 1):
+                value = value + got[k, pl.ds(at, step)].astype(jnp.float32)
+            total(at, step, value)
+            return carry
+        lax.fori_loop(0, size // step, one, 0)
+
+    def keep(ref, base):
+        def store(at, step, value):
+            ref[pl.ds(base + at, step)] = value.astype(ref.dtype)
+        return store
+
+    scatter(sum0, u1, got1, keep(sum1, 0), ss1, rs1, in_first, first, 4, 8)
+    scatter(sum1, u2, got2, keep(sum2, 0), ss2, rs2, in_second, second, 4, 8)
+    place = core * u0 + first * u1 + second * u2
+    scatter(sum2, u3, got3, keep(out, place + deep * u3), ss3, rs3, in_deep, deep, 8, 5)
+
+    def gather(start, size, send, recv, where, n):
+        copies = []
+        block = out.at[pl.ds(start, size)]
+        for k in range(1, n):
+            c = copy(block, block, send.at[k - 1], recv.at[k - 1], where(k)[1])
+            c.start()
+            copies.append(c)
+        for c in copies:
+            c.wait()
+
+    gather(place + deep * u3, u3, sa3, ra3, in_deep, 8)
+    gather(place, u2, sa2, ra2, in_second, 4)
+    gather(core * u0 + first * u1, u1, sa1, ra1, in_first, 4)
+    gather(core * u0, u0, sa0, ra0, lambda k: (0, other), 2)
+
+
+def reduce_units(g):
+    unit = (8, 128)
+    b16 = jnp.bfloat16
+    dma = pltpu.SemaphoreType.DMA
+    return pl.pallas_call(
+        reduce_kernel,
+        out_shape=jax.ShapeDtypeStruct((UNITS,) + unit, b16),
+        in_specs=[pl.BlockSpec(memory_space=pltpu.VMEM)],
+        out_specs=pl.BlockSpec(memory_space=pltpu.VMEM),
+        scratch_shapes=[
+            pltpu.VMEM((UNITS // 2,) + unit, b16),
+            pltpu.VMEM((UNITS // 2,) + unit, b16),
+            pltpu.VMEM((3, UNITS // 8) + unit, b16),
+            pltpu.VMEM((UNITS // 8,) + unit, b16),
+            pltpu.VMEM((3, UNITS // 32) + unit, b16),
+            pltpu.VMEM((UNITS // 32,) + unit, b16),
+            pltpu.VMEM((7, UNITS // 256) + unit, b16),
+            dma((4,)), dma((4,)), dma((3,)), dma((3,)), dma((3,)), dma((3,)), dma((7,)), dma((7,)),
+            dma((7,)), dma((7,)), dma((3,)), dma((3,)), dma((3,)), dma((3,)), dma((1,)), dma((1,)),
+        ],
+        compiler_params=pltpu.CompilerParams(collective_id=7, has_side_effects=True,
+                                             vmem_limit_bytes=40 * 1024 * 1024),
+    )(g)
+
+
+def tiles(array):
+    rows, columns = array.shape
+    return array.reshape(rows // 8, 8, columns // 128, 128).transpose(0, 2, 1, 3).reshape(-1, 8, 128)
+
+
+def untile(units, rows, columns):
+    return units.reshape(rows // 8, columns // 128, 8, 128).transpose(0, 2, 1, 3).reshape(rows, columns)
+
+
+def reduce_all(grad_qkv, grad_out, grad_up, grad_conv, grad_head, loss_row):
+    tail = jnp.concatenate([grad_head.T, loss_row, jnp.zeros((6, 128), jnp.float32)], axis=0)
+    parts = [tiles(grad_qkv), tiles(grad_out), tiles(grad_up), tiles(grad_conv.reshape(1152, 128)), tail.reshape(2, 8, 128)]
+    used = sum(part.shape[0] for part in parts)
+    parts.append(jnp.zeros((UNITS - used, 8, 128), jnp.float32))
+    g = jnp.concatenate([part.astype(jnp.bfloat16) for part in parts], axis=0)
+    total = reduce_units(g).astype(jnp.float32)
+    tail = total[1232:1234].reshape(16, 128)
+    return (
+        untile(total[:768], 512, 1536),
+        untile(total[768:1024], 512, 512),
+        untile(total[1024:1088], 512, 128),
+        total[1088:1232].reshape(3, 3, 128, 128),
+        tail[:9].T,
+        jnp.sum(tail[9]),
+    )
 
 
 def with_halo(block, sides, width):
@@ -82,9 +240,10 @@
     groups = coarse_rows * coarse_cols // peers
     grid_tokens = regroup(coarse.reshape(peers, groups, width))
     result, saved = attend(grid_tokens, w_qkv, w_out)
-    attended = regroup(result.astype(jnp.bfloat16)).reshape(coarse.shape)
-    context = (coarse.astype(jnp.float32) + attended.astype(jnp.float32)).astype(jnp.bfloat16)
-    lifted = jnp.einsum("bijw,wc->bijc", context, w_up, preferred_element_type=jnp.float32)
+    attended = result.astype(jnp.bfloat16)
+    context = (grid_tokens.astype(jnp.float32) + attended.astype(jnp.float32)).astype(jnp.bfloat16)
+    raised = jnp.einsum("sgw,wc->sgc", context, w_up, preferred_element_type=jnp.float32).astype(jnp.bfloat16)
+    lifted = regroup(raised).reshape(samples, coarse_rows, coarse_cols, channels).astype(jnp.float32)
     spread = jnp.repeat(jnp.repeat(lifted, 4, axis=1), 4, axis=2)
     hidden = fine_input.astype(jnp.float32) + spread
     active = jax.nn.gelu(hidden).astype(jnp.bfloat16)
@@ -107,7 +266,7 @@
     weight_term = jnp.where(error_term < 0.0, 1.0 - levels, levels)
     magnitude = jnp.abs(error_term)
     huber_term = jnp.where(magnitude <= 1.0, 0.5 * error_term * error_term, magnitude - 0.5)
-    loss_part = jnp.sum(weight_term * huber_term)
+    loss_part = jnp.sum(weight_term * huber_term, axis=(0, 1, 2)).reshape(1, 128)
     pixel_count = (
         samples
         * lax.axis_size("batch")
@@ -150,14 +309,14 @@
         .sum(axis=(2, 4))
         .astype(jnp.bfloat16)
     )
-    grad_up = jnp.einsum("bijw,bijc->wc", context, dlift, preferred_element_type=jnp.float32)
-    dcontext = jnp.einsum("bijc,wc->bijw", dlift, w_up, preferred_element_type=jnp.float32).astype(
+    grid_lift = regroup(dlift.reshape(peers, groups, channels))
+    grad_up = jnp.einsum("sgw,sgc->wc", context, grid_lift, preferred_element_type=jnp.float32)
+    grid_grads = jnp.einsum("sgc,wc->sgw", grid_lift, w_up, preferred_element_type=jnp.float32).astype(
         jnp.bfloat16
     )
-    grid_grads = regroup(dcontext.reshape(peers, groups, width))
     grad_qkv, grad_out = attend_back(grid_tokens, w_out, saved, grid_grads)
-    grad_qkv, grad_out, grad_up, grad_conv, grad_head, loss_total = lax.psum(
-        (grad_qkv, grad_out, grad_up, grad_conv, grad_head, loss_part), ("rows", "cols", "batch")
+    grad_qkv, grad_out, grad_up, grad_conv, grad_head, loss_total = reduce_all(
+        grad_qkv, grad_out, grad_up, grad_conv, grad_head, loss_part
     )
     loss_value = loss_total / (pixel_count * QUANT)
     return (quantiles, loss_value, grad_qkv, grad_out, grad_up, grad_conv, grad_head, grad_fine)

time: 458 us -> 220 us (0.48)
  waiting for transfers between devices: 222 us -> 41.4 us
  blocking collectives: 106 us -> 0 us
  Pallas kernels: 0 us -> 52.9 us
  starting transfers between devices: 45.6 us -> 62 us
  between operations: 16.4 us -> 3.1 us
  matrix products: 44.5 us -> 37.2 us
    psum x1 -> x0, waiting for transfers between devices: 188 us -> none  [body(): lax.psum((grad_qkv, grad_out, grad_up, grad_conv, grad_head, loss_part),...]
    psum x1 -> x0, blocking collectives: 73.5 us -> none  [body(): lax.psum((grad_qkv, grad_out, grad_up, grad_conv, grad_head, loss_part),...]
    pallas_call x0 -> x1, Pallas kernels: none -> 52.9 us  [reduce_units(): pl.pallas_call(reduce_kernel, out_shape=jax.ShapeDtypeStruct((UNITS,) + u...]
    all_to_all x1 -> x0, blocking collectives: 32.1 us -> none  [regroup(): lax.all_to_all(block, ('rows', 'cols'), split_axis=0, concat_axis=0, tile...]
    all_to_all x2 -> x3, starting transfers between devices: 24.4 us -> 39.9 us  [regroup(): lax.all_to_all(block, ('rows', 'cols'), split_axis=0, concat_axis=0, tile...]
    unnamed x73 -> x58, local copies, waits for them, and re-layouts: 10.7 us -> 3.06 us
    all_to_all x2 -> x3, waiting for transfers between devices: 28.4 us -> 35.5 us  [regroup(): lax.all_to_all(block, ('rows', 'cols'), split_axis=0, concat_axis=0, tile...]
    dot_general x9, matrix products: 9.96 us -> 4.96 us  [body(): jnp.einsum('bhwc,bhwk->ck', window, douter_b, preferred_element_type=jnp....]
  transfers between devices with their start and end apart: 11 -> 11, of which waited for: 5 -> 5; matrix products, arithmetic and copies ran while one was open for 2% -> 4% of each run, Pallas kernels for 0% -> 0%
where the time goes in v1:
time: 220 us; the launch traced here: 219 us
  starting transfers between devices  62 us (28%)
  Pallas kernels  52.9 us (24%)
  waiting for transfers between devices  41.4 us (19%)
  matrix products  37.2 us (17%)
  local copies, waits for them, and re-layouts  13.7 us (6%)
  other arithmetic  8.51 us (4%)
  between operations  3.1 us (1%)
    pallas_call x1, Pallas kernels, reduce_units(): pl.pallas_call(reduce_kernel, out_shape=jax.ShapeDtypeStruct((UNITS,) + u...  52.9 us
    all_to_all x3, starting transfers between devices, regroup(): lax.all_to_all(block, ('rows', 'cols'), split_axis=0, concat_axis=0, tile...  39.9 us
    all_to_all x3, waiting for transfers between devices, regroup(): lax.all_to_all(block, ('rows', 'cols'), split_axis=0, concat_axis=0, tile...  35.5 us
    ppermute x4, starting transfers between devices, with_halo(): lax.ppermute(lax.slice_in_dim(block, block.shape[dim] - width, None, axis...  15.4 us
    dot_general x9, matrix products, body(): jnp.einsum('bhwk,ck->bhwc', back_window, w_conv[row_tap, col_tap], prefer...  7.05 us
    ppermute x4, starting transfers between devices, with_halo(): lax.ppermute(lax.slice_in_dim(block, 0, width, axis=dim), axis, backward)  6.65 us
    ppermute x4, waiting for transfers between devices, with_halo(): lax.ppermute(lax.slice_in_dim(block, 0, width, axis=dim), axis, backward)  5.87 us
    dot_general x9, matrix products, body(): jnp.einsum('bhwc,bhwk->ck', window, douter_b, preferred_element_type=jnp....  4.96 us
  transfers between devices with their start and end apart: 11, of which 5 were waited for; matrix products, arithmetic and copies ran while one was open for 4% of the time, Pallas kernels for 0%

profile of v1, /device:TPU:1, one launch (start us, length us, event | category | flops | bytes accessed | tf_op | source)
XLA Modules:
  0.0 218.7 jit_solution(7579393940480019786)
XLA Ops:
  0.6 1.9 reshape.281
  2.5 16.4 %all-to-all-start = ((bf16[128,2,512]{2,1,0:T(2,128)(2,1)}), bf16[128,2,512]{2,1,0:T(2,128)(2,1)S(1)}, u32[]{:S(2)}, u32[]{:S(2)}) async-start(bf16[128,2,512]{2,1,0:T(2,128)(2,1)} %reshape.281), calls=%async_computation | async-start | bytes 524288 | tf_op jit(solution)/shard_map/all_to_all | solution.py:182
  19.7 15.1 %all-to-all-done = bf16[128,2,512]{2,1,0:T(2,128)(2,1)S(1)} async-done(((bf16[128,2,512]{2,1,0:T(2,128)(2,1)}), bf16[128,2,512]{2,1,0:T(2,128)(2,1)S(1)}, u32[]{:S(2)}, u32[]{:S(2)}) %all-to-all-start) | async-done | bytes 262176 | tf_op jit(solution)/shard_map/all_to_all | solution.py:182
  36.0 2.2 %fusion.177 = (f32[2,16,128]{2,1,0:T(8,128)S(1)}, f32[2,16,128,128]{2,3,1,0:T(8,128)}) fusion(bf16[128,2,16,32]{0,3,2,1:T(8,128)(2,1)S(1)} %bitcast.428, bf16[128,2,16,32]{0,3,2,1:T(8,128)(2,1)S(1)} %bitcast.426), kind=kOutput, calls=%fused_computation.240 | convolution fusion | flops 35127424 | bytes 2637824 | tf_op jit(solution)/shard_map/sub | solution.py:198
  38.2 2.0 convolution_convert_fusion.5
  42.3 6.0 %all-to-all-start.1 = ((bf16[128,2,128]{2,1,0:T(2,128)(2,1)}), bf16[128,2,128]{2,1,0:T(2,128)(2,1)S(1)}, u32[]{:S(2)}, u32[]{:S(2)}) async-start(bf16[128,2,128]{2,1,0:T(2,128)(2,1)} %copy.75), calls=%async_computation.1 | async-start | bytes 131072 | tf_op jit(solution)/shard_map/all_to_all | solution.py:182
  48.4 11.7 %all-to-all-done.1 = bf16[128,2,128]{2,1,0:T(2,128)(2,1)S(1)} async-done(((bf16[128,2,128]{2,1,0:T(2,128)(2,1)}), bf16[128,2,128]{2,1,0:T(2,128)(2,1)S(1)}, u32[]{:S(2)}, u32[]{:S(2)}) %all-to-all-start.1) | async-done | bytes 65568 | tf_op jit(solution)/shard_map/all_to_all | solution.py:182
  61.4 3.2 %collective-permute-start = (bf16[1,1,128,128]{3,2,1,0:T(8,128)(2,1)S(1)}, bf16[1,1,128,128]{3,2,1,0:T(8,128)(2,1)S(1)}, u32[]{:S(2)}, u32[]{:S(2)}) collective-permute-start(bf16[1,1,128,128]{3,2,1,0:T(8,128)(2,1)S(1)} %get-tuple-element.42), channel_id=1, source_target_pairs={{0,32},{32,64},{64,96},{96,128},{128,160},{160,192},{192,224},{1,3... | collective-permute-start | bytes 98312 | tf_op jit(solution)/shard_map/ppermute | solution.py:173
  64.6 1.9 collective-permute-start.1
  67.0 3.8 %collective-permute-done.1 = bf16[1,1,128,128]{3,2,1,0:T(8,128)(2,1)S(1)} collective-permute-done((bf16[1,1,128,128]{3,2,1,0:T(8,128)(2,1)S(1)}, bf16[1,1,128,128]{3,2,1,0:T(8,128)(2,1)S(1)}, u32[]{:S(2)}, u32[]{:S(2)}) %collective-permute-start.1) | collective-permute-done | bytes 32800 | tf_op jit(solution)/shard_map/ppermute | solution.py:176
  70.8 1.3 collective-permute-start.3
  72.1 4.2 %collective-permute-start.2 = (bf16[1,34,1,128]{3,2,1,0:T(2,128)(2,1)S(1)}, bf16[1,34,1,128]{3,2,1,0:T(2,128)(2,1)S(1)}, u32[]{:S(2)}, u32[]{:S(2)}) collective-permute-start(bf16[1,34,1,128]{3,2,1,0:T(2,128)(2,1)S(1)} %get-tuple-element.39), channel_id=1, source_target_pairs={{0,2},{2,4},{4,6},{6,8},{8,10},{10,12},{12,14},{14,16},{16,18},{18... | collective-permute-start | bytes 26120 | tf_op jit(solution)/shard_map/ppermute | solution.py:173
  80.0 1.5 fusion.14
  86.6 1.9 collective-permute-start.5
  88.6 4.5 %collective-permute-start.4 = (bf16[1,1,128,128]{3,2,1,0:T(8,128)(2,1)S(1)}, bf16[1,1,128,128]{3,2,1,0:T(8,128)(2,1)S(1)}, u32[]{:S(2)}, u32[]{:S(2)}) collective-permute-start(bf16[1,1,128,128]{3,2,1,0:T(8,128)(2,1)S(1)} %get-tuple-element.41), channel_id=1, source_target_pairs={{0,32},{32,64},{64,96},{96,128},{128,160},{160,192},{192,224},{1,3... | collective-permute-start | bytes 98312 | tf_op jit(solution)/shard_map/ppermute | solution.py:173
  93.1 1.1 fusion.49
  95.5 3.5 %collective-permute-start.7 = (bf16[1,34,1,128]{3,2,1,0:T(2,128)(2,1)S(1)}, bf16[1,34,1,128]{3,2,1,0:T(2,128)(2,1)S(1)}, u32[]{:S(2)}, u32[]{:S(2)}) collective-permute-start(bf16[1,34,1,128]{3,2,1,0:T(2,128)(2,1)S(1)} %get-tuple-element.34), channel_id=1, source_target_pairs={{0,2},{2,4},{4,6},{6,8},{8,10},{10,12},{12,14},{14,16},{16,18},{18... | collective-permute-start | bytes 26120 | tf_op jit(solution)/shard_map/ppermute | solution.py:173
  98.9 1.5 collective-permute-start.6
  101.3 2.1 collective-permute-done.6
  106.4 3.6 %broadcast_multiply_fusion = (f32[1,32,128,128]{3,2,1,0:T(8,128)}, f32[1,32,128,128]{3,2,1,0:T(8,128)S(1)}) fusion(f32[1,32,128,128]{3,2,1,0:T(8,128)S(1)} %bitcast.408, bf16[1,32,128,128]{3,2,1,0:T(8,128)(2,1)S(1)} %copy-done.2, bf16[3,3,128,128]{3,2,1,0:T(8,128)(2,1)S(1)} %copy-done.9, bf16[1,34,129,128]{3,2,1,0:T(8,128)(2,1)S(1)} %get-tuple-element.32, ...), kind=kOutput, calls=%fused_computation.119 | convolution fusion | flops 150470656 | bytes 27295744 | tf_op jit(solution)/shard_map/bhwk,ck->bhwc/dot_general | solution.py:296
  109.9 1.3 reduce_sum.46
  111.2 17.5 %all-to-all-start.2 = ((bf16[128,2,128]{2,1,0:T(2,128)(2,1)}), bf16[128,2,128]{2,1,0:T(2,128)(2,1)S(1)}, u32[]{:S(2)}, u32[]{:S(2)}) async-start(bf16[128,2,128]{2,1,0:T(2,128)(2,1)} %bitcast.65), calls=%async_computation.2 | async-start | bytes 131072 | tf_op jit(solution)/shard_map/all_to_all | solution.py:182
  130.2 1.6 pad_maximum_fusion.6
  131.9 8.7 %all-to-all-done.2 = bf16[128,2,128]{2,1,0:T(2,128)(2,1)S(1)} async-done(((bf16[128,2,128]{2,1,0:T(2,128)(2,1)}), bf16[128,2,128]{2,1,0:T(2,128)(2,1)S(1)}, u32[]{:S(2)}, u32[]{:S(2)}) %all-to-all-start.2) | async-done | bytes 65568 | tf_op jit(solution)/shard_map/all_to_all | solution.py:182
  141.3 3.0 %convolution_convert_fusion.1 = bf16[2,16,32,128]{3,2,1,0:T(8,128)(2,1)} fusion(bf16[128,2,16,32]{0,3,2,1:T(8,128)(2,1)S(1)} %bitcast.419, f32[2,16,128,128]{2,3,1,0:T(8,128)} %get-tuple-element.48, f32[2,16,128]{2,1,0:T(8,128)S(1)} %copy-done.25), kind=kOutput, calls=%fused_computation.37 | convolution fusion | flops 34734080 | bytes 2637824 | tf_op jit(solution)/shard_map/ghst,sghd->tghd/dot_general | solution.py:219
  145.3 3.7 %fusion.27 = bf16[2,16,32,128]{3,2,1,0:T(8,128)(2,1)} fusion(bf16[128,2,16,32]{0,3,2,1:T(8,128)(2,1)S(1)} %bitcast.427, f32[2,16,128,128]{2,3,1,0:T(8,128)S(1)} %fusion.179, f32[2,16,128,128]{2,3,1,0:T(8,128)} %get-tuple-element.48, f32[2,16,128]{2,1,0:T(8,128)S(1)} %copy-done.26), kind=kOutput, calls=%fused_computation.35 | convolution fusion | flops 37359744 | bytes 4734976 | tf_op jit(solution)/shard_map/ghst,tghd->sghd/dot_general | solution.py:222
  149.0 3.7 %fusion.30 = bf16[2,16,32,128]{3,2,1,0:T(8,128)(2,1)} fusion(bf16[128,2,16,32]{0,3,2,1:T(8,128)(2,1)S(1)} %bitcast.429, f32[2,16,128,128]{2,3,1,0:T(8,128)S(1)} %fusion.179, f32[2,16,128,128]{2,3,1,0:T(8,128)} %get-tuple-element.48, f32[2,16,128]{2,1,0:T(8,128)S(1)} %copy-done.26), kind=kOutput, calls=%fused_computation.36 | convolution fusion | flops 37359744 | bytes 4734976 | tf_op jit(solution)/shard_map/ghst,sghd->tghd/dot_general | solution.py:223
  152.7 0.9 copy.84
  153.6 1.7 fusion.3
  157.9 52.9 %shard_map.143 = bf16[1280,8,128]{2,1,0:T(8,128)(2,1)S(1)} custom-call(bf16[1280,8,128]{2,1,0:T(8,128)(2,1)S(1)} %broadcast_dynamic-update-slice_fusion.g), custom_call_target="tpu_custom_call" | custom-call | tf_op jit(solution)/shard_map/pallas_call | solution.py:120
  211.7 1.0 slice.227
  212.7 1.9 slice.226
  (132 shorter events, 28.4 us)
Async XLA Ops:
  0.6 34.2 %copy-start = (bf16[512,1536]{1,0:T(8,128)(2,1)S(1)}, bf16[512,1536]{1,0:T(8,128)(2,1)}, u32[]{:S(2)}) copy-start(bf16[512,1536]{1,0:T(8,128)(2,1)} %param.11) | copy-start | bytes 4718596
  2.5 32.3 %all-to-all-start = ((bf16[128,2,512]{2,1,0:T(2,128)(2,1)}), bf16[128,2,512]{2,1,0:T(2,128)(2,1)S(1)}, u32[]{:S(2)}, u32[]{:S(2)}) async-start(bf16[128,2,512]{2,1,0:T(2,128)(2,1)} %reshape.281), calls=%async_computation | async-start | bytes 524288 | tf_op jit(solution)/shard_map/all_to_all | solution.py:182
  35.6 4.6 %copy-start.19 = (bf16[128,2,512]{0,2,1:T(8,128)(2,1)}, bf16[128,2,512]{0,2,1:T(8,128)(2,1)S(1)}, u32[]{:S(2)}) copy-start(bf16[128,2,512]{0,2,1:T(8,128)(2,1)S(1)} %copy.72) | copy-start | bytes 786436
  35.8 4.5 %copy-start.21 = (bf16[128,2,512]{0,2,1:T(8,128)(2,1)}, bf16[128,2,512]{0,2,1:T(8,128)(2,1)S(1)}, u32[]{:S(2)}) copy-start(bf16[128,2,512]{0,2,1:T(8,128)(2,1)S(1)} %copy.71) | copy-start | bytes 786436
  36.0 4.3 %copy-start.11 = (bf16[128,2,512]{0,2,1:T(8,128)(2,1)}, bf16[128,2,512]{0,2,1:T(8,128)(2,1)S(1)}, u32[]{:S(2)}) copy-start(bf16[128,2,512]{0,2,1:T(8,128)(2,1)S(1)} %copy.70) | copy-start | bytes 786436
  38.2 2.1 copy-start.24
  38.2 2.8 %copy-start.7 = (bf16[512,512]{1,0:T(8,128)(2,1)S(1)}, bf16[512,512]{1,0:T(8,128)(2,1)}, u32[]{:S(2)}) copy-start(bf16[512,512]{1,0:T(8,128)(2,1)} %param.12) | copy-start | bytes 1572868
  38.2 3.1 %copy-start.16 = (bf16[512,128]{1,0:T(8,128)(2,1)S(1)}, bf16[512,128]{1,0:T(8,128)(2,1)}, u32[]{:S(2)}) copy-start(bf16[512,128]{1,0:T(8,128)(2,1)} %param.13) | copy-start | bytes 393220
  41.3 19.2 %copy-start.3 = (bf16[128,2,512]{2,0,1:T(8,128)(2,1)}, bf16[128,2,512]{2,0,1:T(8,128)(2,1)S(1)}, u32[]{:S(2)}) copy-start(bf16[128,2,512]{2,0,1:T(8,128)(2,1)S(1)} %fusion.35) | copy-start | bytes 786436
  41.4 19.2 %copy-start.2 = (bf16[1,32,128,128]{3,2,1,0:T(8,128)(2,1)S(1)}, bf16[1,32,128,128]{3,2,1,0:T(8,128)(2,1)}, u32[]{:S(2)}) copy-start(bf16[1,32,128,128]{3,2,1,0:T(8,128)(2,1)} %param.8) | copy-start | bytes 3145732
  42.3 17.8 %all-to-all-start.1 = ((bf16[128,2,128]{2,1,0:T(2,128)(2,1)}), bf16[128,2,128]{2,1,0:T(2,128)(2,1)S(1)}, u32[]{:S(2)}, u32[]{:S(2)}) async-start(bf16[128,2,128]{2,1,0:T(2,128)(2,1)} %copy.75), calls=%async_computation.1 | async-start | bytes 131072 | tf_op jit(solution)/shard_map/all_to_all | solution.py:182
  60.5 6.0 %copy-start.9 = (bf16[3,3,128,128]{3,2,1,0:T(8,128)(2,1)S(1)}, bf16[3,3,128,128]{3,2,1,0:T(8,128)(2,1)}, u32[]{:S(2)}) copy-start(bf16[3,3,128,128]{3,2,1,0:T(8,128)(2,1)} %param.14) | copy-start | bytes 884740
  61.4 5.6 %collective-permute-start = (bf16[1,1,128,128]{3,2,1,0:T(8,128)(2,1)S(1)}, bf16[1,1,128,128]{3,2,1,0:T(8,128)(2,1)S(1)}, u32[]{:S(2)}, u32[]{:S(2)}) collective-permute-start(bf16[1,1,128,128]{3,2,1,0:T(8,128)(2,1)S(1)} %get-tuple-element.42), channel_id=1, source_target_pairs={{0,32},{32,64},{64,96},{96,128},{128,160},{160,192},{192,224},{1,3... | collective-permute-start | bytes 98312 | tf_op jit(solution)/shard_map/ppermute | solution.py:173
  64.6 6.1 %collective-permute-start.1 = (bf16[1,1,128,128]{3,2,1,0:T(8,128)(2,1)S(1)}, bf16[1,1,128,128]{3,2,1,0:T(8,128)(2,1)S(1)}, u32[]{:S(2)}, u32[]{:S(2)}) collective-permute-start(bf16[1,1,128,128]{3,2,1,0:T(8,128)(2,1)S(1)} %get-tuple-element.43), channel_id=1, source_target_pairs={{32,0},{64,32},{96,64},{128,96},{160,128},{192,160},{224,192},{33,... | collective-permute-start | bytes 98312 | tf_op jit(solution)/shard_map/ppermute | solution.py:176
  70.8 6.3 %collective-permute-start.3 = (bf16[1,34,1,128]{3,2,1,0:T(2,128)(2,1)S(1)}, bf16[1,34,1,128]{3,2,1,0:T(2,128)(2,1)S(1)}, u32[]{:S(2)}, u32[]{:S(2)}) collective-permute-start(bf16[1,34,1,128]{3,2,1,0:T(2,128)(2,1)S(1)} %get-tuple-element.38), channel_id=1, source_target_pairs={{2,0},{4,2},{6,4},{8,6},{10,8},{12,10},{14,12},{16,14},{18,16},{20... | collective-permute-start | bytes 26120 | tf_op jit(solution)/shard_map/ppermute | solution.py:176
  72.1 5.0 %collective-permute-start.2 = (bf16[1,34,1,128]{3,2,1,0:T(2,128)(2,1)S(1)}, bf16[1,34,1,128]{3,2,1,0:T(2,128)(2,1)S(1)}, u32[]{:S(2)}, u32[]{:S(2)}) collective-permute-start(bf16[1,34,1,128]{3,2,1,0:T(2,128)(2,1)S(1)} %get-tuple-element.39), channel_id=1, source_target_pairs={{0,2},{2,4},{4,6},{6,8},{8,10},{10,12},{12,14},{14,16},{16,18},{18... | collective-permute-start | bytes 26120 | tf_op jit(solution)/shard_map/ppermute | solution.py:173
  80.0 1.5 copy-start.23
  86.6 8.8 %collective-permute-start.5 = (bf16[1,1,128,128]{3,2,1,0:T(8,128)(2,1)S(1)}, bf16[1,1,128,128]{3,2,1,0:T(8,128)(2,1)S(1)}, u32[]{:S(2)}, u32[]{:S(2)}) collective-permute-start(bf16[1,1,128,128]{3,2,1,0:T(8,128)(2,1)S(1)} %get-tuple-element.40), channel_id=1, source_target_pairs={{32,0},{64,32},{96,64},{128,96},{160,128},{192,160},{224,192},{33,... | collective-permute-start | bytes 98312 | tf_op jit(solution)/shard_map/ppermute | solution.py:176
  88.6 6.8 %collective-permute-start.4 = (bf16[1,1,128,128]{3,2,1,0:T(8,128)(2,1)S(1)}, bf16[1,1,128,128]{3,2,1,0:T(8,128)(2,1)S(1)}, u32[]{:S(2)}, u32[]{:S(2)}) collective-permute-start(bf16[1,1,128,128]{3,2,1,0:T(8,128)(2,1)S(1)} %get-tuple-element.41), channel_id=1, source_target_pairs={{0,32},{32,64},{64,96},{96,128},{128,160},{160,192},{192,224},{1,3... | collective-permute-start | bytes 98312 | tf_op jit(solution)/shard_map/ppermute | solution.py:173
  95.5 5.9 %collective-permute-start.7 = (bf16[1,34,1,128]{3,2,1,0:T(2,128)(2,1)S(1)}, bf16[1,34,1,128]{3,2,1,0:T(2,128)(2,1)S(1)}, u32[]{:S(2)}, u32[]{:S(2)}) collective-permute-start(bf16[1,34,1,128]{3,2,1,0:T(2,128)(2,1)S(1)} %get-tuple-element.34), channel_id=1, source_target_pairs={{0,2},{2,4},{4,6},{6,8},{8,10},{10,12},{12,14},{14,16},{16,18},{18... | collective-permute-start | bytes 26120 | tf_op jit(solution)/shard_map/ppermute | solution.py:173
  98.9 4.5 %collective-permute-start.6 = (bf16[1,34,1,128]{3,2,1,0:T(2,128)(2,1)S(1)}, bf16[1,34,1,128]{3,2,1,0:T(2,128)(2,1)S(1)}, u32[]{:S(2)}, u32[]{:S(2)}) collective-permute-start(bf16[1,34,1,128]{3,2,1,0:T(2,128)(2,1)S(1)} %get-tuple-element.35), channel_id=1, source_target_pairs={{2,0},{4,2},{6,4},{8,6},{10,8},{12,10},{14,12},{16,14},{18,16},{20... | collective-permute-start | bytes 26120 | tf_op jit(solution)/shard_map/ppermute | solution.py:176
  109.9 19.6 %copy-start.6 = (f32[32,128,9]{1,2,0:T(8,128)S(1)}, f32[32,128,9]{1,2,0:T(8,128)}, u32[]{:S(2)}) copy-start(f32[32,128,9]{1,2,0:T(8,128)} %copy-done.5) | copy-start | bytes 442372
  109.9 20.3 %copy-start.18 = (bf16[1,3,128,128]{3,2,1,0:T(8,128)(2,1)S(1)}, bf16[1,3,128,128]{3,2,1,0:T(8,128)(2,1)}, u32[]{:S(2)}) copy-start(bf16[1,3,128,128]{3,2,1,0:T(8,128)(2,1)} %get-tuple-element.55) | copy-start | bytes 294916
  109.9 30.7 %copy-start.17 = (bf16[512,128]{1,0:T(8,128)(2,1)S(1)}, bf16[512,128]{1,0:T(8,128)(2,1)}, u32[]{:S(2)}) copy-start(bf16[512,128]{1,0:T(8,128)(2,1)} %param.13) | copy-start | bytes 393220
  109.9 30.9 %copy-start.8 = (bf16[512,512]{1,0:T(8,128)(2,1)S(1)}, bf16[512,512]{1,0:T(8,128)(2,1)}, u32[]{:S(2)}) copy-start(bf16[512,512]{1,0:T(8,128)(2,1)} %param.12) | copy-start | bytes 1572868
  111.2 30.1 %copy-start.25 = (f32[2,16,128]{2,1,0:T(8,128)S(1)}, f32[2,16,128]{2,1,0:T(8,128)}, u32[]{:S(2)}) copy-start(f32[2,16,128]{2,1,0:T(8,128)} %copy-done.24) | copy-start | bytes 49156
  111.2 29.3 %all-to-all-start.2 = ((bf16[128,2,128]{2,1,0:T(2,128)(2,1)}), bf16[128,2,128]{2,1,0:T(2,128)(2,1)S(1)}, u32[]{:S(2)}, u32[]{:S(2)}) async-start(bf16[128,2,128]{2,1,0:T(2,128)(2,1)} %bitcast.65), calls=%async_computation.2 | async-start | bytes 131072 | tf_op jit(solution)/shard_map/all_to_all | solution.py:182
  141.3 3.0 %copy-start.12 = (bf16[128,2,512]{0,2,1:T(8,128)(2,1)S(1)}, bf16[128,2,512]{0,2,1:T(8,128)(2,1)}, u32[]{:S(2)}) copy-start(bf16[128,2,512]{0,2,1:T(8,128)(2,1)} %copy-done.11) | copy-start | bytes 786436
  145.3 3.7 %copy-start.22 = (bf16[128,2,512]{0,2,1:T(8,128)(2,1)S(1)}, bf16[128,2,512]{0,2,1:T(8,128)(2,1)}, u32[]{:S(2)}) copy-start(bf16[128,2,512]{0,2,1:T(8,128)(2,1)} %copy-done.21) | copy-start | bytes 786436
  156.0 1.4 copy-start.4
  156.0 1.7 copy-start.10
  214.6 3.0 %copy-start.1 = (bf16[512,1536]{1,0:T(8,128)(2,1)S(1)}, bf16[512,1536]{1,0:T(8,128)(2,1)}, u32[]{:S(2)}) copy-start(bf16[512,1536]{1,0:T(8,128)(2,1)} %param.11) | copy-start | bytes 4718596
  (6 other events, 5.5 us)

commit v2 on v1

v2 whole, which is shorter than its diff:
```python
import jax
import jax.numpy as jnp
import numpy as np
from jax import lax
from jax.experimental import pallas as pl
from jax.experimental.pallas import tpu as pltpu
from jax.sharding import PartitionSpec as P

HEAD_DIM = 32
QUANT = 9
UNITS = 1280
MESH = pl.DeviceIdType.MESH


def meet(targets):
    barrier = pltpu.get_barrier_semaphore()
    for target in targets:
        pl.semaphore_signal(barrier, inc=1, device_id=target, device_id_type=MESH)
    pl.semaphore_wait(barrier, len(targets))


def add_blocks(dst, dst_at, terms, count, step):
    def one(i, carry):
        at = i * step
        total = None
        for ref, start in terms:
            value = ref[pl.ds(start + at, step)].astype(jnp.float32)
            total = value if total is None else total + value
        dst[pl.ds(dst_at + at, step)] = total.astype(dst.dtype)
        return carry

    lax.fori_loop(0, count // step, one, 0)


def reduce_kernel(g, out, got0, sum0, got1, sum1, got2, sum2, got3, ss0, rs0, ss1, rs1, ss2, rs2, ss3, rs3,
                  sa3, ra3, sa2, ra2, sa1, ra1, sa0, ra0):
    row, col, batch = lax.axis_index("rows"), lax.axis_index("cols"), lax.axis_index("batch")
    core, deep = row % 2, (row // 2) * 2 + batch
    x, y = col // 4, col % 4
    first = x * (1 - core) + y * core
    second = y * (1 - core) + x * core
    other = {"rows": row + 1 - 2 * core}
    u0, u1, u2, u3 = UNITS // 2, UNITS // 8, UNITS // 32, UNITS // 256

    def in_first(k):
        p = (first + k) % 4
        return p, {"cols": (p * 4 + y) * (1 - core) + (x * 4 + p) * core}

    def in_second(k):
        p = (second + k) % 4
        return p, {"cols": (x * 4 + p) * (1 - core) + (p * 4 + y) * core}

    def in_deep(k):
        p = (deep + k) % 8
        return p, {"rows": (p // 2) * 2 + core, "batch": p % 2}

    def copy(src, dst, send, recv, to):
        return pltpu.make_async_remote_copy(src_ref=src, dst_ref=dst, send_sem=send, recv_sem=recv,
                                            device_id=to, device_id_type=MESH)

    meet([other] + [in_first(k)[1] for k in (1, 2, 3)] + [in_second(k)[1] for k in (1, 2, 3)]
         + [in_deep(k)[1] for k in range(1, 8)])

    near = []
    for q in range(4):
        c = copy(g.at[pl.ds((1 - core) * u0 + q * u1, u1)], got0.at[pl.ds(q * u1, u1)], ss0.at[q], rs0.at[q], other)
        c.start()
        near.append(c)
    for c in near:
        c.wait()
    add_blocks(sum0, 0, [(g, core * u0), (got0, 0)], u0, 8)

    def scatter(src, size, got, total, send, recv, where, mine, n, step):
        copies = []
        for k in range(1, n):
            p, to = where(k)
            c = copy(src.at[pl.ds(p * size, size)], got.at[k - 1], send.at[k - 1], recv.at[k - 1], to)
            c.start()
            copies.append(c)
        for c in copies:
            c.wait()
        def one(i, carry):
            at = i * step
            value = src[pl.ds(mine * size + at, step)].astype(jnp.float32)
            for k in range(n - 1):
                value = value + got[k, pl.ds(at, step)].astype(jnp.float32)
            total(at, step, value)
            return carry
        lax.fori_loop(0, size // step, one, 0)

    def keep(ref, base):
        def store(at, step, value):
            ref[pl.ds(base + at, step)] = value.astype(ref.dtype)
        return store

    scatter(sum0, u1, got1, keep(sum1, 0), ss1, rs1, in_first, first, 4, 8)
    scatter(sum1, u2, got2, keep(sum2, 0), ss2, rs2, in_second, second, 4, 8)
    place = core * u0 + first * u1 + second * u2
    scatter(sum2, u3, got3, keep(out, place + deep * u3), ss3, rs3, in_deep, deep, 8, 5)

    def gather(start, size, send, recv, where, n):
        copies = []
        block = out.at[pl.ds(start, size)]
        for k in range(1, n):
            c = copy(block, block, send.at[k - 1], recv.at[k - 1], where(k)[1])
            c.start()
            copies.append(c)
        for c in copies:
            c.wait()

    gather(place + deep * u3, u3, sa3, ra3, in_deep, 8)
    gather(place, u2, sa2, ra2, in_second, 4)
    gather(core * u0 + first * u1, u1, sa1, ra1, in_first, 4)
    gather(core * u0, u0, sa0, ra0, lambda k: (0, other), 2)


def reduce_units(g):
    unit = (8, 128)
    b16 = jnp.bfloat16
    dma = pltpu.SemaphoreType.DMA
    return pl.pallas_call(
        reduce_kernel,
        out_shape=jax.ShapeDtypeStruct((UNITS,) + unit, b16),
        in_specs=[pl.BlockSpec(memory_space=pltpu.VMEM)],
        out_specs=pl.BlockSpec(memory_space=pltpu.VMEM),
        scratch_shapes=[
            pltpu.VMEM((UNITS // 2,) + unit, b16),
            pltpu.VMEM((UNITS // 2,) + unit, b16),
            pltpu.VMEM((3, UNITS // 8) + unit, b16),
            pltpu.VMEM((UNITS // 8,) + unit, b16),
            pltpu.VMEM((3, UNITS // 32) + unit, b16),
            pltpu.VMEM((UNITS // 32,) + unit, b16),
            pltpu.VMEM((7, UNITS // 256) + unit, b16),
            dma((4,)), dma((4,)), dma((3,)), dma((3,)), dma((3,)), dma((3,)), dma((7,)), dma((7,)),
            dma((7,)), dma((7,)), dma((3,)), dma((3,)), dma((3,)), dma((3,)), dma((1,)), dma((1,)),
        ],
        compiler_params=pltpu.CompilerParams(collective_id=7, has_side_effects=True,
                                             vmem_limit_bytes=40 * 1024 * 1024),
    )(g)


F32, B16 = jnp.float32, jnp.bfloat16
DMA = pltpu.SemaphoreType.DMA
SCALE = HEAD_DIM ** (-0.5)
LIMIT = 56 * 1024 * 1024


def onehot(rows, cols, pairs):
    table = np.zeros((rows, cols), np.float32)
    for row, col in pairs:
        table[row, col] = 1.0
    return jnp.asarray(table, B16)


def mid_table():
    return onehot(256, 256, [(p * 16 + r * 2 + m, r * 32 + p * 2 + m)
                             for p in range(16) for r in range(8) for m in range(2)])


def group_table():
    return onehot(256, 256, [(m * 128 + c * 8 + r, c * 16 + r * 2 + m)
                             for m in range(2) for c in range(16) for r in range(8)])


def back_table():
    pairs = []
    for r in range(8):
        for j in range(32):
            pairs.append((r * 48 + j, (1 + j // 2) * 16 + r * 2 + j % 2))
        pairs.append((r * 48 + 32, 17 * 16 + r * 2))
        pairs.append((r * 48 + 35, r * 2 + 1))
    return onehot(384, 288, pairs)


def pick_table(first):
    return onehot(16, 128, [(2 * i + s, 16 * i + first + s) for i in range(8) for s in range(2)])


def spread_table(first):
    return onehot(128, 16, [(16 * i + first + s, 2 * i + s) for i in range(8) for s in range(2)])


def bins_table():
    return onehot(48, 64, [(0, 15)] + [(1 + y, 16 + y) for y in range(32)] + [(33, 48)])


def up_table():
    return onehot(144, 48, [(p, p // 4) for p in range(144)])


def sum_table():
    return onehot(32, 128, [(p // 4, p) for p in range(128)])


def dot(a, b):
    return jnp.dot(a, b, preferred_element_type=F32)


def dot_nt(a, b):
    return lax.dot_general(a, b, (((1,), (1,)), ((), ())), preferred_element_type=F32)


def rcopy(src, dst, send, recv, to):
    return pltpu.make_async_remote_copy(src_ref=src, dst_ref=dst, send_sem=send, recv_sem=recv,
                                        device_id=to, device_id_type=MESH)


def row_peers(row):
    return [{"rows": (row + k) % 8} for k in range(1, 8)]


def col_peers(col):
    return [{"cols": (col + k) % 16} for k in range(1, 16)]


def rows_out(src, got, send, recv, row):
    copies = []
    for k in range(1, 8):
        p = (row + k) % 8
        c = rcopy(src.at[p], got.at[row], send.at[k - 1], recv.at[k - 1], {"rows": p})
        c.start()
        copies.append(c)
    got[row] = src[row]
    return copies


def cols_out(src, got, send, recv, col):
    copies = []
    for k in range(1, 16):
        p = (col + k) % 16
        c = rcopy(src.at[p], got.at[col], send.at[k - 1], recv.at[k - 1], {"cols": p})
        c.start()
        copies.append(c)
    got[col] = src[col]
    return copies


def wait_all(copies):
    for c in copies:
        c.wait()


def tokens_kernel(coarse, fine, bins, mid, pick_lo, pick_hi, spread_lo, spread_hi, place, tokens, field, rain, rain_lo, rain_hi,
                  got, turned, bin_got, edge_out, edge_in, bin_out, s_r, r_r, s_c, r_c, s_h, r_h, s_e, r_e, s_l):
    row, col = lax.axis_index("rows"), lax.axis_index("cols")
    meet(row_peers(row) + col_peers(col))
    own = pltpu.make_async_copy(fine, field.at[pl.ds(4, 32), pl.ds(0, 128)], s_l.at[0])
    own.start()
    first = rows_out(coarse, got, s_r, r_r, row)

    def halo(start):
        lower, upper = row > 0, row < 7

        def down():
            for n, (src, dst) in enumerate([
                (fine.at[pl.ds(30, 2)], field.at[pl.ds(2, 2), pl.ds(0, 128)]),
                (bins.at[pl.ds(16, 16)], bin_got.at[pl.ds(0, 16)]),
            ]):
                c = rcopy(src, dst, s_h.at[n], r_h.at[n], {"rows": row + 1})
                c.start() if start else c.wait_send()

        def up():
            for n, (src, dst) in enumerate([
                (fine.at[pl.ds(0, 2)], field.at[pl.ds(36, 2), pl.ds(0, 128)]),
                (bins.at[pl.ds(0, 16)], bin_got.at[pl.ds(48, 16)]),
            ]):
                c = rcopy(src, dst, s_h.at[2 + n], r_h.at[2 + n], {"rows": row - 1})
                c.start() if start else c.wait_send()

        def from_low():
            for n, (src, dst) in enumerate([
                (fine.at[pl.ds(30, 2)], field.at[pl.ds(2, 2), pl.ds(0, 128)]),
                (bins.at[pl.ds(16, 16)], bin_got.at[pl.ds(0, 16)]),
            ]):
                rcopy(src, dst, s_h.at[n], r_h.at[n], {"rows": row - 1}).wait_recv()

        def from_high():
            for n, (src, dst) in enumerate([
                (fine.at[pl.ds(0, 2)], field.at[pl.ds(36, 2), pl.ds(0, 128)]),
                (bins.at[pl.ds(0, 16)], bin_got.at[pl.ds(48, 16)]),
            ]):
                rcopy(src, dst, s_h.at[2 + n], r_h.at[2 + n], {"rows": row + 1}).wait_recv()

        pl.when(upper)(down)
        pl.when(lower)(up)
        if not start:
            pl.when(lower)(from_low)
            pl.when(upper)(from_high)

    halo(True)

    @pl.when(row == 0)
    def _():
        field[pl.ds(0, 4), :128] = jnp.zeros((4, 128, 128), B16)
        bin_got[pl.ds(0, 16)] = jnp.zeros((16, 128), B16)

    @pl.when(row > 0)
    def _():
        field[pl.ds(0, 2), :128] = jnp.zeros((2, 128, 128), B16)

    @pl.when(row == 7)
    def _():
        field[pl.ds(36, 4), :128] = jnp.zeros((4, 128, 128), B16)
        bin_got[pl.ds(48, 16)] = jnp.zeros((16, 128), B16)

    @pl.when(row < 7)
    def _():
        field[pl.ds(38, 2), :128] = jnp.zeros((2, 128, 128), B16)

    bin_got[pl.ds(16, 32)] = bins[...]

    wait_all(first)
    turned[...] = dot(mid[...], got[...].reshape(256, 512)).astype(B16).reshape(16, 16, 512)
    second = cols_out(turned, tokens, s_c, r_c, col)

    own.wait()
    halo(False)
    rows = dot(place[...], bin_got[...])
    rain[...] = rows
    bin_out[0] = jnp.broadcast_to(rows[:, 127:128], (48, 128)).astype(B16)
    bin_out[1] = jnp.broadcast_to(rows[:, 0:1], (48, 128)).astype(B16)
    for q in range(5):
        edge_out[0, q] = dot(pick_hi[...], field[8 * q:8 * q + 8, 112:128].reshape(128, 128)).astype(B16)
        edge_out[1, q] = dot(pick_lo[...], field[8 * q:8 * q + 8, 0:16].reshape(128, 128)).astype(B16)

    @pl.when(col == 0)
    def _():
        edge_in[0] = jnp.zeros((5, 16, 128), B16)
        rain_lo[...] = jnp.zeros((48, 128), B16)

    @pl.when(col == 15)
    def _():
        edge_in[1] = jnp.zeros((5, 16, 128), B16)
        rain_hi[...] = jnp.zeros((48, 128), B16)

    def sides(side, to):
        into = (rain_lo, rain_hi)[side]
        return [rcopy(edge_out.at[side], edge_in.at[side], s_e.at[2 * side], r_e.at[2 * side], {"cols": to}),
                rcopy(bin_out.at[side], into, s_e.at[2 * side + 1], r_e.at[2 * side + 1], {"cols": to})]

    @pl.when(col < 15)
    def _():
        for c in sides(0, col + 1):
            c.start()

    @pl.when(col > 0)
    def _():
        for c in sides(1, col - 1):
            c.start()

    @pl.when(col < 15)
    def _():
        for c in sides(0, col + 1):
            c.wait_send()
        for c in sides(1, col + 1):
            c.wait_recv()

    @pl.when(col > 0)
    def _():
        for c in sides(1, col - 1):
            c.wait_send()
        for c in sides(0, col - 1):
            c.wait_recv()

    for q in range(5):
        edge = dot(spread_hi[...], edge_in[0, q]) + dot(spread_lo[...], edge_in[1, q])
        field[8 * q:8 * q + 8, 128:144] = edge.astype(B16).reshape(8, 16, 128)
    wait_all(second)


def vmem(shape, dtype):
    return pltpu.VMEM(shape, dtype)


def call(kernel, out, scratch, args, collective=None, hbm=()):
    extra = {} if collective is None else {"collective_id": collective, "has_side_effects": True}
    return pl.pallas_call(
        kernel,
        out_shape=[jax.ShapeDtypeStruct(shape, dtype) for shape, dtype in out],
        in_specs=[pl.BlockSpec(memory_space=pl.ANY if n in hbm else pltpu.VMEM) for n in range(len(args))],
        out_specs=[pl.BlockSpec(memory_space=pltpu.VMEM) for _ in out],
        scratch_shapes=scratch,
        compiler_params=pltpu.CompilerParams(vmem_limit_bytes=LIMIT, **extra),
    )(*args)


def lift_kernel(raised, back, lifted, slots, turned, s_c, r_c, s_x, r_x, s_r, r_r, s_y, r_y):
    row, col = lax.axis_index("rows"), lax.axis_index("cols")
    meet(row_peers(row) + col_peers(col))

    def spread(count, axis, me, src, low, main, copies_sems, extra_sems):
        send, recv = copies_sems
        send_x, recv_x = extra_sems
        copies = []
        for k in range(1, count):
            p = (me + k) % count
            c = rcopy(src.at[p], main.at[1 + me], send.at[k - 1], recv.at[k - 1], {axis: p})
            c.start()
            copies.append(c)
        main[1 + me] = src[me]

        def after(t):
            return rcopy(src.at[t - 1], main.at[0], send_x.at[t], recv_x.at[0], {axis: t})

        def before(t):
            return rcopy(src.at[t + 1], main.at[count + 1], send_x.at[t], recv_x.at[1], {axis: t})

        @pl.when(me == count - 1)
        def _():
            for t in range(1, count - 1):
                after(t).start()
            main[0] = src[count - 2]
            main[count + 1] = jnp.zeros(main.shape[1:], B16)

        @pl.when(me == 0)
        def _():
            for t in range(1, count - 1):
                before(t).start()
            main[count + 1] = src[1]
            main[0] = jnp.zeros(main.shape[1:], B16)

        @pl.when(me == count - 1)
        def _():
            for t in range(1, count - 1):
                after(t).wait_send()

        @pl.when(me == 0)
        def _():
            for t in range(1, count - 1):
                before(t).wait_send()

        @pl.when((me > 0) & (me < count - 1))
        def _():
            after(1).wait_recv()
            before(1).wait_recv()

        wait_all(copies)

    spread(16, "cols", col, raised, None, slots, (s_c, r_c), (s_x, r_x))
    turned[...] = dot(back[...], slots[...].reshape(288, 128)).astype(B16).reshape(8, 48, 128)
    spread(8, "rows", row, turned, None, lifted, (s_r, r_r), (s_y, r_y))


def fold_kernel(dlift, mid, out, got, turned, s_r, r_r, s_c, r_c):
    row, col = lax.axis_index("rows"), lax.axis_index("cols")
    meet(row_peers(row) + col_peers(col))
    wait_all(rows_out(dlift, got, s_r, r_r, row))
    turned[...] = dot(mid[...], got[...].reshape(256, 128)).astype(B16).reshape(16, 16, 128)
    wait_all(cols_out(turned, out, s_c, r_c, col))


def head_mask(h):
    lane = lax.broadcasted_iota(jnp.int32, (1, 128), 1)
    return jnp.where((lane >> 5) == h, 1.0, 0.0).astype(B16)


def heads_down(tile):
    return jnp.concatenate([tile * head_mask(h) for h in range(4)], axis=0)


def heads_across(tile):
    turned = tile.astype(F32).T
    line = lax.broadcasted_iota(jnp.int32, (128, 1), 0) >> 5
    return jnp.concatenate([jnp.where(line == h, turned, 0.0) for h in range(4)], axis=1).astype(B16)


def side_by_side(stack):
    return jnp.concatenate([stack[h * 128:(h + 1) * 128] for h in range(4)], axis=1)


def attend_kernel(tokens, w_qkv, w_out, w_up, group, ungroup, raised, tok, qkv, prob, mixed, context):
    tok[...] = dot(group[...], tokens[...]).astype(B16)
    for n in range(3):
        qkv[:, n * 512:(n + 1) * 512] = dot(tok[...], w_qkv[:, n * 512:(n + 1) * 512]).astype(B16)
    for g in range(2):
        for t in range(4):
            rows, at = slice(g * 128, g * 128 + 128), t * 128
            query = qkv[rows, at:at + 128]
            keyed = qkv[rows, 512 + at:512 + at + 128]
            valued = qkv[rows, 1024 + at:1024 + at + 128]
            scores = dot_nt(heads_down(query), keyed) * SCALE
            peak = jnp.max(scores, axis=-1, keepdims=True)
            powers = jnp.exp(scores - peak)
            share = powers / jnp.sum(powers, axis=-1, keepdims=True)
            prob[g * 4 + t] = share
            mixed[rows, at:at + 128] = dot(side_by_side(share.astype(B16)), heads_down(valued)).astype(B16)
    attended = dot(mixed[...], w_out[...]).astype(B16)
    context[...] = (tok[...].astype(F32) + attended.astype(F32)).astype(B16)
    lifted = dot(context[...], w_up[...]).astype(B16)
    raised[...] = dot(ungroup[...], lifted).astype(B16)


def put(g, at, value):
    rows, cols = value.shape
    size = rows // 8
    for n in range(cols // 128):
        g[at + n * size:at + (n + 1) * size] = value[:, n * 128:(n + 1) * 128].reshape(size, 8, 128).astype(B16)


def attend_back_kernel(folded, group, w_out, w_up, tok, qkv, prob, mixed, context, local, g, dquery, dkey, dvalue):
    lift = dot(group[...], folded[...]).astype(B16)
    dcontext = dot_nt(lift, w_up[...]).astype(B16)
    mix_grad = dot_nt(dcontext, w_out[...]).astype(B16)
    g[1088:1234] = local[...]
    g[1234:UNITS] = jnp.zeros((UNITS - 1234, 8, 128), B16)
    for s in range(2):
        for t in range(4):
            rows, at = slice(s * 128, s * 128 + 128), t * 128
            query = qkv[rows, at:at + 128]
            keyed = qkv[rows, 512 + at:512 + at + 128]
            valued = qkv[rows, 1024 + at:1024 + at + 128]
            mine = mix_grad[rows, at:at + 128]
            dprob = dot_nt(heads_down(mine), valued)
            share = prob[s * 4 + t]
            inner = jnp.sum(share * dprob, axis=-1, keepdims=True)
            dscore = (share * (dprob - inner) * SCALE).astype(B16)
            dquery[rows, at:at + 128] = dot(side_by_side(dscore), heads_down(keyed)).astype(B16)
            dkey[at:at + 128, rows] = dot(heads_across(query), dscore).astype(B16)
            dvalue[at:at + 128, rows] = dot(heads_across(mine), share.astype(B16)).astype(B16)
    turned = tok[...].astype(F32).T.astype(B16)
    put(g, 0, dot(turned, dquery[...]))
    put(g, 256, dot_nt(turned, dkey[...]))
    put(g, 512, dot_nt(turned, dvalue[...]))
    put(g, 768, dot(mixed[...].astype(F32).T.astype(B16), dcontext))
    put(g, 1024, dot(context[...].astype(F32).T.astype(B16), lift))


ROOT_2_PI = 0.7978845608028654


def shifted(line):
    return jnp.concatenate([pltpu.roll(line, 1, 0), line, pltpu.roll(line, 143, 0)], axis=1)


def conv_kernel(field, lifted, rain, rain_lo, rain_hi, up, fold, w_conv, w_head, w_head_t,
                quantiles, grad_fine, dlift, local,
                hidden, slope, active, outer, out_grad, out_wide, out_turned, halo_grad, kernel_sum, loss_sum, head_sum):
    row, col = lax.axis_index("rows"), lax.axis_index("cols")
    place = lax.broadcasted_iota(jnp.int32, (144, 1), 0)
    right = jnp.where(col < 15, 130, 128)
    left = jnp.where(col > 0, 142, 144)
    inside = (place < right) | (place >= left)

    def start(i, carry):
        raised = dot(up[...], lifted[i])
        for s in range(4):
            y = 4 * i + s - 4
            x = field[4 * i + s].astype(F32) + raised
            square = x * x
            bend = jnp.tanh(ROOT_2_PI * x * (1.0 + 0.044715 * square))
            half = 0.5 * (1.0 + bend)
            seen = (row * 32 + y >= 0) & (row * 32 + y < 256)
            act = jnp.where(inside & seen, x * half, 0.0)
            hidden[4 * i + s] = x
            active[4 * i + s] = shifted(act).astype(B16)
            slope[4 * i + s] = half[:128] + (0.5 * ROOT_2_PI) * x[:128] * (1.0 - bend[:128] * bend[:128]) * (
                1.0 + (3 * 0.044715) * square[:128])
        return carry

    lax.fori_loop(0, 10, start, 0)

    def forward(i, carry):
        total = hidden[pl.ds(4 * i + 3, 4)].reshape(576, 128)
        for a in range(3):
            window = active[pl.ds(4 * i + 2 + a, 4)].reshape(576, 384)
            total = total + dot(window, w_conv[a].reshape(384, 128))
        outer[pl.ds(4 * i, 4)] = total.astype(B16).reshape(4, 144, 128)
        return carry

    lax.fori_loop(0, 9, forward, 0)

    def quantile_terms(predicted, target, keep):
        level = (lax.broadcasted_iota(jnp.int32, (16, 1), 0) + 1).astype(F32) / 10.0
        error = target - predicted
        weight = jnp.where(error < 0.0, 1.0 - level, level)
        down = jnp.where(keep, -weight * jnp.clip(error, -1.0, 1.0) * (1.0 / 1024.0), 0.0)
        return error, weight, down

    quant = lax.broadcasted_iota(jnp.int32, (16, 1), 0) < QUANT

    lane = lax.broadcasted_iota(jnp.int32, (48, 640), 1)
    line = lax.broadcasted_iota(jnp.int32, (48, 640), 0)
    wide_lo = jnp.concatenate([rain_lo[...].astype(F32)] * 5, axis=1)
    wide_hi = jnp.concatenate([rain_hi[...].astype(F32)] * 5, axis=1)
    here = (lane >> 4) == line
    edge_bins = jnp.sum(jnp.where(here & ((lane & 15) == 0), wide_hi, 0.0)
                        + jnp.where(here & ((lane & 15) == 15), wide_lo, 0.0), axis=0, keepdims=True)
    edge = jnp.concatenate([outer[:, 128:144, :].reshape(576, 128), jnp.zeros((64, 128), B16)], axis=0)
    predicted = dot_nt(w_head_t[...], edge)
    at = lax.broadcasted_iota(jnp.int32, (1, 640), 1)
    glob = row * 32 + (at >> 4) - 1
    keep = ((((at & 15) == 0) & (col < 15)) | (((at & 15) == 15) & (col > 0))) & (at < 544) & (glob >= 0) & (glob < 256)
    down = quantile_terms(predicted, edge_bins * (1.0 / 16.0) - 1.0, keep & quant)[2].astype(B16)
    halo_grad[...] = dot(down.astype(F32).T.astype(B16), w_head_t[...]).reshape(40, 16, 128)

    loss_sum[...] = jnp.zeros((16, 128), F32)
    head_sum[...] = jnp.zeros((16, 128), F32)
    kernel_sum[...] = jnp.zeros((3, 128, 384), F32)

    def turn(i, carry):
        lines = [rain[pl.ds(4 * i + s, 1), :] for s in range(4)]
        target = jnp.concatenate(lines, axis=1) * (1.0 / 16.0) - 1.0
        pixels = outer[pl.ds(4 * i, 4), :128].reshape(512, 128)
        predicted = dot_nt(w_head_t[...], pixels)
        glob = row * 32 + 4 * i - 1
        at = lax.broadcasted_iota(jnp.int32, (1, 512), 1) >> 7
        mine = (4 * i - 1 + at >= 0) & (4 * i - 1 + at < 32)
        seen = (glob + at >= 0) & (glob + at < 256) & (4 * i - 1 + at < 33)
        error, weight, down = quantile_terms(predicted, target, seen & quant)
        size = jnp.abs(error)
        loss = weight * jnp.where(size <= 1.0, 0.5 * error * error, size - 0.5)
        loss = jnp.where(mine & quant, loss, 0.0)
        loss_sum[...] += loss[:, :128] + loss[:, 128:256] + loss[:, 256:384] + loss[:, 384:]
        down_b = down.astype(B16)
        head_sum[...] += dot(jnp.where(mine, down, 0.0).astype(B16), pixels)
        across = dot(w_head[...], down_b).astype(B16)
        along = dot(down_b.astype(F32).T.astype(B16), w_head_t[...])
        for s in range(4):
            y = 4 * i + s - 1
            value = predicted[:, s * 128:(s + 1) * 128]

            @pl.when((y >= 0) & (y < 32))
            def _():
                for q in range(QUANT):
                    quantiles[q, pl.ds(y, 1), :] = value[q:q + 1]

            out_turned[4 * i + s] = across[:, s * 128:(s + 1) * 128]
            mid_part = along[s * 128:(s + 1) * 128]
            out_grad[4 * i + s] = mid_part
            full = jnp.concatenate([mid_part, halo_grad[4 * i + s]], axis=0)
            out_wide[4 * i + s] = shifted(full).astype(B16)
        return carry

    lax.fori_loop(0, 9, turn, 0)

    def back(i, carry):
        total = None
        for a in range(3):
            window = out_wide[pl.ds(4 * i + a, 4), :128].reshape(512, 384)
            turned = jnp.concatenate([w_conv[2 - a, 2 - b] for b in range(3)], axis=1)
            part = dot_nt(window, turned)
            total = part if total is None else total + part
        across = jnp.concatenate([out_turned[4 * i + 1 + s] for s in range(4)], axis=1)
        for a in range(3):
            window = active[pl.ds(4 * i + 3 + a, 4), :128].reshape(512, 384)
            kernel_sum[a] += dot(across, window)
        dhidden = out_grad[pl.ds(4 * i + 1, 4)] + slope[pl.ds(4 * i + 4, 4)] * total.reshape(4, 128, 128)
        grad_fine[pl.ds(4 * i, 4)] = dhidden * 1024.0
        summed = dhidden[0] + dhidden[1] + dhidden[2] + dhidden[3]
        high = summed.astype(B16)
        low = (summed - high.astype(F32)).astype(B16)
        dlift[i] = (dot(fold[...], high) + dot(fold[...], low)).astype(B16)
        return carry

    lax.fori_loop(0, 8, back, 0)
    for a in range(3):
        for b in range(3):
            local[a * 48 + b * 16:a * 48 + b * 16 + 16] = kernel_sum[a, :, b * 128:(b + 1) * 128].T.reshape(16, 8, 128).astype(B16)
    spot = lax.broadcasted_iota(jnp.int32, (16, 1), 0)
    total = jnp.sum(loss_sum[...], axis=0, keepdims=True)
    tail = jnp.where(spot < QUANT, head_sum[...], jnp.where(spot == QUANT, total, 0.0))
    local[144:146] = tail.reshape(2, 8, 128).astype(B16)


def unpack_kernel(g, grad_qkv, grad_out, grad_up, grad_conv, tail):
    for n in range(12):
        grad_qkv[:, n * 128:(n + 1) * 128] = g[n * 64:(n + 1) * 64].astype(F32).reshape(512, 128)
    for n in range(4):
        grad_out[:, n * 128:(n + 1) * 128] = g[768 + n * 64:768 + (n + 1) * 64].astype(F32).reshape(512, 128)
    grad_up[...] = g[1024:1088].astype(F32).reshape(512, 128)
    grad_conv[...] = g[1088:1232].astype(F32).reshape(1152, 128)
    tail[...] = g[1232:1234].astype(F32).reshape(16, 128)


def body(fine_input, coarse, rain_bins, w_qkv, w_out, w_up, w_conv, w_head):
    fine, bins = fine_input[0], rain_bins[0].astype(B16)
    mid, group = mid_table(), group_table()
    head = jnp.pad(w_head, ((0, 0), (0, 16 - QUANT)))
    head_t = head.T
    tokens, field, rain, rain_lo, rain_hi = call(
        tokens_kernel,
        [((16, 16, 512), B16), ((40, 144, 128), B16), ((48, 128), F32), ((48, 128), B16), ((48, 128), B16)],
        [vmem((8, 32, 512), B16), vmem((16, 16, 512), B16), vmem((64, 128), B16),
         vmem((2, 5, 16, 128), B16), vmem((2, 5, 16, 128), B16), vmem((2, 48, 128), B16),
         DMA((7,)), DMA((7,)), DMA((15,)), DMA((15,)), DMA((4,)), DMA((4,)), DMA((4,)), DMA((4,)), DMA((1,))],
        [coarse[0], fine, bins, mid, pick_table(0), pick_table(14), spread_table(0), spread_table(14), bins_table()],
        collective=1, hbm=(1,),
    )
    raised, tok, qkv, prob, mixed, context = call(
        attend_kernel,
        [((256, 128), B16), ((256, 512), B16), ((256, 1536), B16), ((8, 512, 128), F32), ((256, 512), B16),
         ((256, 512), B16)],
        [],
        [tokens.reshape(256, 512), w_qkv, w_out, w_up, group, group.T],
    )
    lifted, = call(
        lift_kernel,
        [((10, 48, 128), B16)],
        [vmem((18, 16, 128), B16), vmem((8, 48, 128), B16),
         DMA((15,)), DMA((15,)), DMA((16,)), DMA((2,)), DMA((7,)), DMA((7,)), DMA((8,)), DMA((2,))],
        [raised.reshape(16, 16, 128), back_table()],
        collective=2,
    )
    quantiles, grad_fine, dlift, local = call(
        conv_kernel,
        [((9, 32, 128), F32), ((32, 128, 128), F32), ((8, 32, 128), B16), ((146, 8, 128), B16)],
        [vmem((40, 144, 128), F32), vmem((40, 128, 128), F32), vmem((40, 144, 384), B16), vmem((36, 144, 128), B16),
         vmem((36, 128, 128), F32), vmem((36, 144, 384), B16), vmem((36, 128, 128), B16), vmem((40, 16, 128), F32),
         vmem((3, 128, 384), F32), vmem((16, 128), F32), vmem((16, 128), F32)],
        [field, lifted, rain, rain_lo, rain_hi, up_table(), sum_table(), w_conv, head, head_t],
    )
    folded, = call(
        fold_kernel,
        [((16, 16, 128), B16)],
        [vmem((8, 32, 128), B16), vmem((16, 16, 128), B16), DMA((7,)), DMA((7,)), DMA((15,)), DMA((15,))],
        [dlift, mid],
        collective=3,
    )
    g, = call(
        attend_back_kernel,
        [((UNITS, 8, 128), B16)],
        [vmem((256, 512), B16), vmem((512, 256), B16), vmem((512, 256), B16)],
        [folded.reshape(256, 128), group, w_out, w_up, tok, qkv, prob, mixed, context, local],
    )
    grad_qkv, grad_out, grad_up, grad_conv, tail = call(
        unpack_kernel,
        [((512, 1536), F32), ((512, 512), F32), ((512, 128), F32), ((1152, 128), F32), ((16, 128), F32)],
        [],
        [reduce_units(g)],
    )
    loss_value = jnp.sum(tail[QUANT]) / (1048576.0 * QUANT)
    return (quantiles[None], loss_value, grad_qkv, grad_out, grad_up, grad_conv.reshape(3, 3, 128, 128),
            tail[:QUANT].T, grad_fine[None])


def solution(mesh):
    placed = (
        P("batch", "rows", "cols", None),
        P("batch", "rows", "cols", None),
        P("batch", "rows", "cols"),
        P(),
        P(),
        P(),
        P(),
        P(),
    )
    return jax.shard_map(
        body,
        mesh=mesh,
        in_specs=placed,
        out_specs=(
            P("batch", None, "rows", "cols"),
            P(),
            P(),
            P(),
            P(),
            P(),
            P(),
            P("batch", "rows", "cols", None),
        ),
        check_vma=False,
    )
```

time: 220 us -> 168 us (0.76)
  Pallas kernels: 52.9 us -> 155 us
  starting transfers between devices: 62 us -> 0 us
  waiting for transfers between devices: 41.4 us -> 0 us
  matrix products: 37.2 us -> 0 us
  local copies, waits for them, and re-layouts: 13.7 us -> 7.24 us
  other arithmetic: 8.51 us -> 2.61 us
    pallas_call x0 -> x7, Pallas kernels: none -> 99.6 us  [call(): pl.pallas_call(kernel, out_shape=[jax.ShapeDtypeStruct(shape, dtype) for...]
    all_to_all x3 -> x0, starting transfers between devices: 39.9 us -> none  [regroup(): lax.all_to_all(block, ('rows', 'cols'), split_axis=0, concat_axis=0, tile...]
    all_to_all x3 -> x0, waiting for transfers between devices: 35.5 us -> none  [regroup(): lax.all_to_all(block, ('rows', 'cols'), split_axis=0, concat_axis=0, tile...]
    dot_general x43 -> x0, matrix products: 35 us -> none  [the longest x9 7.05 us: body(): jnp.einsum('bhwk,ck->bhwc', back_window, w_conv[row_tap, col_tap], prefer...]
    ppermute x8 -> x0, starting transfers between devices: 22.1 us -> none  [the longest x4 15.4 us: with_halo(): lax.ppermute(lax.slice_in_dim(block, block.shape[dim] - width, None, axis...]
    ppermute x8 -> x0, waiting for transfers between devices: 5.88 us -> none  [the longest x4 5.87 us: with_halo(): lax.ppermute(lax.slice_in_dim(block, 0, width, axis=dim), axis, backward)]
    slice x9 -> x0, local copies, waits for them, and re-layouts: 4.35 us -> none  [the longest x1 1.87 us: reduce_all(): total[:768]]
    another operation x3 -> x0, other arithmetic: 3.11 us -> none  [body(): grad_conv = jnp.stack(kernel_rows)]
  transfers between devices with their start and end apart: 11 -> 0, of which waited for: 5 -> 0; matrix products, arithmetic and copies ran while one was open for 4% -> 0% of each run, Pallas kernels for 0% -> 0%
where the time goes in v2:
time: 168 us; the launch traced here: 167 us
  Pallas kernels  155 us (92%)
  local copies, waits for them, and re-layouts  7.24 us (4%)
  other arithmetic  2.61 us (2%)
  between operations  2.46 us (1%)
    pallas_call x7, Pallas kernels, call(): pl.pallas_call(kernel, out_shape=[jax.ShapeDtypeStruct(shape, dtype) for...  99.6 us
    pallas_call x1, Pallas kernels, reduce_units(): pl.pallas_call(reduce_kernel, out_shape=jax.ShapeDtypeStruct((UNITS,) + u...  55.1 us
    unnamed x5, local copies, waits for them, and re-layouts  4.05 us

profile of v2, /device:TPU:1, one launch (start us, length us, event | category | flops | bytes accessed | tf_op | source)
XLA Modules:
  0.0 167.0 jit_solution(7046453894573518225)
XLA Ops:
  0.6 1.3 pad_bitcast_fusion.w_head_t
  1.9 1.3 convert_bitcast_fusion.bins
  3.2 0.8 copy.27
  4.0 0.6 pad.4.clone.w_head
  4.7 28.6 %shard_map.233 = (bf16[16,16,512]{2,1,0:T(8,128)(2,1)}, bf16[40,144,128]{2,1,0:T(8,128)(2,1)}, f32[48,128]{1,0:T(8,128)}, bf16[48,128]{1,0:T(8,128)(2,1)}, bf16[48,128]{1,0:T(8,128)(2,1)}) custom-call(bf16[8,32,512]{2,1,0:T(8,128)(2,1)} %bitcast.16, bf16[32,128,128]{2,1,0:T(8,128)(2,1)} %bitcast.14, bf16[32,128]{1,0:T(8,128)(2,1)} %convert_bitcast_fusion.bins, ...), custom_call_target="tpu_custom_call" | custom-call | tf_op jit(solution)/shard_map/pallas_call | solution.py:377
  33.3 5.2 %shard_map.234 = (bf16[256,128]{1,0:T(8,128)(2,1)}, bf16[256,512]{1,0:T(8,128)(2,1)}, bf16[256,1536]{1,0:T(8,128)(2,1)}, f32[8,512,128]{2,1,0:T(8,128)}, bf16[25...) custom-call(bf16[256,512]{1,0:T(8,128)(2,1)} %bitcast.17, bf16[512,1536]{1,0:T(8,128)(2,1)} %w_qkv.1, bf16[512,512]{1,0:T(8,128)(2,1)} %w_out.3, ...), custom_call_target="tpu_custom_call" | custom-call | tf_op jit(solution)/shard_map/pallas_call | solution.py:377
  38.5 17.3 %shard_map.235.lifted = bf16[10,48,128]{2,1,0:T(8,128)(2,1)} custom-call(bf16[16,16,128]{2,1,0:T(8,128)(2,1)} %bitcast.18, bf16[384,288]{1,0:T(8,128)(2,1)} %constant.35.clone.back), custom_call_target="tpu_custom_call" | custom-call | tf_op jit(solution)/shard_map/pallas_call | solution.py:377
  55.8 22.1 %shard_map.236 = (f32[9,32,128]{2,1,0:T(8,128)}, f32[32,128,128]{2,1,0:T(8,128)}, bf16[8,32,128]{2,1,0:T(8,128)(2,1)}, bf16[146,8,128]{2,1,0:T(8,128)(2,1)}) custom-call(bf16[40,144,128]{2,1,0:T(8,128)(2,1)} %get-tuple-element.28.field, bf16[10,48,128]{2,1,0:T(8,128)(2,1)} %shard_map.235.lifted, f32[48,128]{1,0:T(8,128)} %get-tuple-element.31.rain, ...), custom_call_target="tpu_custom_call" | custom-call | tf_op jit(solution)/shard_map/pallas_call | solution.py:377
  77.9 14.5 %shard_map.237 = bf16[16,16,128]{2,1,0:T(8,128)(2,1)} custom-call(bf16[8,32,128]{2,1,0:T(8,128)(2,1)} %get-tuple-element.35.dlift, bf16[256,256]{1,0:T(8,128)(2,1)} %constant.28.clone.mid), custom_call_target="tpu_custom_call" | custom-call | tf_op jit(solution)/shard_map/pallas_call | solution.py:377
  92.4 7.8 %shard_map.238.g = bf16[1280,8,128]{2,1,0:T(8,128)(2,1)} custom-call(bf16[256,128]{1,0:T(8,128)(2,1)} %bitcast.15, bf16[256,256]{1,0:T(8,128)(2,1)} %constant.29.clone.group, bf16[512,512]{1,0:T(8,128)(2,1)} %w_out.3, bf16[512,128]{1,0:T(8,128)(2,1)} %w_up.3, bf16[256,512]{1,0:T(8,128)(2,1)} %get-tuple-element.36.tok, ...), custom_call_target="tpu_custom_call" | custom-call | tf_op jit(solution)/shard_map/pallas_call | solution.py:377
  100.2 0.0 copy-start
  100.2 1.7 %copy-done = bf16[1280,8,128]{2,1,0:T(8,128)(2,1)S(1)} copy-done((bf16[1280,8,128]{2,1,0:T(8,128)(2,1)S(1)}, bf16[1280,8,128]{2,1,0:T(8,128)(2,1)}, u32[]{:S(2)}) %copy-start) | copy-done | bytes 2621464
  101.9 55.1 %shard_map.239.g = bf16[1280,8,128]{2,1,0:T(8,128)(2,1)S(1)} custom-call(bf16[1280,8,128]{2,1,0:T(8,128)(2,1)S(1)} %copy-done), custom_call_target="tpu_custom_call" | custom-call | tf_op jit(solution)/shard_map/pallas_call | solution.py:121
  157.0 0.0 copy-start.1
  157.0 1.5 copy-done.1
  158.5 4.2 %shard_map.240 = (f32[512,1536]{1,0:T(8,128)}, f32[512,512]{1,0:T(8,128)}, f32[512,128]{1,0:T(8,128)}, f32[1152,128]{1,0:T(8,128)}, f32[16,128]{1,0:T(8,128)}) custom-call(bf16[1280,8,128]{2,1,0:T(8,128)(2,1)} %copy-done.1), custom_call_target="tpu_custom_call" | custom-call | tf_op jit(solution)/shard_map/pallas_call | solution.py:377
  162.7 1.3 slice_reduce_fusion
  164.6 1.3 slice_bitcast_fusion
Async XLA Ops:
  100.2 1.7 %copy-start = (bf16[1280,8,128]{2,1,0:T(8,128)(2,1)S(1)}, bf16[1280,8,128]{2,1,0:T(8,128)(2,1)}, u32[]{:S(2)}) copy-start(bf16[1280,8,128]{2,1,0:T(8,128)(2,1)} %shard_map.238.g) | copy-start | bytes 7864324
  157.0 1.5 copy-start.1

commit v3 on v0

v3 whole, which is shorter than its diff:
```python
import jax
import jax.numpy as jnp
import numpy as np
from types import SimpleNamespace
from jax import lax
from jax.experimental import pallas as pl
from jax.experimental.pallas import tpu as pltpu
from jax.sharding import PartitionSpec as P

HEAD_DIM = 32
QUANT = 9
MESH = pl.DeviceIdType.MESH
F32, B16 = jnp.float32, jnp.bfloat16
DMA = pltpu.SemaphoreType.DMA
SCALE = HEAD_DIM ** (-0.5)
ROOT_2_PI = 0.7978845608028654
LIMIT = 58 * 1024 * 1024
EARLY, LATE = 512, 768


def onehot(rows, cols, pairs):
    table = np.zeros((rows, cols), np.float32)
    for row, col in pairs:
        table[row, col] = 1.0
    return jnp.asarray(table, B16)


def mid_table():
    return onehot(256, 256, [(p * 16 + r * 2 + m, r * 32 + p * 2 + m)
                             for p in range(16) for r in range(8) for m in range(2)])


def group_table():
    return onehot(256, 256, [(m * 128 + c * 8 + r, c * 16 + r * 2 + m)
                             for m in range(2) for c in range(16) for r in range(8)])


def back_table():
    pairs = []
    for r in range(8):
        for j in range(32):
            pairs.append((r * 48 + j, (1 + j // 2) * 16 + r * 2 + j % 2))
        pairs.append((r * 48 + 32, 17 * 16 + r * 2))
        pairs.append((r * 48 + 35, r * 2 + 1))
    return onehot(384, 288, pairs)


def pick_table(first):
    return onehot(16, 128, [(2 * i + s, 16 * i + first + s) for i in range(8) for s in range(2)])


def spread_table(first):
    return onehot(128, 16, [(16 * i + first + s, 2 * i + s) for i in range(8) for s in range(2)])


def bins_table():
    return onehot(48, 64, [(0, 15)] + [(1 + y, 16 + y) for y in range(32)] + [(33, 48)])


def up_table():
    return onehot(144, 48, [(p, p // 4) for p in range(144)])


def sum_table():
    return onehot(32, 128, [(p // 4, p) for p in range(128)])


def dot(a, b):
    return jnp.dot(a, b, preferred_element_type=F32)


def dot_nt(a, b):
    return lax.dot_general(a, b, (((1,), (1,)), ((), ())), preferred_element_type=F32)


def rcopy(src, dst, send, recv, to):
    return pltpu.make_async_remote_copy(src_ref=src, dst_ref=dst, send_sem=send, recv_sem=recv,
                                        device_id=to, device_id_type=MESH)


def wait_all(copies):
    for c in copies:
        c.wait()


def scatter_out(axis, count, src, got, send, recv, me):
    copies = []
    for k in range(1, count):
        p = (me + k) % count
        c = rcopy(src.at[p], got.at[me], send.at[k - 1], recv.at[k - 1], {axis: p})
        c.start()
        copies.append(c)
    return copies


def spread_out(axis, count, me, src, main, send, recv, send_x, recv_x):
    copies = []
    for k in range(1, count):
        p = (me + k) % count
        c = rcopy(src.at[p], main.at[1 + me], send.at[k - 1], recv.at[k - 1], {axis: p})
        c.start()
        copies.append(c)
    main[1 + me] = src[me]

    def after(t):
        return rcopy(src.at[t - 1], main.at[0], send_x.at[t], recv_x.at[0], {axis: t})

    def before(t):
        return rcopy(src.at[t + 1], main.at[count + 1], send_x.at[t], recv_x.at[1], {axis: t})

    @pl.when(me == count - 1)
    def _():
        for t in range(1, count - 1):
            after(t).start()
        main[0] = src[count - 2]
        main[count + 1] = jnp.zeros(main.shape[1:], B16)

    @pl.when(me == 0)
    def _():
        for t in range(1, count - 1):
            before(t).start()
        main[count + 1] = src[1]
        main[0] = jnp.zeros(main.shape[1:], B16)

    def finish():
        @pl.when(me == count - 1)
        def _():
            for t in range(1, count - 1):
                after(t).wait_send()

        @pl.when(me == 0)
        def _():
            for t in range(1, count - 1):
                before(t).wait_send()

        @pl.when((me > 0) & (me < count - 1))
        def _():
            after(1).wait_recv()
            before(1).wait_recv()

        wait_all(copies)

    return finish


def head_mask(h):
    lane = lax.broadcasted_iota(jnp.int32, (1, 128), 1)
    return jnp.where((lane >> 5) == h, 1.0, 0.0).astype(B16)


def heads_down(tile):
    return jnp.concatenate([tile * head_mask(h) for h in range(4)], axis=0)


def heads_across(tile):
    turned = tile.astype(F32).T
    line = lax.broadcasted_iota(jnp.int32, (128, 1), 0) >> 5
    return jnp.concatenate([jnp.where(line == h, turned, 0.0) for h in range(4)], axis=1).astype(B16)


def side_by_side(stack):
    return jnp.concatenate([stack[h * 128:(h + 1) * 128] for h in range(4)], axis=1)


def put(g, at, value):
    rows, cols = value.shape
    size = rows // 8
    for n in range(cols // 128):
        g[at + n * size:at + (n + 1) * size] = value[:, n * 128:(n + 1) * 128].reshape(size, 8, 128).astype(B16)


def shifted(line):
    return jnp.concatenate([pltpu.roll(line, 1, 0), line, pltpu.roll(line, 143, 0)], axis=1)


def reducer(me, units, g, out, got0, sum0, got1, sum1, got2, sum2, got3, sems):
    core, first, second, deep = me.core, me.first, me.second, me.deep
    u0, u1, u2, u3 = units // 2, units // 8, units // 32, units // 256
    s0, r0, s1, r1, s2, r2, s3, r3, as3, ar3, as2, ar2, as1, ar1, as0, ar0 = sems
    place = core * u0 + first * u1 + second * u2
    held = {}

    def sum_up(terms):
        total = terms[0].astype(F32)
        for term in terms[1:]:
            total = total + term.astype(F32)
        return total

    def near_start():
        held["near"] = []
        for n, k in enumerate((1, 2, 3, 0)):
            p = (second + k) % 4
            c = rcopy(g.at[pl.ds((1 - core) * u0 + p * u1, u1)], got0.at[p], s0.at[n], r0.at[n], me.other)
            c.start()
            held["near"].append(c)

    def first_start():
        held["first"] = []
        for n, k in enumerate((1, 2, 3)):
            p = (first + k) % 4
            held["near"][n].wait_recv()
            sum0[p] = sum_up([g[pl.ds(core * u0 + p * u1, u1)], got0[p]]).astype(B16)
            c = rcopy(sum0.at[p], got1.at[k - 1], s1.at[k - 1], r1.at[k - 1], me.in_first(k))
            c.start()
            held["first"].append(c)
        held["near"][3].wait_recv()

    def second_start():
        wait_all(held["first"])
        sum1[...] = sum_up([g[pl.ds(core * u0 + first * u1, u1)], got0[first], got1[0], got1[1], got1[2]]).astype(B16)
        held["second"] = []
        for k in (1, 2, 3):
            p = (second + k) % 4
            c = rcopy(sum1.at[pl.ds(p * u2, u2)], got2.at[k - 1], s2.at[k - 1], r2.at[k - 1], me.in_second(k))
            c.start()
            held["second"].append(c)
        for c in held["near"]:
            c.wait_send()

    def deep_start():
        wait_all(held["second"])
        sum2[...] = sum_up([sum1[pl.ds(second * u2, u2)], got2[0], got2[1], got2[2]]).astype(B16)
        held["deep"] = []
        for k in range(1, 8):
            p = (deep + k) % 8
            c = rcopy(sum2.at[pl.ds(p * u3, u3)], got3.at[k - 1], s3.at[k - 1], r3.at[k - 1], me.in_deep(k))
            c.start()
            held["deep"].append(c)

    def deep_gather():
        wait_all(held["deep"])
        mine = sum_up([sum2[pl.ds(deep * u3, u3)]] + [got3[k] for k in range(7)])
        out[pl.ds(place + deep * u3, u3)] = mine.astype(B16)
        block = out.at[pl.ds(place + deep * u3, u3)]
        held["deep"] = []
        for k in range(1, 8):
            c = rcopy(block, block, as3.at[k - 1], ar3.at[k - 1], me.in_deep(k))
            c.start()
            held["deep"].append(c)

    def second_gather():
        wait_all(held["deep"])
        block = out.at[pl.ds(place, u2)]
        held["second"] = []
        for k in (1, 2, 3):
            c = rcopy(block, block, as2.at[k - 1], ar2.at[k - 1], me.in_second(k))
            c.start()
            held["second"].append(c)

    def forward(n, p):
        block = out.at[pl.ds(core * u0 + p * u1, u1)]
        c = rcopy(block, block, as0.at[n], ar0.at[n], me.other)
        c.start()
        held["near"].append(c)

    def first_gather():
        wait_all(held["second"])
        block = out.at[pl.ds(core * u0 + first * u1, u1)]
        held["first"], held["near"] = [], []
        for k in (1, 2, 3):
            c = rcopy(block, block, as1.at[k - 1], ar1.at[k - 1], me.in_first(k))
            c.start()
            held["first"].append(c)
        forward(0, first)

    def near_gather():
        for k in (1, 2, 3):
            held["first"][k - 1].wait_recv()
            forward(k, (first + 4 - k) % 4)

    def finish():
        for c in held["first"]:
            c.wait_send()
        wait_all(held["near"])

    return [near_start, first_start, second_start, deep_start, deep_gather, second_gather, first_gather,
            near_gather, finish]


def reducer_scratch(tag, units):
    unit = (8, 128)
    u1, u2, u3 = units // 8, units // 32, units // 256
    shapes = [("g", (units,) + unit), ("got0", (4, u1) + unit), ("sum0", (4, u1) + unit), ("got1", (3, u1) + unit),
              ("sum1", (u1,) + unit), ("got2", (3, u2) + unit), ("sum2", (u2,) + unit), ("got3", (7, u3) + unit)]
    result = [(tag + name, pltpu.VMEM(shape, B16)) for name, shape in shapes]
    for n, count in enumerate((4, 4, 3, 3, 3, 3, 7, 7, 7, 7, 3, 3, 3, 3, 4, 4)):
        result.append((tag + "sem" + str(n), DMA((count,))))
    return result


INPUTS = ("coarse", "fine", "bins", "w_qkv_in", "w_out_in", "w_up", "w_conv_in", "w_head",
          "mid", "group", "ungroup", "back", "pick_lo", "pick_hi", "spread_lo", "spread_hi", "place", "up", "fold", "eye")
IN_HBM = ("coarse", "fine", "w_qkv_in", "w_out_in", "w_conv_in")
OUTPUTS = (("quantiles", (9, 32, 128), F32), ("grad_fine", (32, 128, 128), F32),
           ("early", (EARLY, 8, 128), B16), ("late", (LATE, 8, 128), B16))


def scratch():
    buffers = [
        ("w_qkv", (512, 1536), B16), ("w_out", (512, 512), B16), ("w_conv", (3, 3, 128, 128), B16),
        ("got", (8, 32, 512), B16), ("turned", (16, 16, 512), B16), ("tokens", (16, 16, 512), B16),
        ("field", (40, 144, 128), B16), ("bins16", (32, 128), B16), ("bin_got", (64, 128), B16),
        ("edge_out", (2, 5, 16, 128), B16), ("edge_in", (2, 5, 16, 128), B16), ("bin_out", (2, 48, 128), B16),
        ("bin_in", (2, 48, 128), B16), ("rain", (48, 128), F32), ("edge_bins", (16, 128), F32),
        ("tok", (256, 512), B16), ("qkv", (256, 1536), B16), ("prob", (8, 512, 128), F32), ("mixed", (256, 512), B16),
        ("context", (256, 512), B16), ("raised", (16, 16, 128), B16),
        ("slots", (18, 16, 128), B16), ("lift_turned", (8, 48, 128), B16), ("lifted", (10, 48, 128), B16),
        ("query_turned", (8, 128, 512), B16), ("tok_turned", (512, 256), B16), ("mixed_turned", (512, 256), B16),
        ("context_turned", (512, 256), B16),
        ("hidden", (40, 144, 128), F32), ("slope", (40, 128, 128), F32), ("active", (40, 144, 384), B16),
        ("outer", (36, 144, 128), B16), ("out_grad", (36, 128, 128), F32), ("out_wide", (36, 144, 384), B16),
        ("out_turned", (36, 128, 128), B16), ("kernel_sum", (3, 128, 384), F32), ("loss_sum", (16, 128), F32),
        ("head_sum", (16, 128), F32), ("dlift", (8, 32, 128), B16),
        ("fold_got", (8, 32, 128), B16), ("fold_turned", (16, 16, 128), B16), ("folded", (16, 16, 128), B16),
        ("dquery", (256, 512), B16), ("dkey", (512, 256), B16), ("dvalue", (512, 256), B16),
    ]
    sems = [("s_l", 6), ("s_tr", 7), ("r_tr", 7), ("s_tc", 15), ("r_tc", 15), ("s_h", 4), ("r_h", 4), ("s_e", 4), ("r_e", 4),
            ("s_lc", 15), ("r_lc", 15), ("s_lx", 16), ("r_lx", 2), ("s_lr", 7), ("r_lr", 7), ("s_ly", 8), ("r_ly", 2),
            ("s_fr", 7), ("r_fr", 7), ("s_fc", 15), ("r_fc", 15)]
    return ([(name, pltpu.VMEM(shape, dtype)) for name, shape, dtype in buffers]
            + [(name, DMA((count,))) for name, count in sems]
            + reducer_scratch("a_", EARLY) + reducer_scratch("b_", LATE))


def halo_rows(v, row):
    sends = [
        ((v.fine.at[pl.ds(30, 2)], v.field.at[pl.ds(2, 2), pl.ds(0, 128)], v.s_h.at[0], v.r_h.at[0]),
         (v.bins16.at[pl.ds(16, 16)], v.bin_got.at[pl.ds(0, 16)], v.s_h.at[1], v.r_h.at[1])),
        ((v.fine.at[pl.ds(0, 2)], v.field.at[pl.ds(36, 2), pl.ds(0, 128)], v.s_h.at[2], v.r_h.at[2]),
         (v.bins16.at[pl.ds(0, 16)], v.bin_got.at[pl.ds(48, 16)], v.s_h.at[3], v.r_h.at[3])),
    ]

    def start():
        @pl.when(row < 7)
        def _():
            for args in sends[0]:
                rcopy(*args, {"rows": row + 1}).start()

        @pl.when(row > 0)
        def _():
            for args in sends[1]:
                rcopy(*args, {"rows": row - 1}).start()

    def finish():
        @pl.when(row < 7)
        def _():
            for args in sends[0]:
                rcopy(*args, {"rows": row + 1}).wait_send()
            for args in sends[1]:
                rcopy(*args, {"rows": row + 1}).wait_recv()

        @pl.when(row > 0)
        def _():
            for args in sends[1]:
                rcopy(*args, {"rows": row - 1}).wait_send()
            for args in sends[0]:
                rcopy(*args, {"rows": row - 1}).wait_recv()

    return start, finish


def halo_cols(v, col):
    sends = [((v.edge_out.at[n], v.edge_in.at[n], v.s_e.at[2 * n], v.r_e.at[2 * n]),
              (v.bin_out.at[n], v.bin_in.at[n], v.s_e.at[2 * n + 1], v.r_e.at[2 * n + 1])) for n in range(2)]

    def start():
        @pl.when(col < 15)
        def _():
            for args in sends[0]:
                rcopy(*args, {"cols": col + 1}).start()

        @pl.when(col > 0)
        def _():
            for args in sends[1]:
                rcopy(*args, {"cols": col - 1}).start()

    def finish():
        @pl.when(col < 15)
        def _():
            for args in sends[0]:
                rcopy(*args, {"cols": col + 1}).wait_send()
            for args in sends[1]:
                rcopy(*args, {"cols": col + 1}).wait_recv()

        @pl.when(col > 0)
        def _():
            for args in sends[1]:
                rcopy(*args, {"cols": col - 1}).wait_send()
            for args in sends[0]:
                rcopy(*args, {"cols": col - 1}).wait_recv()

    return start, finish


def exchange_tokens(v, row, col, loads):
    sends = scatter_out("rows", 8, v.coarse, v.got, v.s_tr, v.r_tr, row)
    own = pltpu.make_async_copy(v.coarse.at[row], v.got.at[row], v.s_l.at[0])
    own.start()
    v.bins16[...] = v.bins[...].astype(F32).astype(B16)
    rows_start, rows_finish = halo_rows(v, row)
    rows_start()
    for c in loads:
        c.start()

    @pl.when(row == 0)
    def _():
        v.field[pl.ds(2, 2), :128] = jnp.zeros((2, 128, 128), B16)
        v.bin_got[pl.ds(0, 16)] = jnp.zeros((16, 128), B16)

    @pl.when(row == 7)
    def _():
        v.field[pl.ds(36, 2), :128] = jnp.zeros((2, 128, 128), B16)
        v.bin_got[pl.ds(48, 16)] = jnp.zeros((16, 128), B16)

    v.field[pl.ds(0, 2), :128] = jnp.zeros((2, 128, 128), B16)
    v.field[pl.ds(38, 2), :128] = jnp.zeros((2, 128, 128), B16)
    v.bin_got[pl.ds(16, 32)] = v.bins16[...]

    own.wait()
    wait_all(sends)
    v.turned[...] = dot(v.mid[...], v.got[...].reshape(256, 512)).astype(B16).reshape(16, 16, 512)
    sends = scatter_out("cols", 16, v.turned, v.tokens, v.s_tc, v.r_tc, col)
    v.tokens[col] = v.turned[col]

    loads[0].wait()
    rows_finish()
    rows = dot(v.place[...], v.bin_got[...])
    v.rain[...] = rows
    v.bin_out[0] = jnp.broadcast_to(rows[:, 127:128], (48, 128)).astype(B16)
    v.bin_out[1] = jnp.broadcast_to(rows[:, 0:1], (48, 128)).astype(B16)
    for q in range(5):
        v.edge_out[0, q] = dot(v.pick_hi[...], v.field[8 * q:8 * q + 8, 112:128].reshape(128, 128)).astype(B16)
        v.edge_out[1, q] = dot(v.pick_lo[...], v.field[8 * q:8 * q + 8, 0:16].reshape(128, 128)).astype(B16)
    cols_start, cols_finish = halo_cols(v, col)
    cols_start()

    @pl.when(col == 0)
    def _():
        v.edge_in[0] = jnp.zeros((5, 16, 128), B16)
        v.bin_in[0] = jnp.zeros((48, 128), B16)

    @pl.when(col == 15)
    def _():
        v.edge_in[1] = jnp.zeros((5, 16, 128), B16)
        v.bin_in[1] = jnp.zeros((48, 128), B16)

    wait_all(sends)
    return cols_finish


def attend(v):
    v.tok[...] = dot(v.group[...], v.tokens[...].reshape(256, 512)).astype(B16)
    for n in range(3):
        v.qkv[:, n * 512:(n + 1) * 512] = dot(v.tok[...], v.w_qkv[:, n * 512:(n + 1) * 512]).astype(B16)
    for g in range(2):
        for t in range(4):
            rows, at = slice(g * 128, g * 128 + 128), t * 128
            query = v.qkv[rows, at:at + 128]
            keyed = v.qkv[rows, 512 + at:512 + at + 128]
            valued = v.qkv[rows, 1024 + at:1024 + at + 128]
            scores = dot_nt(heads_down(query), keyed) * SCALE
            peak = jnp.max(scores, axis=-1, keepdims=True)
            powers = jnp.exp(scores - peak)
            share = powers / jnp.sum(powers, axis=-1, keepdims=True)
            v.prob[g * 4 + t] = share
            v.mixed[rows, at:at + 128] = dot(side_by_side(share.astype(B16)), heads_down(valued)).astype(B16)
    attended = dot(v.mixed[...], v.w_out[...]).astype(B16)
    v.context[...] = (v.tok[...].astype(F32) + attended.astype(F32)).astype(B16)
    lifted = dot(v.context[...], v.w_up[...]).astype(B16)
    v.raised[...] = dot(v.ungroup[...], lifted).astype(B16).reshape(16, 16, 128)


def edge_targets(v):
    lane = lax.broadcasted_iota(jnp.int32, (48, 128), 1)
    line = lax.broadcasted_iota(jnp.int32, (48, 128), 0)
    low, high = v.bin_in[0].astype(F32), v.bin_in[1].astype(F32)
    picked = jnp.where((lane & 15) == 0, high, jnp.where((lane & 15) == 15, low, 0.0))
    for b in range(9):
        here = line == 4 * b + (lane >> 4)
        v.edge_bins[b:b + 1] = jnp.sum(jnp.where(here, picked, 0.0), axis=0, keepdims=True)


def convolve(v, row, col):
    head_t = dot_nt(v.eye[...], v.w_head[...]).astype(B16)
    head = dot_nt(v.w_head[...], v.eye[...]).astype(B16)
    place = lax.broadcasted_iota(jnp.int32, (144, 1), 0)
    right = jnp.where(col < 15, 130, 128)
    left = jnp.where(col > 0, 142, 144)
    inside = (place < right) | (place >= left)
    level = (lax.broadcasted_iota(jnp.int32, (16, 1), 0) + 1).astype(F32) / 10.0
    quant = lax.broadcasted_iota(jnp.int32, (16, 1), 0) < QUANT
    v.loss_sum[...] = jnp.zeros((16, 128), F32)
    v.head_sum[...] = jnp.zeros((16, 128), F32)

    def start(i):
        raised = dot(v.up[...], v.lifted[i])
        for s in range(4):
            y = 4 * i + s - 4
            x = v.field[4 * i + s].astype(F32) + raised
            square = x * x
            bend = jnp.tanh(ROOT_2_PI * x * (1.0 + 0.044715 * square))
            half = 0.5 * (1.0 + bend)
            seen = (row * 32 + y >= 0) & (row * 32 + y < 256)
            act = jnp.where(inside & seen, x * half, 0.0)
            v.hidden[4 * i + s] = x
            v.active[4 * i + s] = shifted(act).astype(B16)
            v.slope[4 * i + s] = half[:128] + (0.5 * ROOT_2_PI) * x[:128] * (1.0 - bend[:128] * bend[:128]) * (
                1.0 + (3 * 0.044715) * square[:128])

    def forward(i):
        total = v.hidden[pl.ds(4 * i + 3, 4)].reshape(576, 128)
        for a in range(3):
            window = v.active[pl.ds(4 * i + 2 + a, 4)].reshape(576, 384)
            total = total + dot(window, v.w_conv[a].reshape(384, 128))
        v.outer[pl.ds(4 * i, 4)] = total.astype(B16).reshape(4, 144, 128)

    def turn(i):
        own = v.outer[pl.ds(4 * i, 4), :128].reshape(512, 128)
        edge = v.outer[pl.ds(4 * i, 4), 128:144].reshape(64, 128)
        pixels = jnp.concatenate([own, edge, jnp.zeros((64, 128), B16)], axis=0)
        predicted = dot_nt(head_t, pixels)
        lines = [v.rain[pl.ds(4 * i + s, 1), :] for s in range(4)] + [v.edge_bins[pl.ds(i, 1), :]]
        target = jnp.concatenate(lines, axis=1) * (1.0 / 16.0) - 1.0
        lane = lax.broadcasted_iota(jnp.int32, (1, 640), 1)
        spot = lane - 512
        inner = lane < 512
        y = 4 * i - 1 + jnp.where(inner, lane >> 7, spot >> 4)
        side = (((spot & 15) == 0) & (col < 15)) | (((spot & 15) == 15) & (col > 0))
        seen = (row * 32 + y >= 0) & (row * 32 + y < 256) & (y < 33) & (inner | (side & (spot < 64)))
        mine = inner & (y >= 0) & (y < 32)
        error = target - predicted
        weight = jnp.where(error < 0.0, 1.0 - level, level)
        down = jnp.where(seen & quant, -weight * jnp.clip(error, -1.0, 1.0) * (1.0 / 1024.0), 0.0)
        size = jnp.abs(error)
        loss = weight * jnp.where(size <= 1.0, 0.5 * error * error, size - 0.5)
        loss = jnp.where(mine & quant, loss, 0.0)
        v.loss_sum[...] += loss[:, :128] + loss[:, 128:256] + loss[:, 256:384] + loss[:, 384:512]
        down_b = down.astype(B16)
        v.head_sum[...] += dot(jnp.where(mine, down, 0.0).astype(B16)[:, :512], own)
        across = dot(head, down_b[:, :512]).astype(B16)
        along = dot(down.T.astype(B16), head_t)
        for s in range(4):
            row_y = 4 * i + s - 1
            value = predicted[:, s * 128:(s + 1) * 128]

            def keep():
                for q in range(QUANT):
                    v.quantiles[q, pl.ds(row_y, 1), :] = value[q:q + 1]

            if isinstance(i, int):
                if 0 <= row_y < 32:
                    keep()
            else:
                keep()
            v.out_turned[4 * i + s] = across[:, s * 128:(s + 1) * 128]
            mid_part = along[s * 128:(s + 1) * 128]
            v.out_grad[4 * i + s] = mid_part
            full = jnp.concatenate([mid_part, along[512 + s * 16:528 + s * 16]], axis=0)
            v.out_wide[4 * i + s] = shifted(full).astype(B16)

    def back(i):
        total = None
        for a in range(3):
            window = v.out_wide[pl.ds(4 * i + a, 4), :128].reshape(512, 384)
            turned = jnp.concatenate([v.w_conv[2 - a, 2 - b] for b in range(3)], axis=1)
            part = dot_nt(window, turned)
            total = part if total is None else total + part
        dhidden = v.out_grad[pl.ds(4 * i + 1, 4)] + v.slope[pl.ds(4 * i + 4, 4)] * total.reshape(4, 128, 128)
        v.grad_fine[pl.ds(4 * i, 4)] = dhidden * 1024.0
        summed = dhidden[0] + dhidden[1] + dhidden[2] + dhidden[3]
        high = summed.astype(B16)
        low = (summed - high.astype(F32)).astype(B16)
        v.dlift[i] = (dot(v.fold[...], high) + dot(v.fold[...], low)).astype(B16)

    def step(t):
        known = isinstance(t, int)
        if not known or 0 <= t - 5 <= 7:
            back(t - 5)
        if not known or 0 <= t - 3 <= 8:
            turn(t - 3)
        if not known or 0 <= t - 2 <= 8:
            forward(t - 2)
        if not known or t <= 9:
            start(t)

    for t in range(5):
        step(t)

    def loop(t, carry):
        step(t)
        return carry

    lax.fori_loop(5, 10, loop, 0)
    for t in range(10, 13):
        step(t)


def kernel_terms(v, low, high):
    def one(i, carry):
        across = jnp.concatenate([v.out_turned[4 * i + 1 + s] for s in range(4)], axis=1)
        for a in range(3):
            window = v.active[pl.ds(4 * i + 3 + a, 4), :128].reshape(512, 384)
            v.kernel_sum[a] += dot(across, window)
        return carry

    lax.fori_loop(low, high, one, 0)


def local_units(v):
    for a in range(3):
        for b in range(3):
            at = 320 + a * 48 + b * 16
            v.a_g[at:at + 16] = v.kernel_sum[a, :, b * 128:(b + 1) * 128].T.reshape(16, 8, 128).astype(B16)
    spot = lax.broadcasted_iota(jnp.int32, (16, 1), 0)
    total = jnp.sum(v.loss_sum[...], axis=0, keepdims=True)
    tail = jnp.where(spot < QUANT, v.head_sum[...], jnp.where(spot == QUANT, total, 0.0))
    v.a_g[464:466] = tail.reshape(2, 8, 128).astype(B16)
    v.a_g[466:EARLY] = jnp.zeros((EARLY - 466, 8, 128), B16)


def attend_back(v, mix_grad, s):
    for t in range(4):
        rows, at = slice(s * 128, s * 128 + 128), t * 128
        keyed = v.qkv[rows, 512 + at:512 + at + 128]
        valued = v.qkv[rows, 1024 + at:1024 + at + 128]
        mine = mix_grad[rows, at:at + 128]
        dprob = dot_nt(heads_down(mine), valued)
        share = v.prob[s * 4 + t]
        inner = jnp.sum(share * dprob, axis=-1, keepdims=True)
        dscore = (share * (dprob - inner) * SCALE).astype(B16)
        v.dquery[rows, at:at + 128] = dot(side_by_side(dscore), heads_down(keyed)).astype(B16)
        v.dkey[at:at + 128, rows] = dot(v.query_turned[s * 4 + t], dscore).astype(B16)
        v.dvalue[at:at + 128, rows] = dot(heads_across(mine), share.astype(B16)).astype(B16)


def whole_kernel(names, *refs):
    v = SimpleNamespace(**dict(zip(names, refs)))
    row, col, batch = lax.axis_index("rows"), lax.axis_index("cols"), lax.axis_index("batch")
    core, deep = row % 2, (row // 2) * 2 + batch
    x, y = col // 4, col % 4
    me = SimpleNamespace(
        core=core, deep=deep, other={"rows": row + 1 - 2 * core},
        first=x * (1 - core) + y * core, second=y * (1 - core) + x * core,
    )

    def in_first(k):
        p = (me.first + k) % 4
        return {"cols": (p * 4 + y) * (1 - core) + (x * 4 + p) * core}

    def in_second(k):
        p = (me.second + k) % 4
        return {"cols": (x * 4 + p) * (1 - core) + (p * 4 + y) * core}

    def in_deep(k):
        p = (deep + k) % 8
        return {"rows": (p // 2) * 2 + core, "batch": p % 2}

    me.in_first, me.in_second, me.in_deep = in_first, in_second, in_deep

    peers = [{"rows": (row + k) % 8} for k in range(1, 8)] + [{"cols": (col + k) % 16} for k in range(1, 16)]
    peers += [{"rows": (row + 2 * k) % 8, "batch": 1 - batch} for k in range(4)]
    barrier = pltpu.get_barrier_semaphore()
    for peer in peers:
        pl.semaphore_signal(barrier, inc=1, device_id=peer, device_id_type=MESH)
    pl.semaphore_wait(barrier, len(peers))

    loads = [pltpu.make_async_copy(v.fine, v.field.at[pl.ds(4, 32), pl.ds(0, 128)], v.s_l.at[1]),
             pltpu.make_async_copy(v.w_qkv_in, v.w_qkv, v.s_l.at[2]),
             pltpu.make_async_copy(v.w_out_in, v.w_out, v.s_l.at[3]),
             pltpu.make_async_copy(v.w_conv_in, v.w_conv, v.s_l.at[4])]
    cols_finish = exchange_tokens(v, row, col, loads)
    loads[1].wait()
    loads[2].wait()
    attend(v)

    finish = spread_out("cols", 16, col, v.raised, v.slots, v.s_lc, v.r_lc, v.s_lx, v.r_lx)
    cols_finish()
    for q in range(5):
        edge = dot(v.spread_hi[...], v.edge_in[0, q]) + dot(v.spread_lo[...], v.edge_in[1, q])
        v.field[8 * q:8 * q + 8, 128:144] = edge.astype(B16).reshape(8, 16, 128)
    edge_targets(v)
    for s in range(2):
        for t in range(4):
            v.query_turned[s * 4 + t] = heads_across(v.qkv[s * 128:s * 128 + 128, t * 128:t * 128 + 128])
    finish()
    v.lift_turned[...] = dot(v.back[...], v.slots[...].reshape(288, 128)).astype(B16).reshape(8, 48, 128)
    finish = spread_out("rows", 8, row, v.lift_turned, v.lifted, v.s_lr, v.r_lr, v.s_ly, v.r_ly)
    v.tok_turned[...] = v.tok[...].astype(F32).T.astype(B16)
    v.mixed_turned[...] = v.mixed[...].astype(F32).T.astype(B16)
    v.context_turned[...] = v.context[...].astype(F32).T.astype(B16)
    v.kernel_sum[...] = jnp.zeros((3, 128, 384), F32)
    loads[3].wait()
    finish()

    convolve(v, row, col)

    sends = scatter_out("rows", 8, v.dlift, v.fold_got, v.s_fr, v.r_fr, row)
    v.fold_got[row] = v.dlift[row]
    kernel_terms(v, 0, 4)
    wait_all(sends)
    v.fold_turned[...] = dot(v.mid[...], v.fold_got[...].reshape(256, 128)).astype(B16).reshape(16, 16, 128)
    sends = scatter_out("cols", 16, v.fold_turned, v.folded, v.s_fc, v.r_fc, col)
    v.folded[col] = v.fold_turned[col]
    kernel_terms(v, 4, 8)
    local_units(v)
    wait_all(sends)

    early = reducer(me, EARLY, v.a_g, v.early, v.a_got0, v.a_sum0, v.a_got1, v.a_sum1, v.a_got2, v.a_sum2, v.a_got3,
                    [getattr(v, "a_sem" + str(n)) for n in range(16)])
    late = reducer(me, LATE, v.b_g, v.late, v.b_got0, v.b_sum0, v.b_got1, v.b_sum1, v.b_got2, v.b_sum2, v.b_got3,
                   [getattr(v, "b_sem" + str(n)) for n in range(16)])
    lift = dot(v.group[...], v.folded[...].reshape(256, 128)).astype(B16)
    dcontext = dot_nt(lift, v.w_up[...]).astype(B16)
    put(v.a_g, 0, dot(v.mixed_turned[...], dcontext))
    put(v.a_g, 256, dot(v.context_turned[...], lift))
    early[0]()
    mix_grad = dot_nt(dcontext, v.w_out[...]).astype(B16)
    attend_back(v, mix_grad, 0)
    early[1]()
    attend_back(v, mix_grad, 1)
    early[2]()
    put(v.b_g, 0, dot(v.tok_turned[...], v.dquery[...]))
    put(v.b_g, 256, dot_nt(v.tok_turned[...], v.dkey[...]))
    put(v.b_g, 512, dot_nt(v.tok_turned[...], v.dvalue[...]))
    late[0]()
    early[3]()
    late[1]()
    early[4]()
    late[2]()
    early[5]()
    late[3]()
    early[6]()
    late[4]()
    early[7]()
    late[5]()
    early[8]()
    for step in late[6:]:
        step()


def unpack_kernel(early, late, grad_qkv, grad_out, grad_up, grad_conv, grad_head, loss):
    for n in range(12):
        grad_qkv[:, n * 128:(n + 1) * 128] = late[n * 64:(n + 1) * 64].astype(F32).reshape(512, 128)
    for n in range(4):
        grad_out[:, n * 128:(n + 1) * 128] = early[n * 64:(n + 1) * 64].astype(F32).reshape(512, 128)
    grad_up[...] = early[256:320].astype(F32).reshape(512, 128)
    grad_conv[...] = early[320:464].astype(F32).reshape(1152, 128)
    tail = early[464:466].astype(F32).reshape(16, 128)
    grad_head[...] = tail.T[:, :QUANT]
    loss[...] = jnp.sum(tail[QUANT:QUANT + 1], axis=1, keepdims=True) * (1.0 / (1048576.0 * QUANT))


def body(fine_input, coarse, rain_bins, w_qkv, w_out, w_up, w_conv, w_head):
    group = group_table()
    eye = onehot(16, QUANT, [(q, q) for q in range(QUANT)])
    args = [coarse[0], fine_input[0], rain_bins[0], w_qkv, w_out, w_up, w_conv, w_head,
            mid_table(), group, group.T, back_table(), pick_table(0), pick_table(14), spread_table(0), spread_table(14),
            bins_table(), up_table(), sum_table(), eye]
    spaces = scratch()
    names = INPUTS + tuple(name for name, _, _ in OUTPUTS) + tuple(name for name, _ in spaces)
    vmem = pl.BlockSpec(memory_space=pltpu.VMEM)

    def kernel(*refs):
        whole_kernel(names, *refs)

    quantiles, grad_fine, early, late = pl.pallas_call(
        kernel,
        out_shape=[jax.ShapeDtypeStruct(shape, dtype) for _, shape, dtype in OUTPUTS],
        in_specs=[pl.BlockSpec(memory_space=pl.ANY) if name in IN_HBM else vmem for name in INPUTS],
        out_specs=[vmem] * len(OUTPUTS),
        scratch_shapes=[space for _, space in spaces],
        compiler_params=pltpu.CompilerParams(vmem_limit_bytes=LIMIT, collective_id=1, has_side_effects=True),
    )(*args)
    grad_qkv, grad_out, grad_up, grad_conv, grad_head, loss = pl.pallas_call(
        unpack_kernel,
        out_shape=[jax.ShapeDtypeStruct(shape, F32)
                   for shape in ((512, 1536), (512, 512), (512, 128), (1152, 128), (128, QUANT), (1, 1))],
        in_specs=[vmem] * 2,
        out_specs=[vmem] * 6,
        compiler_params=pltpu.CompilerParams(vmem_limit_bytes=LIMIT),
    )(early, late)
    return (quantiles[None], loss.reshape(()), grad_qkv, grad_out, grad_up, grad_conv.reshape(3, 3, 128, 128),
            grad_head, grad_fine[None])


def solution(mesh):
    placed = (
        P("batch", "rows", "cols", None),
        P("batch", "rows", "cols", None),
        P("batch", "rows", "cols"),
        P(),
        P(),
        P(),
        P(),
        P(),
    )
    return jax.shard_map(
        body,
        mesh=mesh,
        in_specs=placed,
        out_specs=(
            P("batch", None, "rows", "cols"),
            P(),
            P(),
            P(),
            P(),
            P(),
            P(),
            P("batch", "rows", "cols", None),
        ),
        check_vma=False,
    )
```

time: 458 us -> 131 us (0.29)
  waiting for transfers between devices: 222 us -> 0 us
  Pallas kernels: 0 us -> 126 us
  blocking collectives: 106 us -> 0 us
  starting transfers between devices: 45.6 us -> 0 us
  matrix products: 44.5 us -> 0 us
  between operations: 16.4 us -> 0.66 us
  local copies, waits for them, and re-layouts: 14.9 us -> 4.91 us
  other arithmetic: 6.44 us -> 0 us
    psum x1 -> x0, waiting for transfers between devices: 188 us -> none  [body(): lax.psum((grad_qkv, grad_out, grad_up, grad_conv, grad_head, loss_part),...]
    pallas_call x0 -> x2, Pallas kernels: none -> 126 us  [the longest x1 121 us: body(): pl.pallas_call(kernel, out_shape=[jax.ShapeDtypeStruct(shape, dtype) for...]
    psum x1 -> x0, blocking collectives: 73.5 us -> none  [body(): lax.psum((grad_qkv, grad_out, grad_up, grad_conv, grad_head, loss_part),...]
    dot_general x43 -> x0, matrix products: 43.6 us -> none  [the longest x9 9.96 us: body(): jnp.einsum('bhwc,bhwk->ck', window, douter_b, preferred_element_type=jnp....]
    all_to_all x1 -> x0, blocking collectives: 32.1 us -> none  [regroup(): lax.all_to_all(block, ('rows', 'cols'), split_axis=0, concat_axis=0, tile...]
    all_to_all x2 -> x0, waiting for transfers between devices: 28.4 us -> none  [regroup(): lax.all_to_all(block, ('rows', 'cols'), split_axis=0, concat_axis=0, tile...]
    all_to_all x2 -> x0, starting transfers between devices: 24.4 us -> none  [regroup(): lax.all_to_all(block, ('rows', 'cols'), split_axis=0, concat_axis=0, tile...]
    ppermute x8 -> x0, starting transfers between devices: 21.2 us -> none  [the longest x4 14 us: with_halo(): lax.ppermute(lax.slice_in_dim(block, block.shape[dim] - width, None, axis...]
  transfers between devices with their start and end apart: 11 -> 0, of which waited for: 5 -> 0; matrix products, arithmetic and copies ran while one was open for 2% -> 0% of each run, Pallas kernels for 0% -> 0%
where the time goes in v3:
time: 131 us
  Pallas kernels  126 us (96%)
  local copies, waits for them, and re-layouts  4.91 us (4%)
    pallas_call x1, Pallas kernels, body(): pl.pallas_call(kernel, out_shape=[jax.ShapeDtypeStruct(shape, dtype) for...  121 us
    unnamed x8, local copies, waits for them, and re-layouts  4.91 us
    pallas_call x1, Pallas kernels, body(): pl.pallas_call(unpack_kernel, out_shape=[jax.ShapeDtypeStruct(shape, F32)...  4.3 us

profile of v3, /device:TPU:1, one launch (start us, length us, event | category | flops | bytes accessed | tf_op | source)
XLA Modules:
  0.0 131.2 jit_solution(11623696146737726257)
XLA Ops:
  0.6 1.4 %copy.27.refs_7_ = bf16[128,9]{1,0:T(8,128)(2,1)} copy(bf16[128,9]{0,1:T(8,128)(2,1)} %param.26) | data formatting | bytes 4608 | tf_op args[7]
  2.0 121.3 %shard_map.242 = (f32[9,32,128]{2,1,0:T(8,128)}, f32[32,128,128]{2,1,0:T(8,128)}, bf16[512,8,128]{2,1,0:T(8,128)(2,1)}, bf16[768,8,128]{2,1,0:T(8,128)(2,1)}) custom-call(bf16[8,32,512]{2,1,0:T(8,128)(2,1)} %bitcast.9, bf16[32,128,128]{2,1,0:T(8,128)(2,1)} %bitcast.8, s32[32,128]{1,0:T(8,128)} %bitcast.11, bf16[512,1536]{1,0:T(8,128)(2,1)} %refs_3_.1, ...), custom_call_target="tpu_custom_call" | custom-call | tf_op jit(solution)/shard_map/pallas_call | solution.py:766
  123.4 0.0 copy-start.1
  123.4 0.0 copy-start
  123.4 4.3 %shard_map.243 = (f32[512,1536]{1,0:T(8,128)}, f32[512,512]{1,0:T(8,128)}, f32[512,128]{1,0:T(8,128)}, f32[1152,128]{1,0:T(8,128)}, f32[128,9]{1,0:T(8,128)}, /*index=5*/f32[1,1]{1,0:T(1,128)}) custom-call(bf16[512,8,128]{2,1,0:T(8,128)(2,1)} %get-tuple-element.19.early, bf16[768,8,128]{2,1,0:T(8,128)(2,1)} %get-tuple-element.20.late), custom_call_target="tpu_custom_call" | custom-call | tf_op jit(solution)/shard_map/pallas_call | solution.py:774
  127.7 1.5 %copy.28 = f32[128,9]{0,1:T(8,128)} copy(f32[128,9]{1,0:T(8,128)} %get-tuple-element.34) | data formatting | bytes 9216
  129.2 0.0 copy-done.1
  129.2 0.7 copy.31
  129.9 0.0 copy-done
  129.9 1.3 %copy.32 = f32[1,32,128,128]{3,2,1,0:T(8,128)} copy(f32[1,32,128,128]{3,2,1,0:T(8,128)S(1)} %bitcast.7) | data formatting | bytes 4194304
Async XLA Ops:
  123.4 5.8 %copy-start.1 = (f32[9,32,128]{2,1,0:T(8,128)S(1)}, f32[9,32,128]{2,1,0:T(8,128)}, u32[]{:S(2)}) copy-start(f32[9,32,128]{2,1,0:T(8,128)} %get-tuple-element.18) | copy-start | bytes 442372
  123.4 6.5 %copy-start = (f32[32,128,128]{2,1,0:T(8,128)S(1)}, f32[32,128,128]{2,1,0:T(8,128)}, u32[]{:S(2)}) copy-start(f32[32,128,128]{2,1,0:T(8,128)} %get-tuple-element.27) | copy-start | bytes 6291460

commit v4 on v3

--- a/solution.py
+++ b/solution.py
@@ -15,7 +15,7 @@
 SCALE = HEAD_DIM ** (-0.5)
 ROOT_2_PI = 0.7978845608028654
 LIMIT = 58 * 1024 * 1024
-EARLY, LATE = 512, 768
+EARLY, LATE = 256, 768
 
 
 def onehot(rows, cols, pairs):
@@ -288,10 +288,10 @@
     return result
 
 
-INPUTS = ("coarse", "fine", "bins", "w_qkv_in", "w_out_in", "w_up", "w_conv_in", "w_head",
+INPUTS = ("coarse", "fine", "bins", "w_qkv_in", "w_out_in", "w_up", "w_conv_in", "w_head_t",
           "mid", "group", "ungroup", "back", "pick_lo", "pick_hi", "spread_lo", "spread_hi", "place", "up", "fold", "eye")
 IN_HBM = ("coarse", "fine", "w_qkv_in", "w_out_in", "w_conv_in")
-OUTPUTS = (("quantiles", (9, 32, 128), F32), ("grad_fine", (32, 128, 128), F32),
+OUTPUTS = (("quantiles_out", (9, 32, 128), F32), ("grad_fine_out", (32, 128, 128), F32),
            ("early", (EARLY, 8, 128), B16), ("late", (LATE, 8, 128), B16))
 
 
@@ -305,16 +305,16 @@
         ("tok", (256, 512), B16), ("qkv", (256, 1536), B16), ("prob", (8, 512, 128), F32), ("mixed", (256, 512), B16),
         ("context", (256, 512), B16), ("raised", (16, 16, 128), B16),
         ("slots", (18, 16, 128), B16), ("lift_turned", (8, 48, 128), B16), ("lifted", (10, 48, 128), B16),
-        ("query_turned", (8, 128, 512), B16), ("tok_turned", (512, 256), B16), ("mixed_turned", (512, 256), B16),
-        ("context_turned", (512, 256), B16),
+        ("query_turned", (8, 128, 512), B16), ("tok_turned", (512, 256), B16),
         ("hidden", (40, 144, 128), F32), ("slope", (40, 128, 128), F32), ("active", (40, 144, 384), B16),
-        ("outer", (36, 144, 128), B16), ("out_grad", (36, 128, 128), F32), ("out_wide", (36, 144, 384), B16),
-        ("out_turned", (36, 128, 128), B16), ("kernel_sum", (3, 128, 384), F32), ("loss_sum", (16, 128), F32),
-        ("head_sum", (16, 128), F32), ("dlift", (8, 32, 128), B16),
+        ("outer", (36, 144, 128), B16), ("taps", (36, 48, 128), B16), ("taps_turned", (36, 128, 48), B16),
+        ("back_low", (48, 128), B16), ("back_mid", (48, 256), B16), ("back_high", (48, 128), B16),
+        ("tap_sum", (144, 128), F32), ("loss_sum", (16, 128), F32), ("head_sum", (16, 128), F32),
+        ("dlift", (8, 32, 128), B16), ("grad_fine", (32, 128, 128), F32), ("quantiles", (9, 32, 128), F32),
         ("fold_got", (8, 32, 128), B16), ("fold_turned", (16, 16, 128), B16), ("folded", (16, 16, 128), B16),
         ("dquery", (256, 512), B16), ("dkey", (512, 256), B16), ("dvalue", (512, 256), B16),
     ]
-    sems = [("s_l", 6), ("s_tr", 7), ("r_tr", 7), ("s_tc", 15), ("r_tc", 15), ("s_h", 4), ("r_h", 4), ("s_e", 4), ("r_e", 4),
+    sems = [("s_l", 7), ("s_tr", 7), ("r_tr", 7), ("s_tc", 15), ("r_tc", 15), ("s_h", 4), ("r_h", 4), ("s_e", 4), ("r_e", 4),
             ("s_lc", 15), ("r_lc", 15), ("s_lx", 16), ("r_lx", 2), ("s_lr", 7), ("r_lr", 7), ("s_ly", 8), ("r_ly", 2),
             ("s_fr", 7), ("r_fr", 7), ("s_fc", 15), ("r_fc", 15)]
     return ([(name, pltpu.VMEM(shape, dtype)) for name, shape, dtype in buffers]
@@ -396,11 +396,8 @@
     sends = scatter_out("rows", 8, v.coarse, v.got, v.s_tr, v.r_tr, row)
     own = pltpu.make_async_copy(v.coarse.at[row], v.got.at[row], v.s_l.at[0])
     own.start()
-    v.bins16[...] = v.bins[...].astype(F32).astype(B16)
     rows_start, rows_finish = halo_rows(v, row)
     rows_start()
-    for c in loads:
-        c.start()
 
     @pl.when(row == 0)
     def _():
@@ -481,8 +478,7 @@
 
 
 def convolve(v, row, col):
-    head_t = dot_nt(v.eye[...], v.w_head[...]).astype(B16)
-    head = dot_nt(v.w_head[...], v.eye[...]).astype(B16)
+    head_t = dot(v.eye[...], v.w_head_t[...]).astype(B16)
     place = lax.broadcasted_iota(jnp.int32, (144, 1), 0)
     right = jnp.where(col < 15, 130, 128)
     left = jnp.where(col > 0, 142, 144)
@@ -491,6 +487,7 @@
     quant = lax.broadcasted_iota(jnp.int32, (16, 1), 0) < QUANT
     v.loss_sum[...] = jnp.zeros((16, 128), F32)
     v.head_sum[...] = jnp.zeros((16, 128), F32)
+    v.tap_sum[...] = jnp.zeros((144, 128), F32)
 
     def start(i):
         raised = dot(v.up[...], v.lifted[i])
@@ -509,9 +506,8 @@
 
     def forward(i):
         total = v.hidden[pl.ds(4 * i + 3, 4)].reshape(576, 128)
-        for a in range(3):
-            window = v.active[pl.ds(4 * i + 2 + a, 4)].reshape(576, 384)
-            total = total + dot(window, v.w_conv[a].reshape(384, 128))
+        windows = [v.active[pl.ds(4 * i + 2 + a, 4)].reshape(576, 384) for a in range(3)]
+        total = total + dot(jnp.concatenate(windows, axis=1), v.w_conv[...].reshape(1152, 128))
         v.outer[pl.ds(4 * i, 4)] = total.astype(B16).reshape(4, 144, 128)
 
     def turn(i):
@@ -535,42 +531,36 @@
         loss = weight * jnp.where(size <= 1.0, 0.5 * error * error, size - 0.5)
         loss = jnp.where(mine & quant, loss, 0.0)
         v.loss_sum[...] += loss[:, :128] + loss[:, 128:256] + loss[:, 256:384] + loss[:, 384:512]
-        down_b = down.astype(B16)
         v.head_sum[...] += dot(jnp.where(mine, down, 0.0).astype(B16)[:, :512], own)
-        across = dot(head, down_b[:, :512]).astype(B16)
-        along = dot(down.T.astype(B16), head_t)
+        edge = down[:, 512:]
+        at = lax.broadcasted_iota(jnp.int32, (1, 128), 1)
+        sets = []
         for s in range(4):
+            line = down[:, s * 128:(s + 1) * 128]
+            before = jnp.where(at == 0, pltpu.roll(edge, 113 - 16 * s, 1), pltpu.roll(line, 1, 1))
+            after = jnp.where(at == 127, pltpu.roll(edge, 127 - 16 * s, 1), pltpu.roll(line, 127, 1))
+            sets.append(jnp.concatenate([before, line, after], axis=0))
+            v.taps[4 * i + s] = sets[s].astype(B16)
             row_y = 4 * i + s - 1
             value = predicted[:, s * 128:(s + 1) * 128]
-
-            def keep():
+            if not isinstance(i, int) or 0 <= row_y < 32:
                 for q in range(QUANT):
                     v.quantiles[q, pl.ds(row_y, 1), :] = value[q:q + 1]
-
-            if isinstance(i, int):
-                if 0 <= row_y < 32:
-                    keep()
-            else:
-                keep()
-            v.out_turned[4 * i + s] = across[:, s * 128:(s + 1) * 128]
-            mid_part = along[s * 128:(s + 1) * 128]
-            v.out_grad[4 * i + s] = mid_part
-            full = jnp.concatenate([mid_part, along[512 + s * 16:528 + s * 16]], axis=0)
-            v.out_wide[4 * i + s] = shifted(full).astype(B16)
+        v.taps_turned[pl.ds(4 * i, 4)] = jnp.concatenate(sets, axis=1).T.astype(B16).reshape(4, 128, 48)
 
     def back(i):
-        total = None
-        for a in range(3):
-            window = v.out_wide[pl.ds(4 * i + a, 4), :128].reshape(512, 384)
-            turned = jnp.concatenate([v.w_conv[2 - a, 2 - b] for b in range(3)], axis=1)
-            part = dot_nt(window, turned)
-            total = part if total is None else total + part
-        dhidden = v.out_grad[pl.ds(4 * i + 1, 4)] + v.slope[pl.ds(4 * i + 4, 4)] * total.reshape(4, 128, 128)
+        windows = [v.taps_turned[pl.ds(4 * i + a, 4)].reshape(512, 48) for a in range(3)]
+        both = dot(windows[1], v.back_mid[...])
+        dactive = both[:, :128] + dot(windows[0], v.back_low[...]) + dot(windows[2], v.back_high[...])
+        dhidden = (both[:, 128:] + v.slope[pl.ds(4 * i + 4, 4)].reshape(512, 128) * dactive).reshape(4, 128, 128)
         v.grad_fine[pl.ds(4 * i, 4)] = dhidden * 1024.0
         summed = dhidden[0] + dhidden[1] + dhidden[2] + dhidden[3]
         high = summed.astype(B16)
         low = (summed - high.astype(F32)).astype(B16)
         v.dlift[i] = (dot(v.fold[...], high) + dot(v.fold[...], low)).astype(B16)
+        lines = [jnp.concatenate([v.taps[4 * i + a + s] for s in range(4)], axis=1) for a in range(3)]
+        seen = v.active[pl.ds(4 * i + 4, 4), :128, 128:256].reshape(512, 128)
+        v.tap_sum[...] += dot(jnp.concatenate(lines, axis=0), seen)
 
     def step(t):
         known = isinstance(t, int)
@@ -595,27 +585,22 @@
         step(t)
 
 
-def kernel_terms(v, low, high):
-    def one(i, carry):
-        across = jnp.concatenate([v.out_turned[4 * i + 1 + s] for s in range(4)], axis=1)
-        for a in range(3):
-            window = v.active[pl.ds(4 * i + 3 + a, 4), :128].reshape(512, 384)
-            v.kernel_sum[a] += dot(across, window)
-        return carry
-
-    lax.fori_loop(low, high, one, 0)
+def back_weights(v):
+    head_t = dot(v.eye[...], v.w_head_t[...]).astype(B16)
+    for a, name in enumerate(("back_low", "back_mid", "back_high")):
+        parts = [dot_nt(head_t, v.w_conv[2 - a, 2 - b]).astype(B16) for b in range(3)]
+        getattr(v, name)[:, :128] = jnp.concatenate(parts, axis=0)
+    blank = jnp.zeros((16, 128), B16)
+    v.back_mid[:, 128:] = jnp.concatenate([blank, head_t, blank], axis=0)
 
 
 def local_units(v):
-    for a in range(3):
-        for b in range(3):
-            at = 320 + a * 48 + b * 16
-            v.a_g[at:at + 16] = v.kernel_sum[a, :, b * 128:(b + 1) * 128].T.reshape(16, 8, 128).astype(B16)
+    v.a_g[128:146] = v.tap_sum[...].reshape(18, 8, 128).astype(B16)
     spot = lax.broadcasted_iota(jnp.int32, (16, 1), 0)
     total = jnp.sum(v.loss_sum[...], axis=0, keepdims=True)
     tail = jnp.where(spot < QUANT, v.head_sum[...], jnp.where(spot == QUANT, total, 0.0))
-    v.a_g[464:466] = tail.reshape(2, 8, 128).astype(B16)
-    v.a_g[466:EARLY] = jnp.zeros((EARLY - 466, 8, 128), B16)
+    v.a_g[146:148] = tail.reshape(2, 8, 128).astype(B16)
+    v.a_g[148:EARLY] = jnp.zeros((EARLY - 148, 8, 128), B16)
 
 
 def attend_back(v, mix_grad, s):
@@ -662,12 +647,14 @@
     barrier = pltpu.get_barrier_semaphore()
     for peer in peers:
         pl.semaphore_signal(barrier, inc=1, device_id=peer, device_id_type=MESH)
-    pl.semaphore_wait(barrier, len(peers))
-
     loads = [pltpu.make_async_copy(v.fine, v.field.at[pl.ds(4, 32), pl.ds(0, 128)], v.s_l.at[1]),
              pltpu.make_async_copy(v.w_qkv_in, v.w_qkv, v.s_l.at[2]),
              pltpu.make_async_copy(v.w_out_in, v.w_out, v.s_l.at[3]),
              pltpu.make_async_copy(v.w_conv_in, v.w_conv, v.s_l.at[4])]
+    for c in loads:
+        c.start()
+    v.bins16[...] = v.bins[...].astype(F32).astype(B16)
+    pl.semaphore_wait(barrier, len(peers))
     cols_finish = exchange_tokens(v, row, col, loads)
     loads[1].wait()
     loads[2].wait()
@@ -686,34 +673,35 @@
     v.lift_turned[...] = dot(v.back[...], v.slots[...].reshape(288, 128)).astype(B16).reshape(8, 48, 128)
     finish = spread_out("rows", 8, row, v.lift_turned, v.lifted, v.s_lr, v.r_lr, v.s_ly, v.r_ly)
     v.tok_turned[...] = v.tok[...].astype(F32).T.astype(B16)
-    v.mixed_turned[...] = v.mixed[...].astype(F32).T.astype(B16)
-    v.context_turned[...] = v.context[...].astype(F32).T.astype(B16)
-    v.kernel_sum[...] = jnp.zeros((3, 128, 384), F32)
     loads[3].wait()
+    back_weights(v)
     finish()
 
     convolve(v, row, col)
 
+    results = [pltpu.make_async_copy(v.grad_fine, v.grad_fine_out, v.s_l.at[5]),
+               pltpu.make_async_copy(v.quantiles, v.quantiles_out, v.s_l.at[6])]
     sends = scatter_out("rows", 8, v.dlift, v.fold_got, v.s_fr, v.r_fr, row)
     v.fold_got[row] = v.dlift[row]
-    kernel_terms(v, 0, 4)
+    for c in results:
+        c.start()
+    local_units(v)
     wait_all(sends)
     v.fold_turned[...] = dot(v.mid[...], v.fold_got[...].reshape(256, 128)).astype(B16).reshape(16, 16, 128)
     sends = scatter_out("cols", 16, v.fold_turned, v.folded, v.s_fc, v.r_fc, col)
     v.folded[col] = v.fold_turned[col]
-    kernel_terms(v, 4, 8)
-    local_units(v)
     wait_all(sends)
 
     early = reducer(me, EARLY, v.a_g, v.early, v.a_got0, v.a_sum0, v.a_got1, v.a_sum1, v.a_got2, v.a_sum2, v.a_got3,
                     [getattr(v, "a_sem" + str(n)) for n in range(16)])
     late = reducer(me, LATE, v.b_g, v.late, v.b_got0, v.b_sum0, v.b_got1, v.b_sum1, v.b_got2, v.b_sum2, v.b_got3,
                    [getattr(v, "b_sem" + str(n)) for n in range(16)])
-    lift = dot(v.group[...], v.folded[...].reshape(256, 128)).astype(B16)
+    lift_wide = dot(v.group[...], v.folded[...].reshape(256, 128))
+    lift, lift_turned = lift_wide.astype(B16), lift_wide.T.astype(B16)
+    put(v.a_g, 0, dot(lift_turned, v.mixed[...]))
+    put(v.a_g, 64, dot(lift_turned, v.context[...]))
+    early[0]()
     dcontext = dot_nt(lift, v.w_up[...]).astype(B16)
-    put(v.a_g, 0, dot(v.mixed_turned[...], dcontext))
-    put(v.a_g, 256, dot(v.context_turned[...], lift))
-    early[0]()
     mix_grad = dot_nt(dcontext, v.w_out[...]).astype(B16)
     attend_back(v, mix_grad, 0)
     early[1]()
@@ -736,29 +724,59 @@
     early[8]()
     for step in late[6:]:
         step()
-
-
-def unpack_kernel(early, late, grad_qkv, grad_out, grad_up, grad_conv, grad_head, loss):
-    for n in range(12):
-        grad_qkv[:, n * 128:(n + 1) * 128] = late[n * 64:(n + 1) * 64].astype(F32).reshape(512, 128)
+    wait_all(results)
+
+
+def unpack_kernel(early, late, fine, quantiles, w_up, w_head_t, eye,
+                  grad_qkv, grad_out, grad_up, grad_conv, grad_head, loss, fine_out, quantiles_out,
+                  late_in, early_in, wide, square, tall, flat, sems):
+    through = [pltpu.make_async_copy(fine, fine_out, sems.at[0]), pltpu.make_async_copy(quantiles, quantiles_out, sems.at[1])]
+    reads = [pltpu.make_async_copy(late.at[pl.ds(n * 256, 256)], late_in.at[pl.ds(n * 256, 256)], sems.at[2 + n]) for n in range(3)]
+    reads.append(pltpu.make_async_copy(early, early_in, sems.at[5]))
+    for c in reads + through:
+        c.start()
+    writes = []
+
+    def write(src, dst, n):
+        c = pltpu.make_async_copy(src, dst, sems.at[n])
+        c.start()
+        writes.append(c)
+
+    for n in range(3):
+        reads[n].wait()
+        for m in range(4):
+            at = n * 4 + m
+            wide[n, :, m * 128:(m + 1) * 128] = late_in[at * 64:(at + 1) * 64].astype(F32).reshape(512, 128)
+        write(wide.at[n], grad_qkv.at[:, pl.ds(n * 512, 512)], 6 + n)
+    reads[3].wait()
     for n in range(4):
-        grad_out[:, n * 128:(n + 1) * 128] = early[n * 64:(n + 1) * 64].astype(F32).reshape(512, 128)
-    grad_up[...] = early[256:320].astype(F32).reshape(512, 128)
-    grad_conv[...] = early[320:464].astype(F32).reshape(1152, 128)
-    tail = early[464:466].astype(F32).reshape(16, 128)
-    grad_head[...] = tail.T[:, :QUANT]
+        mixed = early_in[n * 16:(n + 1) * 16].astype(F32).reshape(128, 128).T.astype(B16)
+        square[n * 128:(n + 1) * 128] = dot_nt(mixed, w_up[...])
+        tall[n * 128:(n + 1) * 128] = early_in[64 + n * 16:64 + (n + 1) * 16].astype(F32).reshape(128, 128).T
+    write(square, grad_out, 9)
+    write(tall, grad_up, 10)
+    head_t = dot(eye[...], w_head_t[...]).astype(B16)
+    for a in range(3):
+        for b in range(3):
+            at = 128 + (2 - a) * 6 + (2 - b) * 2
+            seen = early_in[at:at + 2].astype(F32).reshape(16, 128).T.astype(B16)
+            flat[(a * 3 + b) * 128:(a * 3 + b + 1) * 128] = dot(seen, head_t)
+    write(flat, grad_conv, 11)
+    tail = early_in[146:148].astype(F32).reshape(16, 128)
+    grad_head[...] = tail[:QUANT]
     loss[...] = jnp.sum(tail[QUANT:QUANT + 1], axis=1, keepdims=True) * (1.0 / (1048576.0 * QUANT))
+    wait_all(writes + through)
 
 
 def body(fine_input, coarse, rain_bins, w_qkv, w_out, w_up, w_conv, w_head):
     group = group_table()
     eye = onehot(16, QUANT, [(q, q) for q in range(QUANT)])
-    args = [coarse[0], fine_input[0], rain_bins[0], w_qkv, w_out, w_up, w_conv, w_head,
+    args = [coarse[0], fine_input[0], rain_bins[0], w_qkv, w_out, w_up, w_conv, w_head.T,
             mid_table(), group, group.T, back_table(), pick_table(0), pick_table(14), spread_table(0), spread_table(14),
             bins_table(), up_table(), sum_table(), eye]
     spaces = scratch()
     names = INPUTS + tuple(name for name, _, _ in OUTPUTS) + tuple(name for name, _ in spaces)
-    vmem = pl.BlockSpec(memory_space=pltpu.VMEM)
+    vmem, anywhere = pl.BlockSpec(memory_space=pltpu.VMEM), pl.BlockSpec(memory_space=pl.ANY)
 
     def kernel(*refs):
         whole_kernel(names, *refs)
@@ -767,20 +785,22 @@
         kernel,
         out_shape=[jax.ShapeDtypeStruct(shape, dtype) for _, shape, dtype in OUTPUTS],
         in_specs=[pl.BlockSpec(memory_space=pl.ANY) if name in IN_HBM else vmem for name in INPUTS],
-        out_specs=[vmem] * len(OUTPUTS),
+        out_specs=[anywhere, anywhere, vmem, vmem],
         scratch_shapes=[space for _, space in spaces],
         compiler_params=pltpu.CompilerParams(vmem_limit_bytes=LIMIT, collective_id=1, has_side_effects=True),
     )(*args)
-    grad_qkv, grad_out, grad_up, grad_conv, grad_head, loss = pl.pallas_call(
+    shapes = ((512, 1536), (512, 512), (512, 128), (1152, 128), (QUANT, 128), (1, 1), (32, 128, 128), (9, 32, 128))
+    grad_qkv, grad_out, grad_up, grad_conv, grad_head, loss, fine, bands = pl.pallas_call(
         unpack_kernel,
-        out_shape=[jax.ShapeDtypeStruct(shape, F32)
-                   for shape in ((512, 1536), (512, 512), (512, 128), (1152, 128), (128, QUANT), (1, 1))],
-        in_specs=[vmem] * 2,
-        out_specs=[vmem] * 6,
+        out_shape=[jax.ShapeDtypeStruct(shape, F32) for shape in shapes],
+        in_specs=[anywhere] * 4 + [vmem] * 3,
+        out_specs=[anywhere] * 4 + [vmem] * 2 + [anywhere] * 2,
+        scratch_shapes=[pltpu.VMEM((LATE, 8, 128), B16), pltpu.VMEM((EARLY, 8, 128), B16), pltpu.VMEM((3, 512, 512), F32),
+                        pltpu.VMEM((512, 512), F32), pltpu.VMEM((512, 128), F32), pltpu.VMEM((1152, 128), F32), DMA((12,))],
         compiler_params=pltpu.CompilerParams(vmem_limit_bytes=LIMIT),
-    )(early, late)
-    return (quantiles[None], loss.reshape(()), grad_qkv, grad_out, grad_up, grad_conv.reshape(3, 3, 128, 128),
-            grad_head, grad_fine[None])
+    )(early, late, grad_fine, quantiles, w_up, w_head.T, eye)
+    return (bands[None], loss.reshape(()), grad_qkv, grad_out, grad_up, grad_conv.reshape(3, 3, 128, 128),
+            grad_head.T, fine[None])
 
 
 def solution(mesh):

time: 131 us -> 189 us (1.44)
  Pallas kernels: 126 us -> 188 us
  local copies, waits for them, and re-layouts: 4.91 us -> 0 us
    pallas_call x1, Pallas kernels: 4.3 us -> 70.7 us  [body(): pl.pallas_call(unpack_kernel, out_shape=[jax.ShapeDtypeStruct(shape, F32)...]
    unnamed x8 -> x0, local copies, waits for them, and re-layouts: 4.91 us -> none
    pallas_call x1, Pallas kernels: 121 us -> 118 us  [body(): pl.pallas_call(kernel, out_shape=[jax.ShapeDtypeStruct(shape, dtype) for...]
where the time goes in v4:
time: 189 us
  Pallas kernels  188 us (99%)
    pallas_call x1, Pallas kernels, body(): pl.pallas_call(kernel, out_shape=[jax.ShapeDtypeStruct(shape, dtype) for...  118 us
    pallas_call x1, Pallas kernels, body(): pl.pallas_call(unpack_kernel, out_shape=[jax.ShapeDtypeStruct(shape, F32)...  70.7 us

profile of v4, /device:TPU:1, one launch (start us, length us, event | category | flops | bytes accessed | tf_op | source)
XLA Modules:
  0.0 189.2 jit_solution(9589019495681361216)
XLA Ops:
  0.6 117.7 %shard_map.242 = (f32[9,32,128]{2,1,0:T(8,128)}, f32[32,128,128]{2,1,0:T(8,128)}, bf16[256,8,128]{2,1,0:T(8,128)(2,1)}, bf16[768,8,128]{2,1,0:T(8,128)(2,1)}) custom-call(bf16[8,32,512]{2,1,0:T(8,128)(2,1)} %bitcast.10, bf16[32,128,128]{2,1,0:T(8,128)(2,1)} %bitcast.9, s32[32,128]{1,0:T(8,128)} %bitcast.11, bf16[512,1536]{1,0:T(8,128)(2,1)} %refs_3_.1, ...), custom_call_target="tpu_custom_call" | custom-call | tf_op jit(solution)/shard_map/pallas_call | solution.py:784
  118.3 70.7 %shard_map.243 = (f32[512,1536]{1,0:T(8,128)}, f32[512,512]{1,0:T(8,128)}, f32[512,128]{1,0:T(8,128)}, f32[1152,128]{1,0:T(8,128)}, f32[9,128]{1,0:T(8,128)}, /*...) custom-call(bf16[256,8,128]{2,1,0:T(8,128)(2,1)} %get-tuple-element.20.early, ...), custom_call_target="tpu_custom_call" | custom-call | tf_op jit(solution)/shard_map/pallas_call | solution.py:793

commit v5 on v4

--- a/solution.py
+++ b/solution.py
@@ -15,7 +15,7 @@
 SCALE = HEAD_DIM ** (-0.5)
 ROOT_2_PI = 0.7978845608028654
 LIMIT = 58 * 1024 * 1024
-EARLY, LATE = 256, 768
+HALF = 512
 
 
 def onehot(rows, cols, pairs):
@@ -83,11 +83,19 @@
         c.wait()
 
 
-def scatter_out(axis, count, src, got, send, recv, me):
+def peer_order(axis, me):
+    if axis == "rows":
+        steps = [(2, 0), (2, 1), (1, 0), (3, 0), (1, 1), (3, 1), (0, 1)]
+        return [((me // 2 + a) % 4) * 2 + (me + b) % 2 for a, b in steps]
+    steps = [(a, b) for a in range(4) for b in range(4) if a + b > 0]
+    steps.sort(key=lambda step: -min(step[0], 4 - step[0]) - min(step[1], 4 - step[1]))
+    return [((me // 4 + a) % 4) * 4 + (me + b) % 4 for a, b in steps]
+
+
+def scatter_out(axis, src, got, send, recv, me):
     copies = []
-    for k in range(1, count):
-        p = (me + k) % count
-        c = rcopy(src.at[p], got.at[me], send.at[k - 1], recv.at[k - 1], {axis: p})
+    for n, p in enumerate(peer_order(axis, me)):
+        c = rcopy(src.at[p], got.at[me], send.at[n], recv.at[n], {axis: p})
         c.start()
         copies.append(c)
     return copies
@@ -95,9 +103,8 @@
 
 def spread_out(axis, count, me, src, main, send, recv, send_x, recv_x):
     copies = []
-    for k in range(1, count):
-        p = (me + k) % count
-        c = rcopy(src.at[p], main.at[1 + me], send.at[k - 1], recv.at[k - 1], {axis: p})
+    for n, p in enumerate(peer_order(axis, me)):
+        c = rcopy(src.at[p], main.at[1 + me], send.at[n], recv.at[n], {axis: p})
         c.start()
         copies.append(c)
     main[1 + me] = src[me]
@@ -173,8 +180,9 @@
     return jnp.concatenate([pltpu.roll(line, 1, 0), line, pltpu.roll(line, 143, 0)], axis=1)
 
 
-def reducer(me, units, g, out, got0, sum0, got1, sum1, got2, sum2, got3, sems):
-    core, first, second, deep = me.core, me.first, me.second, me.deep
+def reducer(me, axes, units, g, out, got0, sum0, got1, sum1, got2, sum2, got3, sems):
+    core, deep = me.core, me.deep
+    (first, in_first), (second, in_second) = axes
     u0, u1, u2, u3 = units // 2, units // 8, units // 32, units // 256
     s0, r0, s1, r1, s2, r2, s3, r3, as3, ar3, as2, ar2, as1, ar1, as0, ar0 = sems
     place = core * u0 + first * u1 + second * u2
@@ -189,7 +197,7 @@
     def near_start():
         held["near"] = []
         for n, k in enumerate((1, 2, 3, 0)):
-            p = (second + k) % 4
+            p = (first + k) % 4
             c = rcopy(g.at[pl.ds((1 - core) * u0 + p * u1, u1)], got0.at[p], s0.at[n], r0.at[n], me.other)
             c.start()
             held["near"].append(c)
@@ -200,7 +208,7 @@
             p = (first + k) % 4
             held["near"][n].wait_recv()
             sum0[p] = sum_up([g[pl.ds(core * u0 + p * u1, u1)], got0[p]]).astype(B16)
-            c = rcopy(sum0.at[p], got1.at[k - 1], s1.at[k - 1], r1.at[k - 1], me.in_first(k))
+            c = rcopy(sum0.at[p], got1.at[k - 1], s1.at[k - 1], r1.at[k - 1], in_first(k))
             c.start()
             held["first"].append(c)
         held["near"][3].wait_recv()
@@ -211,7 +219,7 @@
         held["second"] = []
         for k in (1, 2, 3):
             p = (second + k) % 4
-            c = rcopy(sum1.at[pl.ds(p * u2, u2)], got2.at[k - 1], s2.at[k - 1], r2.at[k - 1], me.in_second(k))
+            c = rcopy(sum1.at[pl.ds(p * u2, u2)], got2.at[k - 1], s2.at[k - 1], r2.at[k - 1], in_second(k))
             c.start()
             held["second"].append(c)
         for c in held["near"]:
@@ -221,7 +229,7 @@
         wait_all(held["second"])
         sum2[...] = sum_up([sum1[pl.ds(second * u2, u2)], got2[0], got2[1], got2[2]]).astype(B16)
         held["deep"] = []
-        for k in range(1, 8):
+        for k in (4, 3, 5, 2, 6, 1, 7):
             p = (deep + k) % 8
             c = rcopy(sum2.at[pl.ds(p * u3, u3)], got3.at[k - 1], s3.at[k - 1], r3.at[k - 1], me.in_deep(k))
             c.start()
@@ -233,7 +241,7 @@
         out[pl.ds(place + deep * u3, u3)] = mine.astype(B16)
         block = out.at[pl.ds(place + deep * u3, u3)]
         held["deep"] = []
-        for k in range(1, 8):
+        for k in (4, 3, 5, 2, 6, 1, 7):
             c = rcopy(block, block, as3.at[k - 1], ar3.at[k - 1], me.in_deep(k))
             c.start()
             held["deep"].append(c)
@@ -243,7 +251,7 @@
         block = out.at[pl.ds(place, u2)]
         held["second"] = []
         for k in (1, 2, 3):
-            c = rcopy(block, block, as2.at[k - 1], ar2.at[k - 1], me.in_second(k))
+            c = rcopy(block, block, as2.at[k - 1], ar2.at[k - 1], in_second(k))
             c.start()
             held["second"].append(c)
 
@@ -258,7 +266,7 @@
         block = out.at[pl.ds(core * u0 + first * u1, u1)]
         held["first"], held["near"] = [], []
         for k in (1, 2, 3):
-            c = rcopy(block, block, as1.at[k - 1], ar1.at[k - 1], me.in_first(k))
+            c = rcopy(block, block, as1.at[k - 1], ar1.at[k - 1], in_first(k))
             c.start()
             held["first"].append(c)
         forward(0, first)
@@ -292,7 +300,7 @@
           "mid", "group", "ungroup", "back", "pick_lo", "pick_hi", "spread_lo", "spread_hi", "place", "up", "fold", "eye")
 IN_HBM = ("coarse", "fine", "w_qkv_in", "w_out_in", "w_conv_in")
 OUTPUTS = (("quantiles_out", (9, 32, 128), F32), ("grad_fine_out", (32, 128, 128), F32),
-           ("early", (EARLY, 8, 128), B16), ("late", (LATE, 8, 128), B16))
+           ("low_half", (HALF, 8, 128), B16), ("high_half", (HALF, 8, 128), B16))
 
 
 def scratch():
@@ -319,7 +327,7 @@
             ("s_fr", 7), ("r_fr", 7), ("s_fc", 15), ("r_fc", 15)]
     return ([(name, pltpu.VMEM(shape, dtype)) for name, shape, dtype in buffers]
             + [(name, DMA((count,))) for name, count in sems]
-            + reducer_scratch("a_", EARLY) + reducer_scratch("b_", LATE))
+            + reducer_scratch("a_", HALF) + reducer_scratch("b_", HALF))
 
 
 def halo_rows(v, row):
@@ -393,7 +401,7 @@
 
 
 def exchange_tokens(v, row, col, loads):
-    sends = scatter_out("rows", 8, v.coarse, v.got, v.s_tr, v.r_tr, row)
+    sends = scatter_out("rows", v.coarse, v.got, v.s_tr, v.r_tr, row)
     own = pltpu.make_async_copy(v.coarse.at[row], v.got.at[row], v.s_l.at[0])
     own.start()
     rows_start, rows_finish = halo_rows(v, row)
@@ -416,7 +424,7 @@
     own.wait()
     wait_all(sends)
     v.turned[...] = dot(v.mid[...], v.got[...].reshape(256, 512)).astype(B16).reshape(16, 16, 512)
-    sends = scatter_out("cols", 16, v.turned, v.tokens, v.s_tc, v.r_tc, col)
+    sends = scatter_out("cols", v.turned, v.tokens, v.s_tc, v.r_tc, col)
     v.tokens[col] = v.turned[col]
 
     loads[0].wait()
@@ -488,17 +496,23 @@
     v.loss_sum[...] = jnp.zeros((16, 128), F32)
     v.head_sum[...] = jnp.zeros((16, 128), F32)
     v.tap_sum[...] = jnp.zeros((144, 128), F32)
+    v.active[pl.ds(38, 2)] = jnp.zeros((2, 144, 384), B16)
+    v.hidden[pl.ds(38, 2)] = jnp.zeros((2, 144, 128), F32)
 
     def start(i):
         raised = dot(v.up[...], v.lifted[i])
-        for s in range(4):
+        rims = {0: (2, 3), 9: (0, 1)}.get(i, range(4)) if isinstance(i, int) else range(4)
+        for s in rims:
             y = 4 * i + s - 4
             x = v.field[4 * i + s].astype(F32) + raised
             square = x * x
             bend = jnp.tanh(ROOT_2_PI * x * (1.0 + 0.044715 * square))
             half = 0.5 * (1.0 + bend)
-            seen = (row * 32 + y >= 0) & (row * 32 + y < 256)
-            act = jnp.where(inside & seen, x * half, 0.0)
+            act = x * half
+            if isinstance(i, int) and i in (0, 9):
+                act = jnp.where(inside & (row * 32 + y >= 0) & (row * 32 + y < 256), act, 0.0)
+            else:
+                act = jnp.concatenate([act[:128], jnp.where(inside[128:], act[128:], 0.0)], axis=0)
             v.hidden[4 * i + s] = x
             v.active[4 * i + s] = shifted(act).astype(B16)
             v.slope[4 * i + s] = half[:128] + (0.5 * ROOT_2_PI) * x[:128] * (1.0 - bend[:128] * bend[:128]) * (
@@ -580,8 +594,8 @@
         step(t)
         return carry
 
-    lax.fori_loop(5, 10, loop, 0)
-    for t in range(10, 13):
+    lax.fori_loop(5, 9, loop, 0)
+    for t in range(9, 13):
         step(t)
 
 
@@ -595,16 +609,16 @@
 
 
 def local_units(v):
-    v.a_g[128:146] = v.tap_sum[...].reshape(18, 8, 128).astype(B16)
+    v.b_g[384:402] = v.tap_sum[...].reshape(18, 8, 128).astype(B16)
     spot = lax.broadcasted_iota(jnp.int32, (16, 1), 0)
     total = jnp.sum(v.loss_sum[...], axis=0, keepdims=True)
     tail = jnp.where(spot < QUANT, v.head_sum[...], jnp.where(spot == QUANT, total, 0.0))
-    v.a_g[146:148] = tail.reshape(2, 8, 128).astype(B16)
-    v.a_g[148:EARLY] = jnp.zeros((EARLY - 148, 8, 128), B16)
-
-
-def attend_back(v, mix_grad, s):
-    for t in range(4):
+    v.b_g[402:404] = tail.reshape(2, 8, 128).astype(B16)
+    v.b_g[404:HALF] = jnp.zeros((HALF - 404, 8, 128), B16)
+
+
+def attend_back(v, mix_grad, g, tiles):
+    for s, t in [(s, t) for s in range(2) for t in tiles]:
         rows, at = slice(s * 128, s * 128 + 128), t * 128
         keyed = v.qkv[rows, 512 + at:512 + at + 128]
         valued = v.qkv[rows, 1024 + at:1024 + at + 128]
@@ -616,6 +630,10 @@
         v.dquery[rows, at:at + 128] = dot(side_by_side(dscore), heads_down(keyed)).astype(B16)
         v.dkey[at:at + 128, rows] = dot(v.query_turned[s * 4 + t], dscore).astype(B16)
         v.dvalue[at:at + 128, rows] = dot(heads_across(mine), share.astype(B16)).astype(B16)
+    at = tiles[0] * 128
+    put(g, 0, dot(v.tok_turned[...], v.dquery[:, at:at + 256]))
+    put(g, 128, dot_nt(v.tok_turned[...], v.dkey[at:at + 256]))
+    put(g, 256, dot_nt(v.tok_turned[...], v.dvalue[at:at + 256]))
 
 
 def whole_kernel(names, *refs):
@@ -625,22 +643,15 @@
     x, y = col // 4, col % 4
     me = SimpleNamespace(
         core=core, deep=deep, other={"rows": row + 1 - 2 * core},
-        first=x * (1 - core) + y * core, second=y * (1 - core) + x * core,
     )
-
-    def in_first(k):
-        p = (me.first + k) % 4
-        return {"cols": (p * 4 + y) * (1 - core) + (x * 4 + p) * core}
-
-    def in_second(k):
-        p = (me.second + k) % 4
-        return {"cols": (x * 4 + p) * (1 - core) + (p * 4 + y) * core}
+    x_axis = (x, lambda k: {"cols": ((x + k) % 4) * 4 + y})
+    y_axis = (y, lambda k: {"cols": x * 4 + (y + k) % 4})
 
     def in_deep(k):
         p = (deep + k) % 8
         return {"rows": (p // 2) * 2 + core, "batch": p % 2}
 
-    me.in_first, me.in_second, me.in_deep = in_first, in_second, in_deep
+    me.in_deep = in_deep
 
     peers = [{"rows": (row + k) % 8} for k in range(1, 8)] + [{"cols": (col + k) % 16} for k in range(1, 16)]
     peers += [{"rows": (row + 2 * k) % 8, "batch": 1 - batch} for k in range(4)]
@@ -681,59 +692,48 @@
 
     results = [pltpu.make_async_copy(v.grad_fine, v.grad_fine_out, v.s_l.at[5]),
                pltpu.make_async_copy(v.quantiles, v.quantiles_out, v.s_l.at[6])]
-    sends = scatter_out("rows", 8, v.dlift, v.fold_got, v.s_fr, v.r_fr, row)
+    sends = scatter_out("rows", v.dlift, v.fold_got, v.s_fr, v.r_fr, row)
     v.fold_got[row] = v.dlift[row]
     for c in results:
         c.start()
     local_units(v)
     wait_all(sends)
     v.fold_turned[...] = dot(v.mid[...], v.fold_got[...].reshape(256, 128)).astype(B16).reshape(16, 16, 128)
-    sends = scatter_out("cols", 16, v.fold_turned, v.folded, v.s_fc, v.r_fc, col)
+    sends = scatter_out("cols", v.fold_turned, v.folded, v.s_fc, v.r_fc, col)
     v.folded[col] = v.fold_turned[col]
     wait_all(sends)
 
-    early = reducer(me, EARLY, v.a_g, v.early, v.a_got0, v.a_sum0, v.a_got1, v.a_sum1, v.a_got2, v.a_sum2, v.a_got3,
-                    [getattr(v, "a_sem" + str(n)) for n in range(16)])
-    late = reducer(me, LATE, v.b_g, v.late, v.b_got0, v.b_sum0, v.b_got1, v.b_sum1, v.b_got2, v.b_sum2, v.b_got3,
-                   [getattr(v, "b_sem" + str(n)) for n in range(16)])
+    low = reducer(me, (x_axis, y_axis), HALF, v.a_g, v.low_half, v.a_got0, v.a_sum0, v.a_got1, v.a_sum1, v.a_got2, v.a_sum2,
+                  v.a_got3, [getattr(v, "a_sem" + str(n)) for n in range(16)])
+    high = reducer(me, (y_axis, x_axis), HALF, v.b_g, v.high_half, v.b_got0, v.b_sum0, v.b_got1, v.b_sum1, v.b_got2, v.b_sum2,
+                   v.b_got3, [getattr(v, "b_sem" + str(n)) for n in range(16)])
     lift_wide = dot(v.group[...], v.folded[...].reshape(256, 128))
     lift, lift_turned = lift_wide.astype(B16), lift_wide.T.astype(B16)
-    put(v.a_g, 0, dot(lift_turned, v.mixed[...]))
-    put(v.a_g, 64, dot(lift_turned, v.context[...]))
-    early[0]()
     dcontext = dot_nt(lift, v.w_up[...]).astype(B16)
     mix_grad = dot_nt(dcontext, v.w_out[...]).astype(B16)
-    attend_back(v, mix_grad, 0)
-    early[1]()
-    attend_back(v, mix_grad, 1)
-    early[2]()
-    put(v.b_g, 0, dot(v.tok_turned[...], v.dquery[...]))
-    put(v.b_g, 256, dot_nt(v.tok_turned[...], v.dkey[...]))
-    put(v.b_g, 512, dot_nt(v.tok_turned[...], v.dvalue[...]))
-    late[0]()
-    early[3]()
-    late[1]()
-    early[4]()
-    late[2]()
-    early[5]()
-    late[3]()
-    early[6]()
-    late[4]()
-    early[7]()
-    late[5]()
-    early[8]()
-    for step in late[6:]:
-        step()
+    put(v.a_g, 384, dot(lift_turned, v.mixed[...]))
+    put(v.a_g, 448, dot(lift_turned, v.context[...]))
+    attend_back(v, mix_grad, v.a_g, (0, 1))
+    low[0]()
+    attend_back(v, mix_grad, v.b_g, (2, 3))
+    high[0]()
+    low[1]()
+    high[1]()
+    for n in range(2, 9):
+        low[n]()
+        high[n]()
     wait_all(results)
 
 
-def unpack_kernel(early, late, fine, quantiles, w_up, w_head_t, eye,
+def unpack_kernel(low, high, fine, quantiles, w_up, w_head_t, eye,
                   grad_qkv, grad_out, grad_up, grad_conv, grad_head, loss, fine_out, quantiles_out,
-                  late_in, early_in, wide, square, tall, flat, sems):
-    through = [pltpu.make_async_copy(fine, fine_out, sems.at[0]), pltpu.make_async_copy(quantiles, quantiles_out, sems.at[1])]
-    reads = [pltpu.make_async_copy(late.at[pl.ds(n * 256, 256)], late_in.at[pl.ds(n * 256, 256)], sems.at[2 + n]) for n in range(3)]
-    reads.append(pltpu.make_async_copy(early, early_in, sems.at[5]))
-    for c in reads + through:
+                  held, wide, square, tall, flat, fine_in, bands_in, sems):
+    through = [(fine.at[pl.ds(n * 8, 8)], fine_in.at[pl.ds(n * 8, 8)], fine_out.at[pl.ds(n * 8, 8)]) for n in range(4)]
+    through.append((quantiles, bands_in, quantiles_out))
+    passing = [pltpu.make_async_copy(src, held, sems.at[12 + n]) for n, (src, held, _) in enumerate(through)]
+    reads = [pltpu.make_async_copy((low, high)[h].at[pl.ds(a, b)], held.at[h, pl.ds(a, b)], sems.at[2 * n + h])
+             for n, (a, b) in enumerate(((0, 384), (384, 128))) for h in range(2)]
+    for c in reads[:2] + passing + reads[2:]:
         c.start()
     writes = []
 
@@ -742,30 +742,36 @@
         c.start()
         writes.append(c)
 
-    for n in range(3):
-        reads[n].wait()
-        for m in range(4):
-            at = n * 4 + m
-            wide[n, :, m * 128:(m + 1) * 128] = late_in[at * 64:(at + 1) * 64].astype(F32).reshape(512, 128)
-        write(wide.at[n], grad_qkv.at[:, pl.ds(n * 512, 512)], 6 + n)
+    for h in range(2):
+        reads[h].wait()
+        for n in range(3):
+            for m in range(2):
+                at = n * 128 + m * 64
+                wide[n, :, h * 256 + m * 128:h * 256 + (m + 1) * 128] = held[h, at:at + 64].astype(F32).reshape(512, 128)
+            if h == 1:
+                write(wide.at[n], grad_qkv.at[:, pl.ds(n * 512, 512)], 6 + n)
+        for m in ((0, 1, 2), (3, 4))[h]:
+            passing[m].wait()
+            write(through[m][1], through[m][2], 17 + m)
+    reads[2].wait()
     reads[3].wait()
     for n in range(4):
-        mixed = early_in[n * 16:(n + 1) * 16].astype(F32).reshape(128, 128).T.astype(B16)
+        mixed = held[0, 384 + n * 16:384 + (n + 1) * 16].astype(F32).reshape(128, 128).T.astype(B16)
         square[n * 128:(n + 1) * 128] = dot_nt(mixed, w_up[...])
-        tall[n * 128:(n + 1) * 128] = early_in[64 + n * 16:64 + (n + 1) * 16].astype(F32).reshape(128, 128).T
+        tall[n * 128:(n + 1) * 128] = held[0, 448 + n * 16:448 + (n + 1) * 16].astype(F32).reshape(128, 128).T
     write(square, grad_out, 9)
     write(tall, grad_up, 10)
     head_t = dot(eye[...], w_head_t[...]).astype(B16)
     for a in range(3):
         for b in range(3):
-            at = 128 + (2 - a) * 6 + (2 - b) * 2
-            seen = early_in[at:at + 2].astype(F32).reshape(16, 128).T.astype(B16)
+            at = 384 + (2 - a) * 6 + (2 - b) * 2
+            seen = held[1, at:at + 2].astype(F32).reshape(16, 128).T.astype(B16)
             flat[(a * 3 + b) * 128:(a * 3 + b + 1) * 128] = dot(seen, head_t)
     write(flat, grad_conv, 11)
-    tail = early_in[146:148].astype(F32).reshape(16, 128)
+    tail = held[1, 402:404].astype(F32).reshape(16, 128)
     grad_head[...] = tail[:QUANT]
     loss[...] = jnp.sum(tail[QUANT:QUANT + 1], axis=1, keepdims=True) * (1.0 / (1048576.0 * QUANT))
-    wait_all(writes + through)
+    wait_all(writes)
 
 
 def body(fine_input, coarse, rain_bins, w_qkv, w_out, w_up, w_conv, w_head):
@@ -781,7 +787,7 @@
     def kernel(*refs):
         whole_kernel(names, *refs)
 
-    quantiles, grad_fine, early, late = pl.pallas_call(
+    quantiles, grad_fine, low, high = pl.pallas_call(
         kernel,
         out_shape=[jax.ShapeDtypeStruct(shape, dtype) for _, shape, dtype in OUTPUTS],
         in_specs=[pl.BlockSpec(memory_space=pl.ANY) if name in IN_HBM else vmem for name in INPUTS],
@@ -795,10 +801,11 @@
         out_shape=[jax.ShapeDtypeStruct(shape, F32) for shape in shapes],
         in_specs=[anywhere] * 4 + [vmem] * 3,
         out_specs=[anywhere] * 4 + [vmem] * 2 + [anywhere] * 2,
-        scratch_shapes=[pltpu.VMEM((LATE, 8, 128), B16), pltpu.VMEM((EARLY, 8, 128), B16), pltpu.VMEM((3, 512, 512), F32),
-                        pltpu.VMEM((512, 512), F32), pltpu.VMEM((512, 128), F32), pltpu.VMEM((1152, 128), F32), DMA((12,))],
+        scratch_shapes=[pltpu.VMEM((2, HALF, 8, 128), B16), pltpu.VMEM((3, 512, 512), F32),
+                        pltpu.VMEM((512, 512), F32), pltpu.VMEM((512, 128), F32), pltpu.VMEM((1152, 128), F32),
+                        pltpu.VMEM((32, 128, 128), F32), pltpu.VMEM((9, 32, 128), F32), DMA((22,))],
         compiler_params=pltpu.CompilerParams(vmem_limit_bytes=LIMIT),
-    )(early, late, grad_fine, quantiles, w_up, w_head.T, eye)
+    )(low, high, grad_fine, quantiles, w_up, w_head.T, eye)
     return (bands[None], loss.reshape(()), grad_qkv, grad_out, grad_up, grad_conv.reshape(3, 3, 128, 128),
             grad_head.T, fine[None])
 

time: 189 us -> 112 us (0.59)
  Pallas kernels: 188 us -> 111 us
    pallas_call x1, Pallas kernels: 70.7 us -> 6.2 us  [body(): pl.pallas_call(unpack_kernel, out_shape=[jax.ShapeDtypeStruct(shape, F32)...]
    pallas_call x1, Pallas kernels: 118 us -> 105 us  [body(): pl.pallas_call(kernel, out_shape=[jax.ShapeDtypeStruct(shape, dtype) for...]
where the time goes in v5:
time: 112 us
  Pallas kernels  111 us (99%)
    pallas_call x1, Pallas kernels, body(): pl.pallas_call(kernel, out_shape=[jax.ShapeDtypeStruct(shape, dtype) for...  105 us
    pallas_call x1, Pallas kernels, body(): pl.pallas_call(unpack_kernel, out_shape=[jax.ShapeDtypeStruct(shape, F32)...  6.2 us

profile of v5, /device:TPU:1, one launch (start us, length us, event | category | flops | bytes accessed | tf_op | source)
XLA Modules:
  0.0 112.1 jit_solution(4322696685722957276)
XLA Ops:
  0.6 105.1 %shard_map.242 = (f32[9,32,128]{2,1,0:T(8,128)}, f32[32,128,128]{2,1,0:T(8,128)}, bf16[512,8,128]{2,1,0:T(8,128)(2,1)}, bf16[512,8,128]{2,1,0:T(8,128)(2,1)}) custom-call(bf16[8,32,512]{2,1,0:T(8,128)(2,1)} %bitcast.10, bf16[32,128,128]{2,1,0:T(8,128)(2,1)} %bitcast.9, s32[32,128]{1,0:T(8,128)} %bitcast.11, bf16[512,1536]{1,0:T(8,128)(2,1)} %refs_3_.1, ...), custom_call_target="tpu_custom_call" | custom-call | tf_op jit(solution)/shard_map/pallas_call | solution.py:790
  105.7 6.2 %shard_map.243 = (f32[512,1536]{1,0:T(8,128)}, f32[512,512]{1,0:T(8,128)}, f32[512,128]{1,0:T(8,128)}, f32[1152,128]{1,0:T(8,128)}, f32[9,128]{1,0:T(8,128)}, /*...) custom-call(bf16[512,8,128]{2,1,0:T(8,128)(2,1)} %get-tuple-element.20.low, ...), custom_call_target="tpu_custom_call" | custom-call | tf_op jit(solution)/shard_map/pallas_call | solution.py:799

commit v6 on v5

--- a/solution.py
+++ b/solution.py
@@ -32,6 +32,11 @@
 
 def group_table():
     return onehot(256, 256, [(m * 128 + c * 8 + r, c * 16 + r * 2 + m)
+                             for m in range(2) for c in range(16) for r in range(8)])
+
+
+def cross_table():
+    return onehot(256, 256, [(m * 128 + c * 8 + r, r * 32 + c * 2 + m)
                              for m in range(2) for c in range(16) for r in range(8)])
 
 
@@ -296,9 +301,9 @@
     return result
 
 
-INPUTS = ("coarse", "fine", "bins", "w_qkv_in", "w_out_in", "w_up", "w_conv_in", "w_head_t",
-          "mid", "group", "ungroup", "back", "pick_lo", "pick_hi", "spread_lo", "spread_hi", "place", "up", "fold", "eye")
-IN_HBM = ("coarse", "fine", "w_qkv_in", "w_out_in", "w_conv_in")
+INPUTS = ("coarse", "fine", "bins", "w_qkv_in", "w_out_in", "w_up_in", "w_conv_in", "w_head_t",
+          "turns_in", "back_in", "pick_lo", "pick_hi", "spread_lo", "spread_hi", "place", "up", "fold", "eye")
+IN_HBM = ("coarse", "fine", "w_qkv_in", "w_out_in", "w_up_in", "w_conv_in", "turns_in", "back_in")
 OUTPUTS = (("quantiles_out", (9, 32, 128), F32), ("grad_fine_out", (32, 128, 128), F32),
            ("low_half", (HALF, 8, 128), B16), ("high_half", (HALF, 8, 128), B16))
 
@@ -306,7 +311,10 @@
 def scratch():
     buffers = [
         ("w_qkv", (512, 1536), B16), ("w_out", (512, 512), B16), ("w_conv", (3, 3, 128, 128), B16),
-        ("got", (8, 32, 512), B16), ("turned", (16, 16, 512), B16), ("tokens", (16, 16, 512), B16),
+        ("w_up", (512, 128), B16), ("turns", (5, 256, 256), B16), ("back", (384, 288), B16),
+        ("got", (8, 32, 256), B16), ("turned", (16, 16, 256), B16), ("tokens", (16, 16, 256), B16),
+        ("half", (8, 32, 256), B16), ("half_turned", (16, 16, 256), B16), ("half_got", (16, 16, 256), B16),
+        ("half_cross", (8, 32, 256), B16), ("half_tokens", (8, 32, 256), B16),
         ("field", (40, 144, 128), B16), ("bins16", (32, 128), B16), ("bin_got", (64, 128), B16),
         ("edge_out", (2, 5, 16, 128), B16), ("edge_in", (2, 5, 16, 128), B16), ("bin_out", (2, 48, 128), B16),
         ("bin_in", (2, 48, 128), B16), ("rain", (48, 128), F32), ("edge_bins", (16, 128), F32),
@@ -317,14 +325,14 @@
         ("hidden", (40, 144, 128), F32), ("slope", (40, 128, 128), F32), ("active", (40, 144, 384), B16),
         ("outer", (36, 144, 128), B16), ("taps", (36, 48, 128), B16), ("taps_turned", (36, 128, 48), B16),
         ("back_low", (48, 128), B16), ("back_mid", (48, 256), B16), ("back_high", (48, 128), B16),
-        ("tap_sum", (144, 128), F32), ("loss_sum", (16, 128), F32), ("head_sum", (16, 128), F32),
+        ("tap_sum", (144, 128), F32), ("pair", (1536, 256), B16), ("loss_sum", (16, 128), F32), ("head_sum", (16, 128), F32),
         ("dlift", (8, 32, 128), B16), ("grad_fine", (32, 128, 128), F32), ("quantiles", (9, 32, 128), F32),
         ("fold_got", (8, 32, 128), B16), ("fold_turned", (16, 16, 128), B16), ("folded", (16, 16, 128), B16),
         ("dquery", (256, 512), B16), ("dkey", (512, 256), B16), ("dvalue", (512, 256), B16),
     ]
-    sems = [("s_l", 7), ("s_tr", 7), ("r_tr", 7), ("s_tc", 15), ("r_tc", 15), ("s_h", 4), ("r_h", 4), ("s_e", 4), ("r_e", 4),
+    sems = [("s_l", 11), ("s_ur", 7), ("r_ur", 7), ("s_uc", 15), ("r_uc", 15), ("s_tr", 7), ("r_tr", 7), ("s_tc", 15), ("r_tc", 15), ("s_h", 4), ("r_h", 4), ("s_e", 4), ("r_e", 4),
             ("s_lc", 15), ("r_lc", 15), ("s_lx", 16), ("r_lx", 2), ("s_lr", 7), ("r_lr", 7), ("s_ly", 8), ("r_ly", 2),
-            ("s_fr", 7), ("r_fr", 7), ("s_fc", 15), ("r_fc", 15)]
+            ("s_fr", 8), ("r_fr", 8), ("s_fc", 15), ("r_fc", 15)]
     return ([(name, pltpu.VMEM(shape, dtype)) for name, shape, dtype in buffers]
             + [(name, DMA((count,))) for name, count in sems]
             + reducer_scratch("a_", HALF) + reducer_scratch("b_", HALF))
@@ -401,9 +409,14 @@
 
 
 def exchange_tokens(v, row, col, loads):
-    sends = scatter_out("rows", v.coarse, v.got, v.s_tr, v.r_tr, row)
-    own = pltpu.make_async_copy(v.coarse.at[row], v.got.at[row], v.s_l.at[0])
+    low = [rcopy(v.coarse.at[p, :, pl.ds(0, 256)], v.got.at[row], v.s_tr.at[n], v.r_tr.at[n], {"rows": p})
+           for n, p in enumerate(peer_order("rows", row))]
+    for c in low:
+        c.start()
+    high = scatter_out("cols", v.half_turned, v.half_got, v.s_uc, v.r_uc, col)
+    own = pltpu.make_async_copy(v.coarse.at[row, :, pl.ds(0, 256)], v.got.at[row], v.s_l.at[0])
     own.start()
+    v.half_got[col] = v.half_turned[col]
     rows_start, rows_finish = halo_rows(v, row)
     rows_start()
 
@@ -422,9 +435,13 @@
     v.bin_got[pl.ds(16, 32)] = v.bins16[...]
 
     own.wait()
-    wait_all(sends)
-    v.turned[...] = dot(v.mid[...], v.got[...].reshape(256, 512)).astype(B16).reshape(16, 16, 512)
-    sends = scatter_out("cols", v.turned, v.tokens, v.s_tc, v.r_tc, col)
+    wait_all(high)
+    v.half_cross[...] = dot(v.turns[1], v.half_got[...].reshape(256, 256)).astype(B16).reshape(8, 32, 256)
+    high = scatter_out("rows", v.half_cross, v.half_tokens, v.s_ur, v.r_ur, row)
+    v.half_tokens[row] = v.half_cross[row]
+    wait_all(low)
+    v.turned[...] = dot(v.turns[0], v.got[...].reshape(256, 256)).astype(B16).reshape(16, 16, 256)
+    low = scatter_out("cols", v.turned, v.tokens, v.s_tc, v.r_tc, col)
     v.tokens[col] = v.turned[col]
 
     loads[0].wait()
@@ -449,12 +466,14 @@
         v.edge_in[1] = jnp.zeros((5, 16, 128), B16)
         v.bin_in[1] = jnp.zeros((48, 128), B16)
 
-    wait_all(sends)
+    wait_all(low)
+    wait_all(high)
     return cols_finish
 
 
 def attend(v):
-    v.tok[...] = dot(v.group[...], v.tokens[...].reshape(256, 512)).astype(B16)
+    v.tok[:, :256] = dot(v.turns[2], v.tokens[...].reshape(256, 256)).astype(B16)
+    v.tok[:, 256:] = dot(v.turns[3], v.half_tokens[...].reshape(256, 256)).astype(B16)
     for n in range(3):
         v.qkv[:, n * 512:(n + 1) * 512] = dot(v.tok[...], v.w_qkv[:, n * 512:(n + 1) * 512]).astype(B16)
     for g in range(2):
@@ -472,7 +491,7 @@
     attended = dot(v.mixed[...], v.w_out[...]).astype(B16)
     v.context[...] = (v.tok[...].astype(F32) + attended.astype(F32)).astype(B16)
     lifted = dot(v.context[...], v.w_up[...]).astype(B16)
-    v.raised[...] = dot(v.ungroup[...], lifted).astype(B16).reshape(16, 16, 128)
+    v.raised[...] = dot(v.turns[4], lifted).astype(B16).reshape(16, 16, 128)
 
 
 def edge_targets(v):
@@ -483,6 +502,16 @@
     for b in range(9):
         here = line == 4 * b + (lane >> 4)
         v.edge_bins[b:b + 1] = jnp.sum(jnp.where(here, picked, 0.0), axis=0, keepdims=True)
+
+
+def fold_copy(v, row, target, source):
+    return rcopy(v.dlift.at[target], v.fold_got.at[source], v.s_fr.at[target], v.r_fr.at[source], {"rows": target})
+
+
+def send_fold(v, row, target):
+    @pl.when(row != target)
+    def _():
+        fold_copy(v, row, target, row).start()
 
 
 def convolve(v, row, col):
@@ -519,10 +548,11 @@
                 1.0 + (3 * 0.044715) * square[:128])
 
     def forward(i):
-        total = v.hidden[pl.ds(4 * i + 3, 4)].reshape(576, 128)
-        windows = [v.active[pl.ds(4 * i + 2 + a, 4)].reshape(576, 384) for a in range(3)]
-        total = total + dot(jnp.concatenate(windows, axis=1), v.w_conv[...].reshape(1152, 128))
-        v.outer[pl.ds(4 * i, 4)] = total.astype(B16).reshape(4, 144, 128)
+        windows = [jnp.concatenate([v.active[4 * i + 2 + a], v.active[4 * i + 4 + a]], axis=0) for a in range(4)]
+        both = dot(jnp.concatenate(windows, axis=1), v.pair[...])
+        for s in range(4):
+            at, part = s // 2 * 144, s % 2 * 128
+            v.outer[4 * i + s] = (v.hidden[4 * i + 3 + s] + both[at:at + 144, part:part + 128]).astype(B16)
 
     def turn(i):
         own = v.outer[pl.ds(4 * i, 4), :128].reshape(512, 128)
@@ -595,8 +625,11 @@
         return carry
 
     lax.fori_loop(5, 9, loop, 0)
+    for n in range(4):
+        send_fold(v, row, n)
     for t in range(9, 13):
         step(t)
+        send_fold(v, row, t - 5)
 
 
 def back_weights(v):
@@ -604,6 +637,10 @@
     for a, name in enumerate(("back_low", "back_mid", "back_high")):
         parts = [dot_nt(head_t, v.w_conv[2 - a, 2 - b]).astype(B16) for b in range(3)]
         getattr(v, name)[:, :128] = jnp.concatenate(parts, axis=0)
+    for a in range(4):
+        for b in range(2):
+            block = v.w_conv[a - b].reshape(384, 128) if 0 <= a - b < 3 else jnp.zeros((384, 128), B16)
+            v.pair[a * 384:(a + 1) * 384, b * 128:(b + 1) * 128] = block
     blank = jnp.zeros((16, 128), B16)
     v.back_mid[:, 128:] = jnp.concatenate([blank, head_t, blank], axis=0)
 
@@ -653,22 +690,32 @@
 
     me.in_deep = in_deep
 
-    peers = [{"rows": (row + k) % 8} for k in range(1, 8)] + [{"cols": (col + k) % 16} for k in range(1, 16)]
-    peers += [{"rows": (row + 2 * k) % 8, "batch": 1 - batch} for k in range(4)]
+    peers = [{"rows": p} for p in peer_order("rows", row)]
+    peers = peers[:2] + [{"rows": (row + 2 * k) % 8, "batch": 1 - batch} for k in (2, 1, 3, 0)] + peers[2:6] + [
+        {"cols": p} for p in peer_order("cols", col)] + peers[6:]
     barrier = pltpu.get_barrier_semaphore()
     for peer in peers:
         pl.semaphore_signal(barrier, inc=1, device_id=peer, device_id_type=MESH)
     loads = [pltpu.make_async_copy(v.fine, v.field.at[pl.ds(4, 32), pl.ds(0, 128)], v.s_l.at[1]),
              pltpu.make_async_copy(v.w_qkv_in, v.w_qkv, v.s_l.at[2]),
              pltpu.make_async_copy(v.w_out_in, v.w_out, v.s_l.at[3]),
-             pltpu.make_async_copy(v.w_conv_in, v.w_conv, v.s_l.at[4])]
-    for c in loads:
-        c.start()
+             pltpu.make_async_copy(v.w_conv_in, v.w_conv, v.s_l.at[4]),
+             pltpu.make_async_copy(v.coarse.at[:, :, pl.ds(256, 256)], v.half, v.s_l.at[7]),
+             pltpu.make_async_copy(v.turns_in, v.turns, v.s_l.at[8]),
+             pltpu.make_async_copy(v.w_up_in, v.w_up, v.s_l.at[9]),
+             pltpu.make_async_copy(v.back_in, v.back, v.s_l.at[10])]
+    for n in (4, 5, 0, 1, 2, 6, 3, 7):
+        loads[n].start()
     v.bins16[...] = v.bins[...].astype(F32).astype(B16)
+    loads[4].wait()
+    loads[5].wait()
+    v.half_turned[...] = dot(v.turns[0], v.half[...].reshape(256, 256)).astype(B16).reshape(16, 16, 256)
     pl.semaphore_wait(barrier, len(peers))
     cols_finish = exchange_tokens(v, row, col, loads)
     loads[1].wait()
     loads[2].wait()
+    loads[6].wait()
+    loads[7].wait()
     attend(v)
 
     finish = spread_out("cols", 16, col, v.raised, v.slots, v.s_lc, v.r_lc, v.s_lx, v.r_lx)
@@ -692,13 +739,13 @@
 
     results = [pltpu.make_async_copy(v.grad_fine, v.grad_fine_out, v.s_l.at[5]),
                pltpu.make_async_copy(v.quantiles, v.quantiles_out, v.s_l.at[6])]
-    sends = scatter_out("rows", v.dlift, v.fold_got, v.s_fr, v.r_fr, row)
     v.fold_got[row] = v.dlift[row]
     for c in results:
         c.start()
     local_units(v)
-    wait_all(sends)
-    v.fold_turned[...] = dot(v.mid[...], v.fold_got[...].reshape(256, 128)).astype(B16).reshape(16, 16, 128)
+    for p in peer_order("rows", row):
+        fold_copy(v, row, p, p).wait()
+    v.fold_turned[...] = dot(v.turns[0], v.fold_got[...].reshape(256, 128)).astype(B16).reshape(16, 16, 128)
     sends = scatter_out("cols", v.fold_turned, v.folded, v.s_fc, v.r_fc, col)
     v.folded[col] = v.fold_turned[col]
     wait_all(sends)
@@ -707,7 +754,7 @@
                   v.a_got3, [getattr(v, "a_sem" + str(n)) for n in range(16)])
     high = reducer(me, (y_axis, x_axis), HALF, v.b_g, v.high_half, v.b_got0, v.b_sum0, v.b_got1, v.b_sum1, v.b_got2, v.b_sum2,
                    v.b_got3, [getattr(v, "b_sem" + str(n)) for n in range(16)])
-    lift_wide = dot(v.group[...], v.folded[...].reshape(256, 128))
+    lift_wide = dot(v.turns[2], v.folded[...].reshape(256, 128))
     lift, lift_turned = lift_wide.astype(B16), lift_wide.T.astype(B16)
     dcontext = dot_nt(lift, v.w_up[...]).astype(B16)
     mix_grad = dot_nt(dcontext, v.w_out[...]).astype(B16)
@@ -733,7 +780,7 @@
     passing = [pltpu.make_async_copy(src, held, sems.at[12 + n]) for n, (src, held, _) in enumerate(through)]
     reads = [pltpu.make_async_copy((low, high)[h].at[pl.ds(a, b)], held.at[h, pl.ds(a, b)], sems.at[2 * n + h])
              for n, (a, b) in enumerate(((0, 384), (384, 128))) for h in range(2)]
-    for c in reads[:2] + passing + reads[2:]:
+    for c in reads[2:] + reads[:2] + passing:
         c.start()
     writes = []
 
@@ -742,17 +789,6 @@
         c.start()
         writes.append(c)
 
-    for h in range(2):
-        reads[h].wait()
-        for n in range(3):
-            for m in range(2):
-                at = n * 128 + m * 64
-                wide[n, :, h * 256 + m * 128:h * 256 + (m + 1) * 128] = held[h, at:at + 64].astype(F32).reshape(512, 128)
-            if h == 1:
-                write(wide.at[n], grad_qkv.at[:, pl.ds(n * 512, 512)], 6 + n)
-        for m in ((0, 1, 2), (3, 4))[h]:
-            passing[m].wait()
-            write(through[m][1], through[m][2], 17 + m)
     reads[2].wait()
     reads[3].wait()
     for n in range(4):
@@ -768,6 +804,17 @@
             seen = held[1, at:at + 2].astype(F32).reshape(16, 128).T.astype(B16)
             flat[(a * 3 + b) * 128:(a * 3 + b + 1) * 128] = dot(seen, head_t)
     write(flat, grad_conv, 11)
+    for h in range(2):
+        reads[h].wait()
+        for n in range(3):
+            for m in range(2):
+                at = n * 128 + m * 64
+                wide[n, :, h * 256 + m * 128:h * 256 + (m + 1) * 128] = held[h, at:at + 64].astype(F32).reshape(512, 128)
+            if h == 1:
+                write(wide.at[n], grad_qkv.at[:, pl.ds(n * 512, 512)], 6 + n)
+        for m in ((0, 1, 2), (3, 4))[h]:
+            passing[m].wait()
+            write(through[m][1], through[m][2], 17 + m)
     tail = held[1, 402:404].astype(F32).reshape(16, 128)
     grad_head[...] = tail[:QUANT]
     loss[...] = jnp.sum(tail[QUANT:QUANT + 1], axis=1, keepdims=True) * (1.0 / (1048576.0 * QUANT))
@@ -775,10 +822,11 @@
 
 
 def body(fine_input, coarse, rain_bins, w_qkv, w_out, w_up, w_conv, w_head):
-    group = group_table()
+    mid, group = mid_table(), group_table()
+    turns = jnp.stack([mid, mid.T, group, cross_table(), group.T])
     eye = onehot(16, QUANT, [(q, q) for q in range(QUANT)])
     args = [coarse[0], fine_input[0], rain_bins[0], w_qkv, w_out, w_up, w_conv, w_head.T,
-            mid_table(), group, group.T, back_table(), pick_table(0), pick_table(14), spread_table(0), spread_table(14),
+            turns, back_table(), pick_table(0), pick_table(14), spread_table(0), spread_table(14),
             bins_table(), up_table(), sum_table(), eye]
     spaces = scratch()
     names = INPUTS + tuple(name for name, _, _ in OUTPUTS) + tuple(name for name, _ in spaces)

time: 112 us -> 106 us (0.946)
  Pallas kernels: 111 us -> 105 us
    pallas_call x1, Pallas kernels: 105 us -> 99.3 us  [body(): pl.pallas_call(kernel, out_shape=[jax.ShapeDtypeStruct(shape, dtype) for...]
where the time goes in v6:
time: 106 us
  Pallas kernels  105 us (99%)
    pallas_call x1, Pallas kernels, body(): pl.pallas_call(kernel, out_shape=[jax.ShapeDtypeStruct(shape, dtype) for...  99.3 us
    pallas_call x1, Pallas kernels, body(): pl.pallas_call(unpack_kernel, out_shape=[jax.ShapeDtypeStruct(shape, F32)...  6.03 us

profile of v6, /device:TPU:1, one launch (start us, length us, event | category | flops | bytes accessed | tf_op | source)
XLA Modules:
  0.0 106.2 jit_solution(4641432130223013381)
XLA Ops:
  0.6 99.3 %shard_map.251 = (f32[9,32,128]{2,1,0:T(8,128)}, f32[32,128,128]{2,1,0:T(8,128)}, bf16[512,8,128]{2,1,0:T(8,128)(2,1)}, bf16[512,8,128]{2,1,0:T(8,128)(2,1)}) custom-call(bf16[8,32,512]{2,1,0:T(8,128)(2,1)} %bitcast.10, bf16[32,128,128]{2,1,0:T(8,128)(2,1)} %bitcast.9, s32[32,128]{1,0:T(8,128)} %bitcast.11, bf16[512,1536]{1,0:T(8,128)(2,1)} %refs_3_.1, ...), custom_call_target="tpu_custom_call" | custom-call | tf_op jit(solution)/shard_map/pallas_call | solution.py:838
  100.0 6.0 %shard_map.252 = (f32[512,1536]{1,0:T(8,128)}, f32[512,512]{1,0:T(8,128)}, f32[512,128]{1,0:T(8,128)}, f32[1152,128]{1,0:T(8,128)}, f32[9,128]{1,0:T(8,128)}, /*...) custom-call(bf16[512,8,128]{2,1,0:T(8,128)(2,1)} %get-tuple-element.20.low, ...), custom_call_target="tpu_custom_call" | custom-call | tf_op jit(solution)/shard_map/pallas_call | solution.py:847

commit v7 on v6

--- a/solution.py
+++ b/solution.py
@@ -530,7 +530,7 @@
 
     def start(i):
         raised = dot(v.up[...], v.lifted[i])
-        rims = {0: (2, 3), 9: (0, 1)}.get(i, range(4)) if isinstance(i, int) else range(4)
+        rims = {0: (2, 3), 9: (0, 1)}.get(i, range(4))
         for s in rims:
             y = 4 * i + s - 4
             x = v.field[4 * i + s].astype(F32) + raised
@@ -538,7 +538,7 @@
             bend = jnp.tanh(ROOT_2_PI * x * (1.0 + 0.044715 * square))
             half = 0.5 * (1.0 + bend)
             act = x * half
-            if isinstance(i, int) and i in (0, 9):
+            if i in (0, 9):
                 act = jnp.where(inside & (row * 32 + y >= 0) & (row * 32 + y < 256), act, 0.0)
             else:
                 act = jnp.concatenate([act[:128], jnp.where(inside[128:], act[128:], 0.0)], axis=0)
@@ -587,7 +587,7 @@
             v.taps[4 * i + s] = sets[s].astype(B16)
             row_y = 4 * i + s - 1
             value = predicted[:, s * 128:(s + 1) * 128]
-            if not isinstance(i, int) or 0 <= row_y < 32:
+            if 0 <= row_y < 32:
                 for q in range(QUANT):
                     v.quantiles[q, pl.ds(row_y, 1), :] = value[q:q + 1]
         v.taps_turned[pl.ds(4 * i, 4)] = jnp.concatenate(sets, axis=1).T.astype(B16).reshape(4, 128, 48)
@@ -606,30 +606,17 @@
         seen = v.active[pl.ds(4 * i + 4, 4), :128, 128:256].reshape(512, 128)
         v.tap_sum[...] += dot(jnp.concatenate(lines, axis=0), seen)
 
-    def step(t):
-        known = isinstance(t, int)
-        if not known or 0 <= t - 5 <= 7:
-            back(t - 5)
-        if not known or 0 <= t - 3 <= 8:
-            turn(t - 3)
-        if not known or 0 <= t - 2 <= 8:
-            forward(t - 2)
-        if not known or t <= 9:
-            start(t)
-
-    for t in range(5):
-        step(t)
-
-    def loop(t, carry):
-        step(t)
-        return carry
-
-    lax.fori_loop(5, 9, loop, 0)
-    for n in range(4):
-        send_fold(v, row, n)
-    for t in range(9, 13):
-        step(t)
-        send_fold(v, row, t - 5)
+    for t in range(10):
+        start(t)
+    for t in range(9):
+        forward(t)
+    for t in range(9):
+        turn(t)
+    for t in range(8):
+        back(t)
+        if t % 4 == 3:
+            for n in range(t - 3, t + 1):
+                send_fold(v, row, n)
 
 
 def back_weights(v):
@@ -780,7 +767,7 @@
     passing = [pltpu.make_async_copy(src, held, sems.at[12 + n]) for n, (src, held, _) in enumerate(through)]
     reads = [pltpu.make_async_copy((low, high)[h].at[pl.ds(a, b)], held.at[h, pl.ds(a, b)], sems.at[2 * n + h])
              for n, (a, b) in enumerate(((0, 384), (384, 128))) for h in range(2)]
-    for c in reads[2:] + reads[:2] + passing:
+    for c in passing + reads[2:] + reads[:2]:
         c.start()
     writes = []
 
@@ -789,6 +776,9 @@
         c.start()
         writes.append(c)
 
+    for m in range(5):
+        passing[m].wait()
+        write(through[m][1], through[m][2], 17 + m)
     reads[2].wait()
     reads[3].wait()
     for n in range(4):
@@ -809,12 +799,8 @@
         for n in range(3):
             for m in range(2):
                 at = n * 128 + m * 64
-                wide[n, :, h * 256 + m * 128:h * 256 + (m + 1) * 128] = held[h, at:at + 64].astype(F32).reshape(512, 128)
-            if h == 1:
-                write(wide.at[n], grad_qkv.at[:, pl.ds(n * 512, 512)], 6 + n)
-        for m in ((0, 1, 2), (3, 4))[h]:
-            passing[m].wait()
-            write(through[m][1], through[m][2], 17 + m)
+                wide[h * 3 + n, :, m * 128:(m + 1) * 128] = held[h, at:at + 64].astype(F32).reshape(512, 128)
+            write(wide.at[h * 3 + n], grad_qkv.at[:, pl.ds(n * 512 + h * 256, 256)], 22 + h * 3 + n)
     tail = held[1, 402:404].astype(F32).reshape(16, 128)
     grad_head[...] = tail[:QUANT]
     loss[...] = jnp.sum(tail[QUANT:QUANT + 1], axis=1, keepdims=True) * (1.0 / (1048576.0 * QUANT))
@@ -849,9 +835,9 @@
         out_shape=[jax.ShapeDtypeStruct(shape, F32) for shape in shapes],
         in_specs=[anywhere] * 4 + [vmem] * 3,
         out_specs=[anywhere] * 4 + [vmem] * 2 + [anywhere] * 2,
-        scratch_shapes=[pltpu.VMEM((2, HALF, 8, 128), B16), pltpu.VMEM((3, 512, 512), F32),
+        scratch_shapes=[pltpu.VMEM((2, HALF, 8, 128), B16), pltpu.VMEM((6, 512, 256), F32),
                         pltpu.VMEM((512, 512), F32), pltpu.VMEM((512, 128), F32), pltpu.VMEM((1152, 128), F32),
-                        pltpu.VMEM((32, 128, 128), F32), pltpu.VMEM((9, 32, 128), F32), DMA((22,))],
+                        pltpu.VMEM((32, 128, 128), F32), pltpu.VMEM((9, 32, 128), F32), DMA((28,))],
         compiler_params=pltpu.CompilerParams(vmem_limit_bytes=LIMIT),
     )(low, high, grad_fine, quantiles, w_up, w_head.T, eye)
     return (bands[None], loss.reshape(()), grad_qkv, grad_out, grad_up, grad_conv.reshape(3, 3, 128, 128),

time: 106 us -> 104 us (0.981)
  Pallas kernels: 105 us -> 103 us
    pallas_call x1, Pallas kernels: 99.3 us -> 96.5 us  [body(): pl.pallas_call(kernel, out_shape=[jax.ShapeDtypeStruct(shape, dtype) for...]
where the time goes in v7:
time: 104 us; the launch traced here: 103 us
  Pallas kernels  103 us (99%)
    pallas_call x1, Pallas kernels, body(): pl.pallas_call(kernel, out_shape=[jax.ShapeDtypeStruct(shape, dtype) for...  96.5 us
    pallas_call x1, Pallas kernels, body(): pl.pallas_call(unpack_kernel, out_shape=[jax.ShapeDtypeStruct(shape, F32)...  6.05 us

profile of v7, /device:TPU:1, one launch (start us, length us, event | category | flops | bytes accessed | tf_op | source)
XLA Modules:
  0.0 103.4 jit_solution(16622310843469106690)
XLA Ops:
  0.6 96.5 %shard_map.251 = (f32[9,32,128]{2,1,0:T(8,128)}, f32[32,128,128]{2,1,0:T(8,128)}, bf16[512,8,128]{2,1,0:T(8,128)(2,1)}, bf16[512,8,128]{2,1,0:T(8,128)(2,1)}) custom-call(bf16[8,32,512]{2,1,0:T(8,128)(2,1)} %bitcast.10, bf16[32,128,128]{2,1,0:T(8,128)(2,1)} %bitcast.9, s32[32,128]{1,0:T(8,128)} %bitcast.11, bf16[512,1536]{1,0:T(8,128)(2,1)} %refs_3_.1, ...), custom_call_target="tpu_custom_call" | custom-call | tf_op jit(solution)/shard_map/pallas_call | solution.py:824
  97.2 6.0 %shard_map.252 = (f32[512,1536]{1,0:T(8,128)}, f32[512,512]{1,0:T(8,128)}, f32[512,128]{1,0:T(8,128)}, f32[1152,128]{1,0:T(8,128)}, f32[9,128]{1,0:T(8,128)}, /*...) custom-call(bf16[512,8,128]{2,1,0:T(8,128)(2,1)} %get-tuple-element.20.low, ...), custom_call_target="tpu_custom_call" | custom-call | tf_op jit(solution)/shard_map/pallas_call | solution.py:833

commit v8 on v7

--- a/solution.py
+++ b/solution.py
@@ -1,3 +1,4 @@
+import functools
 import jax
 import jax.numpy as jnp
 import numpy as np
@@ -15,7 +16,7 @@
 SCALE = HEAD_DIM ** (-0.5)
 ROOT_2_PI = 0.7978845608028654
 LIMIT = 58 * 1024 * 1024
-HALF = 512
+HALF, SHARES = 480, 5
 
 
 def onehot(rows, cols, pairs):
@@ -185,11 +186,11 @@
     return jnp.concatenate([pltpu.roll(line, 1, 0), line, pltpu.roll(line, 143, 0)], axis=1)
 
 
-def reducer(me, axes, units, g, out, got0, sum0, got1, sum1, got2, sum2, got3, sems):
+def reducer(me, axes, units, g, out, dest, got0, sum0, got1, sum1, got2, sum2, got3, sems):
     core, deep = me.core, me.deep
     (first, in_first), (second, in_second) = axes
-    u0, u1, u2, u3 = units // 2, units // 8, units // 32, units // 256
-    s0, r0, s1, r1, s2, r2, s3, r3, as3, ar3, as2, ar2, as1, ar1, as0, ar0 = sems
+    u0, u1, u2, u3 = units // 2, units // 8, units // 32, units // (32 * SHARES)
+    s0, r0, s1, r1, s2, r2, s3, r3, as3, ar3, as2, ar2, as1, ar1, as0, ar0, w0, w1 = sems
     place = core * u0 + first * u1 + second * u2
     held = {}
 
@@ -233,26 +234,46 @@
     def deep_start():
         wait_all(held["second"])
         sum2[...] = sum_up([sum1[pl.ds(second * u2, u2)], got2[0], got2[1], got2[2]]).astype(B16)
-        held["deep"] = []
         for k in (4, 3, 5, 2, 6, 1, 7):
-            p = (deep + k) % 8
-            c = rcopy(sum2.at[pl.ds(p * u3, u3)], got3.at[k - 1], s3.at[k - 1], r3.at[k - 1], me.in_deep(k))
-            c.start()
-            held["deep"].append(c)
+            pl.when((deep + k) % 8 < SHARES)(functools.partial(deep_send, k))
+
+    def deep_copy(k, share):
+        return rcopy(sum2.at[pl.ds(share * u3, u3)], got3.at[k - 1], s3.at[k - 1], r3.at[k - 1], me.in_deep(k))
+
+    def deep_send(k):
+        deep_copy(k, (deep + k) % 8).start()
+
+    def deep_sent(k):
+        deep_copy(k, 0).wait_send()
+
+    def deep_back(k, share):
+        block = out.at[pl.ds(place + share * u3, u3)]
+        return rcopy(block, block, as3.at[k - 1], ar3.at[k - 1], me.in_deep(k))
+
+    def deep_here(k):
+        deep_back(k, 0).wait_recv()
 
     def deep_gather():
-        wait_all(held["deep"])
-        mine = sum_up([sum2[pl.ds(deep * u3, u3)]] + [got3[k] for k in range(7)])
-        out[pl.ds(place + deep * u3, u3)] = mine.astype(B16)
-        block = out.at[pl.ds(place + deep * u3, u3)]
-        held["deep"] = []
-        for k in (4, 3, 5, 2, 6, 1, 7):
-            c = rcopy(block, block, as3.at[k - 1], ar3.at[k - 1], me.in_deep(k))
-            c.start()
-            held["deep"].append(c)
+        for k in range(1, 8):
+            pl.when((deep + k) % 8 < SHARES)(functools.partial(deep_sent, k))
+
+        @pl.when(deep < SHARES)
+        def _():
+            for k in range(1, 8):
+                deep_copy(k, 0).wait_recv()
+            mine = sum_up([sum2[pl.ds(deep * u3, u3)]] + [got3[k] for k in range(7)])
+            out[pl.ds(place + deep * u3, u3)] = mine.astype(B16)
+            for k in (4, 3, 5, 2, 6, 1, 7):
+                deep_back(k, deep).start()
 
     def second_gather():
-        wait_all(held["deep"])
+        @pl.when(deep < SHARES)
+        def _():
+            for k in range(1, 8):
+                deep_back(k, 0).wait_send()
+
+        for k in range(1, 8):
+            pl.when((deep + 8 - k) % 8 < SHARES)(functools.partial(deep_here, k))
         block = out.at[pl.ds(place, u2)]
         held["second"] = []
         for k in (1, 2, 3):
@@ -260,16 +281,23 @@
             c.start()
             held["second"].append(c)
 
+    def leave(at, sem):
+        block = pl.ds(at, u1)
+        c = pltpu.make_async_copy(out.at[block], dest.at[block], sem)
+        c.start()
+        held["leave"].append(c)
+
     def forward(n, p):
         block = out.at[pl.ds(core * u0 + p * u1, u1)]
         c = rcopy(block, block, as0.at[n], ar0.at[n], me.other)
         c.start()
         held["near"].append(c)
+        leave(core * u0 + p * u1, w0.at[n])
 
     def first_gather():
         wait_all(held["second"])
         block = out.at[pl.ds(core * u0 + first * u1, u1)]
-        held["first"], held["near"] = [], []
+        held["first"], held["near"], held["leave"] = [], [], []
         for k in (1, 2, 3):
             c = rcopy(block, block, as1.at[k - 1], ar1.at[k - 1], in_first(k))
             c.start()
@@ -282,9 +310,12 @@
             forward(k, (first + 4 - k) % 4)
 
     def finish():
-        for c in held["first"]:
+        for n, c in enumerate(held["near"]):
+            c.wait_recv()
+            leave((1 - core) * u0 + (first + 4 - n) % 4 * u1, w1.at[n])
+        for c in held["first"] + held["near"]:
             c.wait_send()
-        wait_all(held["near"])
+        wait_all(held["leave"])
 
     return [near_start, first_start, second_start, deep_start, deep_gather, second_gather, first_gather,
             near_gather, finish]
@@ -292,11 +323,11 @@
 
 def reducer_scratch(tag, units):
     unit = (8, 128)
-    u1, u2, u3 = units // 8, units // 32, units // 256
-    shapes = [("g", (units,) + unit), ("got0", (4, u1) + unit), ("sum0", (4, u1) + unit), ("got1", (3, u1) + unit),
+    u1, u2, u3 = units // 8, units // 32, units // (32 * SHARES)
+    shapes = [("g", (units,) + unit), ("out", (units,) + unit), ("got0", (4, u1) + unit), ("sum0", (4, u1) + unit), ("got1", (3, u1) + unit),
               ("sum1", (u1,) + unit), ("got2", (3, u2) + unit), ("sum2", (u2,) + unit), ("got3", (7, u3) + unit)]
     result = [(tag + name, pltpu.VMEM(shape, B16)) for name, shape in shapes]
-    for n, count in enumerate((4, 4, 3, 3, 3, 3, 7, 7, 7, 7, 3, 3, 3, 3, 4, 4)):
+    for n, count in enumerate((4, 4, 3, 3, 3, 3, 7, 7, 7, 7, 3, 3, 3, 3, 4, 4, 4, 4)):
         result.append((tag + "sem" + str(n), DMA((count,))))
     return result
 
@@ -633,12 +664,13 @@
 
 
 def local_units(v):
-    v.b_g[384:402] = v.tap_sum[...].reshape(18, 8, 128).astype(B16)
+    v.a_g[448:466] = v.tap_sum[...].reshape(18, 8, 128).astype(B16)
     spot = lax.broadcasted_iota(jnp.int32, (16, 1), 0)
     total = jnp.sum(v.loss_sum[...], axis=0, keepdims=True)
     tail = jnp.where(spot < QUANT, v.head_sum[...], jnp.where(spot == QUANT, total, 0.0))
-    v.b_g[402:404] = tail.reshape(2, 8, 128).astype(B16)
-    v.b_g[404:HALF] = jnp.zeros((HALF - 404, 8, 128), B16)
+    v.a_g[466:468] = tail.reshape(2, 8, 128).astype(B16)
+    v.a_g[468:HALF] = jnp.zeros((HALF - 468, 8, 128), B16)
+    v.b_g[448:HALF] = jnp.zeros((HALF - 448, 8, 128), B16)
 
 
 def attend_back(v, mix_grad, g, tiles):
@@ -737,16 +769,16 @@
     v.folded[col] = v.fold_turned[col]
     wait_all(sends)
 
-    low = reducer(me, (x_axis, y_axis), HALF, v.a_g, v.low_half, v.a_got0, v.a_sum0, v.a_got1, v.a_sum1, v.a_got2, v.a_sum2,
-                  v.a_got3, [getattr(v, "a_sem" + str(n)) for n in range(16)])
-    high = reducer(me, (y_axis, x_axis), HALF, v.b_g, v.high_half, v.b_got0, v.b_sum0, v.b_got1, v.b_sum1, v.b_got2, v.b_sum2,
-                   v.b_got3, [getattr(v, "b_sem" + str(n)) for n in range(16)])
+    low = reducer(me, (x_axis, y_axis), HALF, v.a_g, v.a_out, v.low_half, v.a_got0, v.a_sum0, v.a_got1, v.a_sum1, v.a_got2, v.a_sum2,
+                  v.a_got3, [getattr(v, "a_sem" + str(n)) for n in range(18)])
+    high = reducer(me, (y_axis, x_axis), HALF, v.b_g, v.b_out, v.high_half, v.b_got0, v.b_sum0, v.b_got1, v.b_sum1, v.b_got2, v.b_sum2,
+                   v.b_got3, [getattr(v, "b_sem" + str(n)) for n in range(18)])
     lift_wide = dot(v.turns[2], v.folded[...].reshape(256, 128))
     lift, lift_turned = lift_wide.astype(B16), lift_wide.T.astype(B16)
     dcontext = dot_nt(lift, v.w_up[...]).astype(B16)
     mix_grad = dot_nt(dcontext, v.w_out[...]).astype(B16)
     put(v.a_g, 384, dot(lift_turned, v.mixed[...]))
-    put(v.a_g, 448, dot(lift_turned, v.context[...]))
+    put(v.b_g, 384, dot(lift_turned, v.context[...]))
     attend_back(v, mix_grad, v.a_g, (0, 1))
     low[0]()
     attend_back(v, mix_grad, v.b_g, (2, 3))
@@ -766,7 +798,7 @@
     through.append((quantiles, bands_in, quantiles_out))
     passing = [pltpu.make_async_copy(src, held, sems.at[12 + n]) for n, (src, held, _) in enumerate(through)]
     reads = [pltpu.make_async_copy((low, high)[h].at[pl.ds(a, b)], held.at[h, pl.ds(a, b)], sems.at[2 * n + h])
-             for n, (a, b) in enumerate(((0, 384), (384, 128))) for h in range(2)]
+             for n, (a, b) in enumerate(((0, 384), (384, HALF - 384))) for h in range(2)]
     for c in passing + reads[2:] + reads[:2]:
         c.start()
     writes = []
@@ -784,14 +816,14 @@
     for n in range(4):
         mixed = held[0, 384 + n * 16:384 + (n + 1) * 16].astype(F32).reshape(128, 128).T.astype(B16)
         square[n * 128:(n + 1) * 128] = dot_nt(mixed, w_up[...])
-        tall[n * 128:(n + 1) * 128] = held[0, 448 + n * 16:448 + (n + 1) * 16].astype(F32).reshape(128, 128).T
+        tall[n * 128:(n + 1) * 128] = held[1, 384 + n * 16:384 + (n + 1) * 16].astype(F32).reshape(128, 128).T
     write(square, grad_out, 9)
     write(tall, grad_up, 10)
     head_t = dot(eye[...], w_head_t[...]).astype(B16)
     for a in range(3):
         for b in range(3):
-            at = 384 + (2 - a) * 6 + (2 - b) * 2
-            seen = held[1, at:at + 2].astype(F32).reshape(16, 128).T.astype(B16)
+            at = 448 + (2 - a) * 6 + (2 - b) * 2
+            seen = held[0, at:at + 2].astype(F32).reshape(16, 128).T.astype(B16)
             flat[(a * 3 + b) * 128:(a * 3 + b + 1) * 128] = dot(seen, head_t)
     write(flat, grad_conv, 11)
     for h in range(2):
@@ -801,7 +833,7 @@
                 at = n * 128 + m * 64
                 wide[h * 3 + n, :, m * 128:(m + 1) * 128] = held[h, at:at + 64].astype(F32).reshape(512, 128)
             write(wide.at[h * 3 + n], grad_qkv.at[:, pl.ds(n * 512 + h * 256, 256)], 22 + h * 3 + n)
-    tail = held[1, 402:404].astype(F32).reshape(16, 128)
+    tail = held[0, 466:468].astype(F32).reshape(16, 128)
     grad_head[...] = tail[:QUANT]
     loss[...] = jnp.sum(tail[QUANT:QUANT + 1], axis=1, keepdims=True) * (1.0 / (1048576.0 * QUANT))
     wait_all(writes)
@@ -825,7 +857,7 @@
         kernel,
         out_shape=[jax.ShapeDtypeStruct(shape, dtype) for _, shape, dtype in OUTPUTS],
         in_specs=[pl.BlockSpec(memory_space=pl.ANY) if name in IN_HBM else vmem for name in INPUTS],
-        out_specs=[anywhere, anywhere, vmem, vmem],
+        out_specs=[anywhere] * 4,
         scratch_shapes=[space for _, space in spaces],
         compiler_params=pltpu.CompilerParams(vmem_limit_bytes=LIMIT, collective_id=1, has_side_effects=True),
     )(*args)

time: 104 us -> 102 us (0.981)
  Pallas kernels: 103 us -> 101 us
    pallas_call x1, Pallas kernels: 96.5 us -> 95.2 us  [body(): pl.pallas_call(kernel, out_shape=[jax.ShapeDtypeStruct(shape, dtype) for...]
where the time goes in v8:
time: 102 us
  Pallas kernels  101 us (99%)
    pallas_call x1, Pallas kernels, body(): pl.pallas_call(kernel, out_shape=[jax.ShapeDtypeStruct(shape, dtype) for...  95.2 us
    pallas_call x1, Pallas kernels, body(): pl.pallas_call(unpack_kernel, out_shape=[jax.ShapeDtypeStruct(shape, F32)...  6 us

profile of v8, /device:TPU:1, one launch (start us, length us, event | category | flops | bytes accessed | tf_op | source)
XLA Modules:
  0.0 102.0 jit_solution(9449151883262205157)
XLA Ops:
  0.6 95.2 %shard_map.251 = (f32[9,32,128]{2,1,0:T(8,128)}, f32[32,128,128]{2,1,0:T(8,128)}, bf16[480,8,128]{2,1,0:T(8,128)(2,1)}, bf16[480,8,128]{2,1,0:T(8,128)(2,1)}) custom-call(bf16[8,32,512]{2,1,0:T(8,128)(2,1)} %bitcast.10, bf16[32,128,128]{2,1,0:T(8,128)(2,1)} %bitcast.9, s32[32,128]{1,0:T(8,128)} %bitcast.11, bf16[512,1536]{1,0:T(8,128)(2,1)} %refs_3_.1, ...), custom_call_target="tpu_custom_call" | custom-call | tf_op jit(solution)/shard_map/pallas_call | solution.py:856
  95.8 6.0 %shard_map.252 = (f32[512,1536]{1,0:T(8,128)}, f32[512,512]{1,0:T(8,128)}, f32[512,128]{1,0:T(8,128)}, f32[1152,128]{1,0:T(8,128)}, f32[9,128]{1,0:T(8,128)}, /*...) custom-call(bf16[480,8,128]{2,1,0:T(8,128)(2,1)} %get-tuple-element.20.low, ...), custom_call_target="tpu_custom_call" | custom-call | tf_op jit(solution)/shard_map/pallas_call | solution.py:865

commit v9 on v8

--- a/solution.py
+++ b/solution.py
@@ -673,7 +673,7 @@
     v.b_g[448:HALF] = jnp.zeros((HALF - 448, 8, 128), B16)
 
 
-def attend_back(v, mix_grad, g, tiles):
+def attend_back(v, mix_grad, tiles):
     for s, t in [(s, t) for s in range(2) for t in tiles]:
         rows, at = slice(s * 128, s * 128 + 128), t * 128
         keyed = v.qkv[rows, 512 + at:512 + at + 128]
@@ -686,6 +686,9 @@
         v.dquery[rows, at:at + 128] = dot(side_by_side(dscore), heads_down(keyed)).astype(B16)
         v.dkey[at:at + 128, rows] = dot(v.query_turned[s * 4 + t], dscore).astype(B16)
         v.dvalue[at:at + 128, rows] = dot(heads_across(mine), share.astype(B16)).astype(B16)
+
+
+def projection_units(v, g, tiles):
     at = tiles[0] * 128
     put(g, 0, dot(v.tok_turned[...], v.dquery[:, at:at + 256]))
     put(g, 128, dot_nt(v.tok_turned[...], v.dkey[at:at + 256]))
@@ -779,11 +782,13 @@
     mix_grad = dot_nt(dcontext, v.w_out[...]).astype(B16)
     put(v.a_g, 384, dot(lift_turned, v.mixed[...]))
     put(v.b_g, 384, dot(lift_turned, v.context[...]))
-    attend_back(v, mix_grad, v.a_g, (0, 1))
+    attend_back(v, mix_grad, (0, 1))
+    projection_units(v, v.a_g, (0, 1))
     low[0]()
-    attend_back(v, mix_grad, v.b_g, (2, 3))
+    attend_back(v, mix_grad, (2, 3))
+    low[1]()
+    projection_units(v, v.b_g, (2, 3))
     high[0]()
-    low[1]()
     high[1]()
     for n in range(2, 9):
         low[n]()

time: 102 us -> 103 us (level)
  no operation moved by 1% of the time
where the time goes in v9:
time: 103 us; the launch traced here: 102 us
  Pallas kernels  102 us (99%)
    pallas_call x1, Pallas kernels, body(): pl.pallas_call(kernel, out_shape=[jax.ShapeDtypeStruct(shape, dtype) for...  95.6 us
    pallas_call x1, Pallas kernels, body(): pl.pallas_call(unpack_kernel, out_shape=[jax.ShapeDtypeStruct(shape, F32)...  6 us

profile of v9, /device:TPU:1, one launch (start us, length us, event | category | flops | bytes accessed | tf_op | source)
XLA Modules:
  0.0 102.4 jit_solution(16498229007102237430)
XLA Ops:
  0.6 95.6 %shard_map.251 = (f32[9,32,128]{2,1,0:T(8,128)}, f32[32,128,128]{2,1,0:T(8,128)}, bf16[480,8,128]{2,1,0:T(8,128)(2,1)}, bf16[480,8,128]{2,1,0:T(8,128)(2,1)}) custom-call(bf16[8,32,512]{2,1,0:T(8,128)(2,1)} %bitcast.10, bf16[32,128,128]{2,1,0:T(8,128)(2,1)} %bitcast.9, s32[32,128]{1,0:T(8,128)} %bitcast.11, bf16[512,1536]{1,0:T(8,128)(2,1)} %refs_3_.1, ...), custom_call_target="tpu_custom_call" | custom-call | tf_op jit(solution)/shard_map/pallas_call | solution.py:861
  96.3 6.0 %shard_map.252 = (f32[512,1536]{1,0:T(8,128)}, f32[512,512]{1,0:T(8,128)}, f32[512,128]{1,0:T(8,128)}, f32[1152,128]{1,0:T(8,128)}, f32[9,128]{1,0:T(8,128)}, /*...) custom-call(bf16[480,8,128]{2,1,0:T(8,128)(2,1)} %get-tuple-element.20.low, ...), custom_call_target="tpu_custom_call" | custom-call | tf_op jit(solution)/shard_map/pallas_call | solution.py:870
